TPU v7x, 512 devices: a whole 4x8x8 slice. The times are simulated.
512 devices in a mesh: gx: 32 (over z_hi, y), gy: 4 (over z_lo, core), pa: 4 (over x).
Axes of the slice: x: 4, y: 8, z: 8 (z_hi: 4, z_lo: 2; z = z_hi * 2 + z_lo), core: 2. Of those that a mesh axis runs over, the one named last changes fastest.
Arguments:
- latents: bfloat16 [512, 128, 768], P(('gx', 'pa'), 'gy'), may hold values from -6 to 6
- noise: bfloat16 [2, 512, 128, 768], P(None, ('gx', 'pa'), 'gy'), may hold values from -6 to 6
- proc_gain: float32 [768], replicated, may hold values from 0.1 to 1.9
- w_qkv: bfloat16 [768, 2304], P(('gx', 'pa')), may hold values from -0.21875 to 0.21875
- w_out: bfloat16 [768, 768], P(('gx', 'pa')), may hold values from -0.21875 to 0.21875
- w_query: bfloat16 [128, 768], P(('gx', 'pa')), may hold values from -0.5 to 0.5
- w_head: bfloat16 [768, 3], P(('gx', 'pa')), may hold values from -0.21875 to 0.21875
- probe_cell: int32 [524288], P(('gx', 'gy', 'pa')), may hold values from 0 to 127
- probe_offset: float32 [2, 524288], P(None, ('gx', 'gy', 'pa')), may hold values from 0 to 1
- probe_count: int32 [512], P(('gx', 'gy', 'pa')), may hold values from 128 to 1024, as said below
Outputs:
- latent_out: bfloat16 [512, 128, 768], P(('gx', 'pa'), 'gy')
- probe_values: float32 [3, 524288], P(None, ('gx', 'gy', 'pa'))
Inputs may be any that keep to these rules, and one draw needn't show every extreme that they name: `probe_cell`: a cell of the device's own 4 x 32 block, numbered row by row. `probe_count`: slots below the count hold probes, the others are empty; in every draw one device has all 1024 slots live.
All inputs are finite; a program needn't handle non-finite values.
Results may differ from a plain program's by a relative error of at most 0.02.
Values may be sent and summed in bfloat16 or wider, within the bound.
No kernel may reach another device: no remote copies, remote signals or barrier semaphores. Data moves between devices by JAX's collectives and lax.ppermute only.
A program may use at most 64 MiB of HBM per device.

v0:
```python
import math

import jax
import jax.numpy as jnp
from jax import lax
from jax.sharding import PartitionSpec as P

HEADS = 12
FQ = 128
CH = 3
RAD = 3
STEPS = 2


EPS = 1e-06
NOISE_COEF = 0.3


def extended(block, sides, width):
    for axis, dim in sides:
        count = lax.axis_size(axis)
        forward = [(i, i + 1) for i in range(count - 1)]
        forward.append((count - 1, 0))
        backward = [(target, source) for source, target in forward]
        low = lax.ppermute(
            lax.slice_in_dim(block, block.shape[dim] - width, None, axis=dim), axis, forward
        )
        high = lax.ppermute(lax.slice_in_dim(block, 0, width, axis=dim), axis, backward)
        block = jnp.concatenate([low, block, high], axis=dim)
    return block


def normalize(tokens, gain_vec):
    values = tokens.astype(jnp.float32)
    factor = lax.rsqrt(jnp.mean(values * values, axis=-1, keepdims=True) + EPS)
    return (values * factor * gain_vec).astype(jnp.bfloat16)


def project(tokens, weight):
    leading = tokens.shape[:-1]
    flat_rows = tokens.reshape(-1, tokens.shape[-1])
    result = jnp.dot(flat_rows, weight, preferred_element_type=jnp.float32).astype(jnp.bfloat16)
    return result.reshape(leading + (weight.shape[1],))


def extend(latent_field):
    return extended(latent_field, ((("gx", "pa"), 0), ("gy", 1)), RAD)


def head_table(model_width):
    head_size = model_width // HEADS
    owner = jnp.arange(model_width, dtype=jnp.int32) // head_size
    return (owner[None, :] == jnp.arange(HEADS, dtype=jnp.int32)[:, None]).astype(jnp.float32)


def head_sums(table, product):
    return lax.dot_general(
        table,
        product,
        (((1,), (1,)), ((), ())),
        precision=lax.Precision.HIGHEST,
        preferred_element_type=jnp.float32,
    )


def head_spread(weight_rows, table_low):
    return lax.dot_general(
        weight_rows, table_low, (((0,), (0,)), ((), ())), preferred_element_type=jnp.float32
    )


def neighbour_attention(queries, key_values, row_count, col_count):
    model_width = queries.shape[-1]
    head_size = model_width // HEADS
    window_span = 2 * RAD + 1
    table = head_table(model_width)
    table_low = table.astype(jnp.bfloat16)
    query_flat = queries.reshape(-1, model_width).astype(jnp.float32)
    score_list = []
    for row_step in range(window_span):
        for col_step in range(window_span):
            key_flat = key_values[
                row_step : row_step + row_count, col_step : col_step + col_count, :model_width
            ].reshape(-1, model_width)
            score_list.append(head_sums(table, query_flat * key_flat.astype(jnp.float32)))
    scores = jnp.stack(score_list) / math.sqrt(head_size)
    weights = jax.nn.softmax(scores, axis=0).astype(jnp.bfloat16)
    summed = jnp.zeros((row_count * col_count, model_width), jnp.float32)
    for row_step in range(window_span):
        for col_step in range(window_span):
            value_flat = key_values[
                row_step : row_step + row_count, col_step : col_step + col_count, model_width:
            ].reshape(-1, model_width)
            spread = head_spread(weights[row_step * window_span + col_step], table_low)
            summed = summed + spread * value_flat.astype(jnp.float32)
    return summed.reshape(row_count, col_count, model_width).astype(jnp.bfloat16)


def decode_block(context, offsets, query_weight, head_weight):
    model_width = context.shape[-1]
    head_size = model_width // HEADS
    table = head_table(model_width)
    table_low = table.astype(jnp.bfloat16)
    freq = jnp.arange(1, FQ // 4 + 1, dtype=jnp.float32)
    angle_x = 2.0 * math.pi * offsets[0][:, None] * freq[None, :]
    angle_y = 2.0 * math.pi * offsets[1][:, None] * freq[None, :]
    features = jnp.concatenate(
        [jnp.sin(angle_x), jnp.cos(angle_x), jnp.sin(angle_y), jnp.cos(angle_y)], axis=1
    ).astype(jnp.bfloat16)
    probe_query = jnp.dot(features, query_weight, preferred_element_type=jnp.float32).astype(
        jnp.bfloat16
    )
    query_wide = probe_query.astype(jnp.float32)
    score_list = []
    for member in range(9):
        score_list.append(head_sums(table, query_wide * context[:, member].astype(jnp.float32)))
    scores = jnp.stack(score_list) / math.sqrt(head_size)
    weights = jax.nn.softmax(scores, axis=0).astype(jnp.bfloat16)
    mixed = jnp.zeros(probe_query.shape, jnp.float32)
    for member in range(9):
        mixed = mixed + head_spread(weights[member], table_low) * context[:, member].astype(
            jnp.float32
        )
    return jnp.dot(mixed.astype(jnp.bfloat16), head_weight, preferred_element_type=jnp.float32)


def local(
    latents, noise, proc_gain, w_qkv, w_out, w_query, w_head, probe_cell, probe_offset, probe_count
):
    qkv_full, out_full, query_full, head_full = (
        lax.all_gather(w_qkv, ("gx", "pa"), axis=0, tiled=True),
        lax.all_gather(w_out, ("gx", "pa"), axis=0, tiled=True),
        lax.all_gather(w_query, ("gx", "pa"), axis=0, tiled=True),
        lax.all_gather(w_head, ("gx", "pa"), axis=0, tiled=True),
    )
    row_count, col_count, model_width = latents.shape
    latent = latents
    for step in range(STEPS):
        normed = normalize(latent, proc_gain)
        triple = project(normed, qkv_full)
        queries = triple[..., :model_width]
        key_values = extend(triple[..., model_width:])
        attended = neighbour_attention(queries, key_values, row_count, col_count)
        update = jnp.dot(
            attended.reshape(-1, model_width), out_full, preferred_element_type=jnp.float32
        )
        update = update.reshape(row_count, col_count, model_width)
        latent = (
            latent.astype(jnp.float32)
            + update / STEPS
            + NOISE_COEF * noise[step].astype(jnp.float32)
        ).astype(jnp.bfloat16)
    final_ext = extended(latent, ((("gx", "pa"), 0), ("gy", 1)), 1)
    flat_ext = final_ext.reshape(-1, model_width)
    cell_row = probe_cell // col_count
    cell_col = probe_cell % col_count
    index_list = []
    for row_step in range(3):
        for col_step in range(3):
            index_list.append((cell_row + row_step) * (col_count + 2) + cell_col + col_step)
    cell_index = jnp.stack(index_list, axis=1)
    slot_count = probe_cell.shape[0]
    block_size = min(256, slot_count)
    live_count = probe_count[0]

    def decode_at(start):
        rows_index = lax.dynamic_slice_in_dim(cell_index, start, block_size, 0)
        context = jnp.take(flat_ext, rows_index, axis=0)
        offsets = lax.dynamic_slice_in_dim(probe_offset, start, block_size, 1)
        return decode_block(context, offsets, query_full, head_full)

    slots = jnp.arange(slot_count, dtype=jnp.int32)
    starts = jnp.arange(slot_count // block_size, dtype=jnp.int32) * block_size
    values = lax.map(decode_at, starts).reshape(slot_count, CH)
    probe_values = jnp.where((slots < live_count)[None, :], values.T, jnp.zeros((), jnp.float32))
    return (latent, probe_values)


def solution(mesh):
    return jax.shard_map(
        local,
        mesh=mesh,
        in_specs=(
            P(("gx", "pa"), "gy", None),
            P(None, ("gx", "pa"), "gy", None),
            P(),
            P(("gx", "pa"), None),
            P(("gx", "pa"), None),
            P(("gx", "pa"), None),
            P(("gx", "pa"), None),
            P(("gx", "gy", "pa")),
            P(None, ("gx", "gy", "pa")),
            P(("gx", "gy", "pa")),
        ),
        out_specs=(P(("gx", "pa"), "gy", None), P(None, ("gx", "gy", "pa"))),
        check_vma=False,
    )
```

profile of v0, /device:TPU:64, one launch (start us, length us, event | category | flops | bytes accessed | tf_op | source)
XLA Modules:
  0.0 1326.4 jit_solution(11120832807026859498)
XLA Ops:
  13.4 135.1 %all-gather.7.cloned.1.call-done = bf16[128,6,2304]{2,1,0:T(8,128)(2,1)} async-done(((bf16[1,6,2304]{2,1,0:T(8,128)(2,1)}), bf16[128,6,2304]{2,1,0:T(8,128)(2,1)}) %all-gather.7.cloned.1.call-update) | async-done | bytes 3538960 | tf_op jit(solution)/shard_map/all_gather | solution.py:131
  148.5 5.0 reshape.856
  156.1 8.7 collective-permute-start.1
  164.8 1.9 collective-permute-start
  167.3 99.8 %all-gather.9.cloned.1.call-done = bf16[128,6,768]{2,1,0:T(8,128)(2,1)} async-done(((bf16[1,6,768]{2,1,0:T(8,128)(2,1)}), bf16[128,6,768]{2,1,0:T(8,128)(2,1)}) %all-gather.9.cloned.1.call-update) | async-done | bytes 1179664 | tf_op jit(solution)/shard_map/all_gather | solution.py:132
  267.1 3.2 reshape.863
  275.4 2.4 collective-permute-start.2
  316.6 6.0 fusion.216
  324.9 7.4 collective-permute-start.5
  334.8 7.7 collective-permute-done.5
  342.5 12.4 collective-permute-done.4
  357.0 2.6 collective-permute-start.6
  360.0 3.2 collective-permute-done.6
  395.8 5.4 fusion.168
  404.5 3.9 collective-permute-start.8
  408.5 8.3 collective-permute-done.8
  418.7 2.4 collective-permute-start.10
  421.2 368.5 %all-gather.2 = bf16[128,1,768]{2,1,0:T(2,128)(2,1)S(1)} all-gather(bf16[1,1,768]{2,1,0:T(2,128)(2,1)S(1)} %bitcast.1582), channel_id=1, replica_groups=mesh['gx'=32,'gy'=4,'pa'=4] {'gx','pa'}, dimensions={0}, use_global_device_ids=true | all-gather | bytes 198144 | tf_op jit(solution)/shard_map/all_gather | solution.py:133
  789.7 369.0 %all-gather.3 = bf16[128,6,3]{1,2,0:T(4,128)(2,1)S(1)} all-gather(bf16[1,6,3]{1,2,0:T(4,128)(2,1)S(1)} %bitcast.1583), channel_id=1, replica_groups=mesh['gx'=32,'gy'=4,'pa'=4] {'gx','pa'}, dimensions={0}, use_global_device_ids=true | all-gather | bytes 4644 | tf_op jit(solution)/shard_map/all_gather | solution.py:134
  1159.3 159.4 %while.12 = (s32[]{:T(128)}, f32[4,256,3]{1,2,0:T(4,128)S(1)}, s32[4]{0:T(128)S(1)}, f32[2,1024]{1,0:T(2,128)}, bf16[128,768]{1,0:T(8,128)(2,1)S(1)}, /*index=5*...) while((s32[]{:T(128)}, f32[4,256,3]{1,2,0:T(4,128)S(1)}, ...), condition=%wide.region_9.10_spmd, body=%wide.region_6.9_spmd.sunk | while | flops 362281760 | bytes 60195296 | solution.py:174
  1162.3 7.9 gather_fusion
  1170.2 7.2 reshape.872
  1177.5 7.1 copy_select_fusion.2
  1202.1 7.9 gather_fusion
  1210.0 7.2 reshape.872
  1217.4 7.1 copy_select_fusion.2
  1242.0 7.9 gather_fusion
  1249.9 7.2 reshape.872
  1257.2 7.1 copy_select_fusion.2
  1281.9 7.9 gather_fusion
  1289.7 7.2 reshape.872
  1297.1 7.1 copy_select_fusion.2
  (443 shorter events, 160.3 us)
Async XLA Ops:
  7.2 141.3 %all-gather.7.cloned.1.call-start = ((), (), s32[]{:S(2)}) async-start(), calls=%async_computation | async-start | bytes 4755456 | tf_op jit(solution)/shard_map/all_gather | solution.py:131
  7.9 259.2 %all-gather.9.cloned.1.call-start = ((), (), s32[]{:S(2)}) async-start(), calls=%async_computation.1 | async-start | bytes 1585152 | tf_op jit(solution)/shard_map/all_gather | solution.py:132
  155.1 9.7 copy-start.1
  156.1 116.3 %collective-permute-start.1 = (bf16[3,32,1536]{2,1,0:T(8,128)(2,1)}, bf16[3,32,1536]{2,1,0:T(8,128)(2,1)}, u32[]{:S(2)}, u32[]{:S(2)}) collective-permute-start(bf16[3,32,1536]{2,1,0:T(8,128)(2,1)} %get-tuple-element.384), channel_id=1, source_target_pairs={{1,0},{2,1},{3,2},{16,3},{17,16},{18,17},{19,18},{32,19},{33,32},{... | collective-permute-start | bytes 884744 | tf_op jit(solution)/shard_map/ppermute | solution.py:28
  164.8 107.6 %collective-permute-start = (bf16[3,32,1536]{2,1,0:T(8,128)(2,1)}, bf16[3,32,1536]{2,1,0:T(8,128)(2,1)}, u32[]{:S(2)}, u32[]{:S(2)}) collective-permute-start(bf16[3,32,1536]{2,1,0:T(8,128)(2,1)} %get-tuple-element.383), channel_id=1, source_target_pairs={{0,1},{1,2},{2,3},{3,16},{16,17},{17,18},{18,19},{19,32},{32,33},{... | collective-permute-start | bytes 884744 | tf_op jit(solution)/shard_map/ppermute | solution.py:25
  270.3 7.5 copy-start.2
  273.5 7.0 collective-permute-start.3
  275.4 6.2 collective-permute-start.2
  316.6 6.1 copy-start.3
  316.6 6.1 copy-start.5
  316.6 7.5 copy-start.6
  324.9 17.7 %collective-permute-start.5 = (bf16[3,32,1536]{2,1,0:T(8,128)(2,1)S(1)}, bf16[3,32,1536]{2,1,0:T(8,128)(2,1)S(1)}, u32[]{:S(2)}, u32[]{:S(2)}) collective-permute-start(bf16[3,32,1536]{2,1,0:T(8,128)(2,1)S(1)} %get-tuple-element.378), channel_id=1, source_target_pairs={{1,0},{2,1},{3,2},{16,3},{17,16},{18,17},{19,18},{32,19},{33,32},{... | collective-permute-start | bytes 884744 | tf_op jit(solution)/shard_map/ppermute | solution.py:28
  332.3 22.7 %collective-permute-start.4 = (bf16[3,32,1536]{2,1,0:T(8,128)(2,1)S(1)}, bf16[3,32,1536]{2,1,0:T(8,128)(2,1)S(1)}, u32[]{:S(2)}, u32[]{:S(2)}) collective-permute-start(bf16[3,32,1536]{2,1,0:T(8,128)(2,1)S(1)} %get-tuple-element.377), channel_id=1, source_target_pairs={{0,1},{1,2},{2,3},{3,16},{16,17},{17,18},{18,19},{19,32},{32,33},{... | collective-permute-start | bytes 884744 | tf_op jit(solution)/shard_map/ppermute | solution.py:25
  355.1 5.0 collective-permute-start.7
  357.0 6.2 collective-permute-start.6
  401.2 20.0 %copy-start.11 = (bf16[1,768]{1,0:T(2,128)(2,1)S(1)}, bf16[1,768]{1,0:T(2,128)(2,1)}, u32[]{:S(2)}) copy-start(bf16[1,768]{1,0:T(2,128)(2,1)} %param.17) | copy-start | bytes 4612
  401.2 388.6 %copy-start.12 = (bf16[6,3]{0,1:T(4,128)(2,1)S(1)}, bf16[6,3]{0,1:T(4,128)(2,1)}, u32[]{:S(2)}) copy-start(bf16[6,3]{0,1:T(4,128)(2,1)} %param.18) | copy-start | bytes 112
  401.2 757.7 %copy-start.7 = (s32[1024]{0:T(1024)S(1)}, s32[1024]{0:T(1024)}, u32[]{:S(2)}) copy-start(s32[1024]{0:T(1024)} %get-tuple-element.153) | copy-start | bytes 12292
  401.2 757.7 %copy-start.8 = (s32[1024]{0:T(1024)S(1)}, s32[1024]{0:T(1024)}, u32[]{:S(2)}) copy-start(s32[1024]{0:T(1024)} %get-tuple-element.395) | copy-start | bytes 12292
  401.2 757.7 %copy-start.9 = (s32[1024]{0:T(1024)S(1)}, s32[1024]{0:T(1024)}, u32[]{:S(2)}) copy-start(s32[1024]{0:T(1024)} %get-tuple-element.397) | copy-start | bytes 12292
  401.2 757.7 %copy-start.10 = (s32[1024]{0:T(1024)S(1)}, s32[1024]{0:T(1024)}, u32[]{:S(2)}) copy-start(s32[1024]{0:T(1024)} %broadcast_add_fusion.5) | copy-start | bytes 12292
  402.5 756.8 %copy-start.4 = (bf16[4,32,768]{2,1,0:T(8,128)(2,1)}, bf16[4,32,768]{2,1,0:T(8,128)(2,1)S(1)}, u32[]{:S(2)}) copy-start(bf16[4,32,768]{2,1,0:T(8,128)(2,1)S(1)} %fusion.63) | copy-start | bytes 589828
  402.5 6.0 collective-permute-start.9
  404.5 12.3 collective-permute-start.8
  416.8 742.2 %collective-permute-start.11 = (bf16[6,1,768]{2,1,0:T(2,128)(2,1)S(1)}, bf16[6,1,768]{2,1,0:T(2,128)(2,1)S(1)}, u32[]{:S(2)}, u32[]{:S(2)}) collective-permute-start(bf16[6,1,768]{2,1,0:T(2,128)(2,1)S(1)} %get-tuple-element.392), channel_id=1, source_target_pairs={{4,0},{8,4},{12,8},{0,12},{5,1},{9,5},{13,9},{1,13},{6,2},{10,6},{... | collective-permute-start | bytes 27656 | tf_op jit(solution)/shard_map/ppermute | solution.py:28
  418.7 740.3 %collective-permute-start.10 = (bf16[6,1,768]{2,1,0:T(2,128)(2,1)S(1)}, bf16[6,1,768]{2,1,0:T(2,128)(2,1)S(1)}, u32[]{:S(2)}, u32[]{:S(2)}) collective-permute-start(bf16[6,1,768]{2,1,0:T(2,128)(2,1)S(1)} %get-tuple-element.391), channel_id=1, source_target_pairs={{0,4},{4,8},{8,12},{12,0},{1,5},{5,9},{9,13},{13,1},{2,6},{6,10},{... | collective-permute-start | bytes 27656 | tf_op jit(solution)/shard_map/ppermute | solution.py:25
  1159.3 159.5 %copy-start.13 = (pred[1024]{0:T(1024)(128)(4,1)S(1)}, pred[1024]{0:T(1024)(128)(4,1)}, u32[]{:S(2)}) copy-start(pred[1024]{0:T(1024)(128)(4,1)} %iota_compare_fusion.217) | copy-start | bytes 3076
  1184.6 7.8 copy-start
  1224.4 7.8 copy-start
  1264.3 7.8 copy-start
  1304.2 7.8 copy-start
Sparse Core Ops, SparseCore 0:
  12.4 135.9 all-gather.6
  152.8 114.3 all-gather.8
where the time goes:
time: 1340 us; the launch traced here: 1330 us
  blocking collectives  738 us (55%)
  waiting for transfers between devices  269 us (20%)
  matrix products  122 us (9%)
  local copies, waits for them, and re-layouts  83.2 us (6%)
  other arithmetic  50.9 us (4%)
  starting transfers between devices  39.1 us (3%)
  between operations  16.1 us (1%)
    all_gather x1, blocking collectives, local(): lax.all_gather(w_head, ('gx', 'pa'), axis=0, tiled=True)  369 us
    all_gather x1, blocking collectives, local(): lax.all_gather(w_query, ('gx', 'pa'), axis=0, tiled=True)  369 us
    all_gather x1, waiting for transfers between devices, local(): lax.all_gather(w_qkv, ('gx', 'pa'), axis=0, tiled=True)  135 us
    all_gather x1, waiting for transfers between devices, local(): lax.all_gather(w_out, ('gx', 'pa'), axis=0, tiled=True)  99.8 us
    dot_general x134, matrix products, head_sums(): lax.dot_general(table, product, (((1,), (1,)), ((), ())), precision=lax.P...  66.4 us
    gather x8, local copies, waits for them, and re-layouts, decode_at(): context = jnp.take(flat_ext, rows_index, axis=0)  60.4 us
    dot_general x130, matrix products, head_spread(): lax.dot_general(weight_rows, table_low, (((0,), (0,)), ((), ())), preferr...  44.2 us
    select_n x8, other arithmetic, decode_at(): context = jnp.take(flat_ext, rows_index, axis=0)  28.3 us
  transfers between devices with their start and end apart: 14, of which 8 were waited for; matrix products, arithmetic and copies ran while one was open for 2% of the time, Pallas kernels for 0%

commit v1 on v0

v1 whole, which is shorter than its diff:
```python
import math

import jax
import jax.numpy as jnp
import numpy as np
from jax import lax
from jax.experimental import pallas as pl
from jax.experimental.pallas import tpu as pltpu
from jax.sharding import PartitionSpec as P

HEADS = 12
FQ = 128
CH = 3
RAD = 3
STEPS = 2
EPS = 1e-06
NOISE_COEF = 0.3

WIDTH = 768
ROWS = 4
COLS = 32
HALO0 = 2 * RAD + 1
HALO1 = RAD + 1
KEY_ROWS = ROWS + 2 * HALO0
KEY_COLS = COLS + 2 * HALO0
PITCH0 = 48
MID_ROWS = ROWS + 2 * HALO1
PITCH1 = COLS + 2 * HALO1
END_ROWS = ROWS + 2
N_KEY0 = KEY_ROWS * PITCH0
N_MID = MID_ROWS * PITCH1
N_END = END_ROWS * PITCH1
PAIR = 2 * PITCH1
KEYS = 384
HALF = 1664
NEG = -1e30
SCALE = math.log2(math.e) / 8.0

BF = jnp.bfloat16
F32 = jnp.float32


def permutation_tables():
    target = np.arange(WIDTH)
    lane, rest = target // 192, target % 192
    source = (rest // 6) * 24 + lane * 6 + rest % 6
    perm = np.zeros((WIDTH, WIDTH), np.float32)
    perm[source, target] = 1.0
    pick = np.zeros((WIDTH, WIDTH), np.float32)
    out = np.arange(WIDTH)
    pick[out, (out % 128) * 6 + out // 128] = 1.0
    return perm, pick


def rms(values, gain):
    factor = lax.rsqrt(jnp.mean(values * values, axis=-1, keepdims=True) + EPS)
    return (values * factor * gain).astype(BF)


def prep_kernel(x0_ref, xq_ref, gain_ref, perm_ref, nk_ref, nq_ref):
    gain = gain_ref[...]
    for src, dst, chunk in ((x0_ref, nk_ref, 288), (xq_ref, nq_ref, 240)):
        for start in range(0, src.shape[0], chunk):
            normed = rms(src[start : start + chunk].astype(F32), gain)
            dst[start : start + chunk] = jnp.dot(
                normed, perm_ref[...], preferred_element_type=F32
            ).astype(BF)


def stair(index, step, count):
    total = jnp.zeros(index.shape, jnp.int32)
    for i in range(1, count):
        total = total + (index >= step * i).astype(jnp.int32)
    return total


def window_mask(pitch, rows_of_keys):
    row = lax.broadcasted_iota(jnp.int32, (PAIR, KEYS), 0)
    lane = lax.broadcasted_iota(jnp.int32, (PAIR, KEYS), 1)
    q_row = stair(row, PITCH1, 2)
    q_col = row - PITCH1 * q_row
    k_row = stair(lane, pitch, rows_of_keys)
    k_col = lane - pitch * k_row
    return q_row, q_col, k_row, k_col


def attend(queries, keys, values, mask):
    lane_head = stair(lax.broadcasted_iota(jnp.int32, (PAIR, 256), 1), 64, 4)
    zero = jnp.zeros((), BF)
    stacked = jnp.concatenate(
        [jnp.where(lane_head == h, queries, zero) for h in range(4)], axis=0
    )
    scores = lax.dot_general(
        stacked, keys, (((1,), (1,)), ((), ())), preferred_element_type=F32
    )
    parts = []
    for h in range(4):
        part = scores[h * PAIR : (h + 1) * PAIR] + mask
        top = jnp.max(part, axis=1, keepdims=True)
        weight = jnp.exp2((part - top) * SCALE)
        total = jnp.sum(weight, axis=1, keepdims=True)
        parts.append((weight.astype(BF), total))
    mixed = jnp.dot(
        jnp.concatenate([p[0] for p in parts], axis=0), values, preferred_element_type=F32
    )
    result = jnp.zeros((PAIR, 256), F32)
    for h in range(4):
        result = jnp.where(
            lane_head == h, mixed[h * PAIR : (h + 1) * PAIR] / parts[h][1], result
        )
    return result.astype(BF)


def main_kernel(
    place_ref,
    nk_ref,
    nq_ref,
    xq_ref,
    n0_ref,
    n1_ref,
    gain_ref,
    feat_ref,
    cell_ref,
    perm_ref,
    pick_ref,
    own_a,
    low_a,
    high_a,
    top_a,
    bot_a,
    own_b,
    low_b,
    high_b,
    top_b,
    bot_b,
    latent_ref,
    probe_ref,
    weights,
    keys,
    values,
    q_low,
    q_wide,
    att,
    att_perm,
    lat_mid,
    mid_perm,
    lat_end,
    end_heads,
    end_turned,
    probe_query,
    mixed_ref,
    sems,
):
    lane = place_ref[0]
    core = place_ref[1]
    live = place_ref[2]
    copies = []
    for slot, group in ((core, (own_a, low_a, high_a, top_a, bot_a)), (1 - core, (own_b, low_b, high_b, top_b, bot_b))):
        spots = (
            lax.rem(lane, 4) * 192,
            lax.rem(lane + 3, 4) * 192,
            lax.rem(lane + 1, 4) * 192,
            lax.rem(lane + 2, 4) * 192,
            lax.rem(lane + 2, 4) * 192 + 96,
        )
        for ref, start in zip(group, spots):
            copy = pltpu.make_async_copy(
                ref,
                weights.at[slot, pl.ds(pl.multiple_of(start, 96), ref.shape[0])],
                sems.at[len(copies)],
            )
            copy.start()
            copies.append(copy)
    for copy in copies:
        copy.wait()

    def project(source, which, column, target, rows, low=True):
        def tile(t, carry):
            offset = pl.multiple_of(t * 256, 256)
            product = jnp.dot(
                source[...],
                weights[which, :, pl.ds(column + offset, 256)],
                preferred_element_type=F32,
            ).astype(BF)
            target[0:rows, pl.ds(offset, 256)] = product.astype(target.dtype)
            return carry

        lax.fori_loop(0, 3, tile, 0)

    def permute_into(source, target, rows):
        target[0:rows] = jnp.dot(
            source[0:rows], perm_ref[...], preferred_element_type=F32
        ).astype(BF)

    project(nk_ref, 0, 0, keys, N_KEY0)
    project(nk_ref, 0, 768, values, N_KEY0)
    project(nq_ref, 1, 0, q_low, N_MID)

    q_row, q_col, k_row, k_col = window_mask(PITCH0, 8)
    inside = (
        (k_row >= q_row)
        & (k_row <= q_row + 2 * RAD)
        & (k_col >= q_col)
        & (k_col <= q_col + 2 * RAD)
    )
    mask = jnp.where(inside, 0.0, NEG).astype(F32)

    def attend0(j, carry):
        q_at = pl.multiple_of(j * PAIR, PAIR)
        k_at = pl.multiple_of(j * 2 * PITCH0, 2 * PITCH0)
        for g in range(3):
            cols = slice(256 * g, 256 * g + 256)
            att[pl.ds(q_at, PAIR), cols] = attend(
                q_low[pl.ds(q_at, PAIR), cols],
                keys[pl.ds(k_at, KEYS), cols],
                values[pl.ds(k_at, KEYS), cols],
                mask,
            )
        return carry

    lax.fori_loop(0, MID_ROWS // 2, attend0, 0)
    permute_into(att, att_perm, N_MID)

    for t in range(3):
        cols = slice(256 * t, 256 * t + 256)
        update = jnp.dot(
            att_perm[...],
            weights[1, :, 768 + 256 * t : 1024 + 256 * t],
            preferred_element_type=F32,
        )
        fresh = (
            xq_ref[:, cols].astype(F32)
            + update / STEPS
            + NOISE_COEF * n0_ref[:, cols].astype(F32)
        )
        lat_mid[:, cols] = fresh.astype(BF).astype(F32)

    mid_perm[...] = jnp.dot(
        rms(lat_mid[...], gain_ref[...]), perm_ref[...], preferred_element_type=F32
    ).astype(BF)
    project(mid_perm, 0, 0, keys, N_MID)
    project(mid_perm, 0, 768, values, N_MID)
    project(mid_perm.at[112:368], 1, 0, q_wide, 256)

    q_row, q_col, k_row, k_col = window_mask(PITCH1, 10)
    inside = (
        (k_row >= q_row)
        & (k_row <= q_row + 2 * RAD)
        & (k_col >= q_col - RAD)
        & (k_col <= q_col + RAD)
    )
    mask = jnp.where(inside, 0.0, NEG).astype(F32)

    def attend1(j, carry):
        at = pl.multiple_of(j * PAIR, PAIR)
        for g in range(3):
            cols = slice(256 * g, 256 * g + 256)
            att[pl.ds(at, PAIR), cols] = attend(
                q_wide[pl.ds(pl.multiple_of(at + 8, 8), PAIR), cols].astype(BF),
                keys[pl.ds(at, KEYS), cols],
                values[pl.ds(at, KEYS), cols],
                mask,
            )
        return carry

    lax.fori_loop(0, END_ROWS // 2, attend1, 0)
    permute_into(att, att_perm, N_END)

    lat_end[N_END:] = jnp.zeros((256 - N_END, WIDTH), F32)
    for t in range(3):
        cols = slice(256 * t, 256 * t + 256)
        update = jnp.dot(
            att_perm[0:N_END],
            weights[1, :, 768 + 256 * t : 1024 + 256 * t],
            preferred_element_type=F32,
        )
        fresh = (
            lat_mid[3 * PITCH1 : 3 * PITCH1 + N_END, cols]
            + update / STEPS
            + NOISE_COEF * n1_ref[:, cols].astype(F32)
        )
        lat_end[0:N_END, cols] = fresh.astype(BF).astype(F32)
    for r in range(ROWS):
        start = PITCH1 * (r + 1) + HALO1
        latent_ref[COLS * r : COLS * r + COLS] = lat_end[start : start + COLS].astype(BF)

    lane_head = stair(lax.broadcasted_iota(jnp.int32, (256, 256), 1), 64, 4)
    for g in range(3):
        quad = lat_end[:, 256 * g : 256 * g + 256]
        low = quad.astype(BF)
        for h in range(4):
            end_heads[4 * g + h] = jnp.where(lane_head == h, low, jnp.zeros((), BF))
        end_turned[256 * g : 256 * g + 256] = quad.T.astype(BF)

    query_rows = jnp.dot(
        pick_ref[...], weights[1, :, 1536:1664], preferred_element_type=F32
    )
    for i in range(6):
        block = query_rows[128 * i : 128 * i + 128].T.astype(BF)
        probe_query[128 * i : 128 * i + 128] = jnp.dot(
            block, feat_ref[...], preferred_element_type=F32
        ).astype(BF)
    head_rows = jnp.dot(perm_ref[...], weights[0, :, 1536:1664], preferred_element_type=F32)
    head_turned = head_rows.T.astype(BF)

    spot = lax.broadcasted_iota(jnp.int32, (256, 256), 0)
    spot_row = stair(spot, PITCH1, 7)
    spot_col = spot - PITCH1 * spot_row

    def decode(b, carry):
        at = pl.multiple_of(b * 256, 256)
        cell = cell_ref[:, pl.ds(at, 256)]
        cell_row = lax.shift_right_logical(cell, 5)
        cell_col = lax.bitwise_and(cell, 31) + HALO1 - 1
        near = (
            (spot_row >= cell_row)
            & (spot_row <= cell_row + 2)
            & (spot_col >= cell_col)
            & (spot_col <= cell_col + 2)
        )
        near_mask = jnp.where(near, 0.0, NEG).astype(F32)
        for h in range(HEADS):
            g = h // 4
            scores = (
                jnp.dot(
                    end_heads[h],
                    probe_query[256 * g : 256 * g + 256, pl.ds(at, 256)],
                    preferred_element_type=F32,
                )
                + near_mask
            )
            top = jnp.max(scores, axis=0, keepdims=True)
            weight = jnp.exp2((scores - top) * SCALE)
            total = jnp.sum(weight, axis=0, keepdims=True)
            mixed = jnp.dot(
                end_turned[64 * h : 64 * h + 64], weight.astype(BF), preferred_element_type=F32
            )
            mixed_ref[64 * h : 64 * h + 64] = (mixed / total).astype(BF)
        decoded = jnp.dot(head_turned[0:8], mixed_ref[...], preferred_element_type=F32)
        slot = lax.broadcasted_iota(jnp.int32, (8, 256), 1) + at
        probe_ref[:, pl.ds(at, 256)] = jnp.where(slot < live, decoded, 0.0)[0:CH]
        return carry

    lax.fori_loop(0, 4, decode, 0)


def run_prep(x0, xq, gain, perm):
    return pl.pallas_call(
        prep_kernel,
        out_shape=(
            jax.ShapeDtypeStruct((N_KEY0, WIDTH), BF),
            jax.ShapeDtypeStruct((N_MID, WIDTH), BF),
        ),
        in_specs=[pl.BlockSpec(memory_space=pltpu.VMEM)] * 4,
        out_specs=(pl.BlockSpec(memory_space=pltpu.VMEM),) * 2,
        compiler_params=pltpu.CompilerParams(vmem_limit_bytes=24 * 1024 * 1024),
        cost_estimate=pl.CostEstimate(
            flops=2 * (N_KEY0 + N_MID) * WIDTH * WIDTH, bytes_accessed=6_000_000, transcendentals=0
        ),
        name="prep",
    )(x0, xq, gain, perm)


def run_main(place, nk, nq, xq, n0, n1, gain, feat, cell, perm, pick, pieces):
    vmem = pl.BlockSpec(memory_space=pltpu.VMEM)
    return pl.pallas_call(
        main_kernel,
        out_shape=(
            jax.ShapeDtypeStruct((ROWS * COLS, WIDTH), BF),
            jax.ShapeDtypeStruct((CH, cell.shape[1]), F32),
        ),
        in_specs=[pl.BlockSpec(memory_space=pltpu.SMEM)]
        + [vmem] * 10
        + [pl.BlockSpec(memory_space=pl.ANY)] * 10,
        out_specs=(vmem, vmem),
        scratch_shapes=[
            pltpu.VMEM((2, WIDTH, HALF), BF),
            pltpu.VMEM((N_KEY0, WIDTH), BF),
            pltpu.VMEM((N_KEY0, WIDTH), BF),
            pltpu.VMEM((N_MID, WIDTH), BF),
            pltpu.VMEM((256, WIDTH), F32),
            pltpu.VMEM((N_MID, WIDTH), BF),
            pltpu.VMEM((N_MID, WIDTH), BF),
            pltpu.VMEM((N_MID, WIDTH), F32),
            pltpu.VMEM((N_MID, WIDTH), BF),
            pltpu.VMEM((256, WIDTH), F32),
            pltpu.VMEM((HEADS, 256, 256), BF),
            pltpu.VMEM((WIDTH, 256), BF),
            pltpu.VMEM((WIDTH, cell.shape[1]), BF),
            pltpu.VMEM((WIDTH, 256), BF),
            pltpu.SemaphoreType.DMA((10,)),
        ],
        compiler_params=pltpu.CompilerParams(vmem_limit_bytes=52 * 1024 * 1024),
        cost_estimate=pl.CostEstimate(
            flops=16_000_000_000, bytes_accessed=14_000_000, transcendentals=6_000_000
        ),
        name="denoise_decode",
    )(place, nk, nq, xq, n0, n1, gain, feat, cell, perm, pick, *pieces)


def features_of(offsets):
    row = np.arange(FQ)
    index = (row % 32) * 4 + row // 32
    kind = index // (FQ // 4)
    freq = (index % (FQ // 4) + 1).astype(np.float32)
    use_y = jnp.asarray((kind >= 2)[:, None])
    shift = jnp.asarray(np.where(kind % 2 == 1, math.pi / 2, 0.0).astype(np.float32)[:, None])
    position = jnp.where(use_y, offsets[1][None, :], offsets[0][None, :])
    cycles = position * jnp.asarray(freq[:, None])
    cycles = cycles - jnp.round(cycles)
    return jnp.sin(2.0 * math.pi * cycles + shift).astype(BF)


def ring(size, shift):
    return [(i, (i + shift) % size) for i in range(size)]


def halo(latents, noise):
    axes = ("gx", "pa")
    size = lax.axis_size(axes)
    n0, n1 = noise[0], noise[1]
    base = jnp.concatenate([n1[:1], latents, n0, n1[ROWS - 1 :]], axis=0)
    from_low = lax.ppermute(base[1:], axes, ring(size, 1))
    from_high = lax.ppermute(base[:-1], axes, ring(size, -1))
    far_low = lax.ppermute(latents[1:], axes, ring(size, 2))
    far_high = lax.ppermute(latents[: ROWS - 1], axes, ring(size, -2))
    lat = jnp.concatenate(
        [far_low, from_low[:ROWS], latents, from_high[1 : ROWS + 1], far_high], axis=0
    )
    first = jnp.concatenate(
        [from_low[ROWS : 2 * ROWS], n0, from_high[ROWS + 1 :]], axis=0
    )
    second = jnp.concatenate([from_low[2 * ROWS :], n1, from_high[:1]], axis=0)
    parts = ((lat, HALO0), (first, HALO1), (second, 1))
    cols = lax.axis_size("gy")

    def sent(high):
        return jnp.concatenate(
            [
                (a[:, COLS - d :] if high else a[:, :d]).reshape(-1, WIDTH)
                for a, d in parts
            ],
            axis=0,
        )

    left = lax.ppermute(sent(True), "gy", ring(cols, 1))
    right = lax.ppermute(sent(False), "gy", ring(cols, -1))
    outs = []
    at = 0
    for (a, d), pitch, lead in zip(parts, (PITCH0, PITCH1, PITCH1), (0, 0, RAD)):
        count = a.shape[0] * d
        l = left[at : at + count].reshape(a.shape[0], d, WIDTH)
        r = right[at : at + count].reshape(a.shape[0], d, WIDTH)
        at += count
        full = jnp.concatenate([l, a, r], axis=1)
        full = jnp.pad(full, ((0, 0), (lead, pitch - lead - full.shape[1]), (0, 0)))
        outs.append(full)
    x0, n0_ext, n1_ext = outs
    xq = x0[RAD : RAD + MID_ROWS, RAD : RAD + PITCH1]
    return (
        x0.reshape(N_KEY0, WIDTH),
        xq.reshape(N_MID, WIDTH),
        n0_ext.reshape(N_MID, WIDTH),
        n1_ext.reshape(N_END, WIDTH),
    )


def gather_weights(w_qkv, w_out, w_query, w_head, core):
    pack = jnp.concatenate(
        [
            w_qkv[:, WIDTH:],
            jnp.pad(w_head, ((0, 0), (0, 128 - CH))),
            w_qkv[:, :WIDTH],
            w_out,
            w_query.reshape(6, 128),
        ],
        axis=1,
    )
    mine = lax.dynamic_slice_in_dim(pack, core * HALF, HALF, 1)
    count = lax.axis_size("gx")
    block = lax.all_to_all(jnp.broadcast_to(mine[None], (count,) + mine.shape), "gx", 0, 0)
    block = block.reshape(192, HALF)
    swap = [(0, 1), (1, 0), (2, 3), (3, 2)]
    low = lax.ppermute(block, "pa", ring(4, 1))
    high = lax.ppermute(block, "pa", ring(4, -1))
    top = lax.ppermute(low[:96], "pa", ring(4, 1))
    bot = lax.ppermute(high[96:], "pa", ring(4, -1))
    mine_all = [block, low, high, top, bot]
    return mine_all + [lax.ppermute(a, "gy", swap) for a in mine_all]


def local(
    latents, noise, proc_gain, w_qkv, w_out, w_query, w_head, probe_cell, probe_offset, probe_count
):
    core = lax.rem(lax.axis_index("gy"), 2)
    place = jnp.stack([lax.axis_index("pa"), core, probe_count[0]]).astype(jnp.int32)
    x0, xq, n0, n1 = halo(latents, noise)
    pieces = gather_weights(w_qkv, w_out, w_query, w_head, core)
    perm_table, pick_table = permutation_tables()
    perm, pick = jnp.asarray(perm_table, BF), jnp.asarray(pick_table, BF)
    gain = proc_gain[None, :]
    feat = features_of(probe_offset)
    nk, nq = run_prep(x0, xq, gain, perm)
    latent, probes = run_main(
        place, nk, nq, xq, n0, n1, gain, feat, probe_cell[None, :], perm, pick, pieces
    )
    return latent.reshape(latents.shape), probes


def solution(mesh):
    return jax.shard_map(
        local,
        mesh=mesh,
        in_specs=(
            P(("gx", "pa"), "gy", None),
            P(None, ("gx", "pa"), "gy", None),
            P(),
            P(("gx", "pa"), None),
            P(("gx", "pa"), None),
            P(("gx", "pa"), None),
            P(("gx", "pa"), None),
            P(("gx", "gy", "pa")),
            P(None, ("gx", "gy", "pa")),
            P(("gx", "gy", "pa")),
        ),
        out_specs=(P(("gx", "pa"), "gy", None), P(None, ("gx", "gy", "pa"))),
        check_vma=False,
    )
```

time: 1340 us -> 181 us (0.14)
  the two profiles are of different devices: /device:TPU:64 before, /device:TPU:1 now
where the time goes in v1:
time: 181 us; the launch traced here: 180 us
  starting transfers between devices  78.7 us (43%)
  Pallas kernels  44.4 us (25%)
  waiting for transfers between devices  23.9 us (13%)
  local copies, waits for them, and re-layouts  22.7 us (13%)
  other arithmetic  8.2 us (5%)
  between operations  2.18 us (1%)
    pallas_call x1, Pallas kernels, run_main(): pl.pallas_call(main_kernel, out_shape=(jax.ShapeDtypeStruct((ROWS * COLS,...  42.4 us
    ppermute x1, waiting for transfers between devices, halo(): from_low = lax.ppermute(base[1:], axes, ring(size, 1))  21.8 us
    ppermute x1, starting transfers between devices, halo(): far_high = lax.ppermute(latents[:ROWS - 1], axes, ring(size, -2))  17 us
    ppermute x1, starting transfers between devices, halo(): right = lax.ppermute(sent(False), 'gy', ring(cols, -1))  15 us
    ppermute x5, starting transfers between devices, gather_weights(): return mine_all + [lax.ppermute(a, 'gy', swap) for a in mine_all]  14 us
    ppermute x1, starting transfers between devices, halo(): from_high = lax.ppermute(base[:-1], axes, ring(size, -1))  9.42 us
    ppermute x1, starting transfers between devices, halo(): left = lax.ppermute(sent(True), 'gy', ring(cols, 1))  4.55 us
    all_to_all x1, starting transfers between devices, gather_weights(): lax.all_to_all(jnp.broadcast_to(mine[None], (count,) + mine.shape), 'gx',...  3.92 us
  transfers between devices with their start and end apart: 16, of which 4 were waited for; matrix products, arithmetic and copies ran while one was open for 15% of the time, Pallas kernels for 1%

profile of v1, /device:TPU:1, one launch (start us, length us, event | category | flops | bytes accessed | tf_op | source)
XLA Modules:
  0.0 180.0 jit_solution(11213847207935630688)
XLA Ops:
  0.6 1.7 fusion.7
  2.4 17.0 %collective-permute-start.3 = (bf16[3,32,768]{2,1,0:T(8,128)(2,1)}, bf16[3,32,768]{2,1,0:T(8,128)(2,1)}, u32[]{:S(2)}, u32[]{:S(2)}) collective-permute-start(bf16[3,32,768]{2,1,0:T(8,128)(2,1)} %get-tuple-element.26), channel_id=1, source_target_pairs={{0,498},{1,499},{2,0},{3,1},{16,2},{17,3},{18,16},{19,17},{32,18},... | collective-permute-start | bytes 442376 | tf_op jit(solution)/shard_map/ppermute | solution.py:426
  19.4 1.9 %collective-permute-start = (bf16[3,32,768]{2,1,0:T(8,128)(2,1)S(1)}, bf16[3,32,768]{2,1,0:T(8,128)(2,1)S(1)}, u32[]{:S(2)}, u32[]{:S(2)}) collective-permute-start(bf16[3,32,768]{2,1,0:T(8,128)(2,1)S(1)} %get-tuple-element.27), channel_id=1, source_target_pairs={{0,2},{1,3},{2,16},{3,17},{16,18},{17,19},{18,32},{19,33},{32,34},... | collective-permute-start | bytes 442376 | tf_op jit(solution)/shard_map/ppermute | solution.py:425
  22.1 1.0 fusion.6
  24.2 2.2 %collective-permute-start.1 = (bf16[9,32,768]{2,1,0:T(8,128)(2,1)}, bf16[9,32,768]{2,1,0:T(8,128)(2,1)S(1)}, u32[]{:S(2)}, u32[]{:S(2)}) collective-permute-start(bf16[9,32,768]{2,1,0:T(8,128)(2,1)} %get-tuple-element.20), channel_id=1, source_target_pairs={{0,1},{1,2},{2,3},{3,16},{16,17},{17,18},{18,19},{19,32},{32,33},{... | collective-permute-start | bytes 1327112 | tf_op jit(solution)/shard_map/ppermute | solution.py:423
  26.4 9.4 %collective-permute-start.2 = (bf16[9,32,768]{2,1,0:T(8,128)(2,1)}, bf16[9,32,768]{2,1,0:T(8,128)(2,1)S(1)}, u32[]{:S(2)}, u32[]{:S(2)}) collective-permute-start(bf16[9,32,768]{2,1,0:T(8,128)(2,1)} %get-tuple-element.21), channel_id=1, source_target_pairs={{0,499},{1,0},{2,1},{3,2},{16,3},{17,16},{18,17},{19,18},{32,19},{... | collective-permute-start | bytes 1327112 | tf_op jit(solution)/shard_map/ppermute | solution.py:424
  37.1 3.9 %all-to-all-start = ((bf16[32,6,1664]{2,1,0:T(8,128)(2,1)}), bf16[32,6,1664]{2,1,0:T(8,128)(2,1)S(1)}, u32[]{:S(2)}, u32[]{:S(2)}) async-start(bf16[32,6,1664]{2,1,0:T(8,128)(2,1)} %broadcast_in_dim.50), calls=%async_computation | async-start | bytes 1703936 | tf_op jit(solution)/shard_map/all_to_all | solution.py:481
  41.9 21.8 %collective-permute-done.1 = bf16[9,32,768]{2,1,0:T(8,128)(2,1)S(1)} collective-permute-done((bf16[9,32,768]{2,1,0:T(8,128)(2,1)}, bf16[9,32,768]{2,1,0:T(8,128)(2,1)S(1)}, u32[]{:S(2)}, u32[]{:S(2)}) %collective-permute-start.1) | collective-permute-done | bytes 442400 | tf_op jit(solution)/shard_map/ppermute | solution.py:423
  67.6 1.6 pad_maximum_fusion.6
  69.2 15.0 %collective-permute-start.5 = (bf16[180,768]{1,0:T(8,128)(2,1)}, bf16[180,768]{1,0:T(8,128)(2,1)S(1)}, u32[]{:S(2)}, u32[]{:S(2)}) collective-permute-start(bf16[180,768]{1,0:T(8,128)(2,1)} %pad_maximum_fusion.6), channel_id=1, source_target_pairs={{0,12},{4,0},{8,4},{12,8},{1,13},{5,1},{9,5},{13,9},{2,14},{6,2},{... | collective-permute-start | bytes 829448 | tf_op jit(solution)/shard_map/ppermute | solution.py:447
  84.3 1.1 reshape.81.own_a
  85.3 1.9 %collective-permute-start.7 = (bf16[192,1664]{1,0:T(8,128)(2,1)}, bf16[192,1664]{1,0:T(8,128)(2,1)}, u32[]{:S(2)}, u32[]{:S(2)}) collective-permute-start(bf16[192,1664]{1,0:T(8,128)(2,1)} %reshape.81.own_a), channel_id=1, source_target_pairs={{0,3},{1,0},{2,1},{3,2},{4,7},{5,4},{6,5},{7,6},{8,11},{9,8},{10,9... | collective-permute-start | bytes 1916936 | tf_op jit(solution)/shard_map/ppermute | solution.py:485
  87.3 3.4 %collective-permute-start.6 = (bf16[192,1664]{1,0:T(8,128)(2,1)}, bf16[192,1664]{1,0:T(8,128)(2,1)}, u32[]{:S(2)}, u32[]{:S(2)}) collective-permute-start(bf16[192,1664]{1,0:T(8,128)(2,1)} %reshape.81.own_a), channel_id=1, source_target_pairs={{0,1},{1,2},{2,3},{3,0},{4,5},{5,6},{6,7},{7,4},{8,9},{9,10},{10,1... | collective-permute-start | bytes 1916936 | tf_op jit(solution)/shard_map/ppermute | solution.py:484
  90.7 4.5 %collective-permute-start.4 = (bf16[180,768]{1,0:T(8,128)(2,1)S(1)}, bf16[180,768]{1,0:T(8,128)(2,1)S(1)}, u32[]{:S(2)}, u32[]{:S(2)}) collective-permute-start(bf16[180,768]{1,0:T(8,128)(2,1)S(1)} %pad_maximum_fusion.5), channel_id=1, source_target_pairs={{0,4},{4,8},{8,12},{12,0},{1,5},{5,9},{9,13},{13,1},{2,6},{6,10},{... | collective-permute-start | bytes 829448 | tf_op jit(solution)/shard_map/ppermute | solution.py:446
  95.3 2.1 %fusion.3.feat_ref = bf16[128,1024]{1,0:T(8,128)(2,1)S(1)} fusion(f32[128]{0:T(128)S(1)} %copy-done.26, f32[128]{0:T(128)S(1)} %copy-done.27, f32[1024]{0:T(1024)S(1)} %bitcast.38, f32[1024]{0:T(1024)S(1)} %bitcast.37, pred[128]{0:T(512)(128)(4,1)S(1)} %copy-done.28), kind=kLoop, calls=%fused_computation.6 | loop fusion | flops 917504 | bytes 271488 | tf_op jit(solution)/shard_map/convert_element_type | solution.py:411
  99.5 2.7 %collective-permute-start.10 = (bf16[192,1664]{1,0:T(8,128)(2,1)}, bf16[192,1664]{1,0:T(8,128)(2,1)}, u32[]{:S(2)}, u32[]{:S(2)}) collective-permute-start(bf16[192,1664]{1,0:T(8,128)(2,1)} %reshape.81.own_a), channel_id=1, source_target_pairs={{0,4},{4,0},{8,12},{12,8},{1,5},{5,1},{9,13},{13,9},{2,6},{6,2},{1... | collective-permute-start | bytes 1916936 | tf_op jit(solution)/shard_map/ppermute | solution.py:489
  102.3 1.3 collective-permute-done.7.high_a
  103.5 1.0 slice.155
  104.5 3.3 %collective-permute-start.9 = (bf16[96,1664]{1,0:T(8,128)(2,1)S(1)}, bf16[96,1664]{1,0:T(8,128)(2,1)S(1)}, u32[]{:S(2)}, u32[]{:S(2)}) collective-permute-start(bf16[96,1664]{1,0:T(8,128)(2,1)S(1)} %slice.155), channel_id=1, source_target_pairs={{0,3},{1,0},{2,1},{3,2},{4,7},{5,4},{6,5},{7,6},{8,11},{9,8},{10,9... | collective-permute-start | bytes 958472 | tf_op jit(solution)/shard_map/ppermute | solution.py:487
  107.9 1.0 slice.154
  108.9 2.1 %collective-permute-start.8 = (bf16[96,1664]{1,0:T(8,128)(2,1)S(1)}, bf16[96,1664]{1,0:T(8,128)(2,1)S(1)}, u32[]{:S(2)}, u32[]{:S(2)}) collective-permute-start(bf16[96,1664]{1,0:T(8,128)(2,1)S(1)} %slice.154), channel_id=1, source_target_pairs={{0,1},{1,2},{2,3},{3,0},{4,5},{5,6},{6,7},{7,4},{8,9},{9,10},{10,1... | collective-permute-start | bytes 958472 | tf_op jit(solution)/shard_map/ppermute | solution.py:486
  111.0 3.3 %collective-permute-start.12 = (bf16[192,1664]{1,0:T(8,128)(2,1)}, bf16[192,1664]{1,0:T(8,128)(2,1)}, u32[]{:S(2)}, u32[]{:S(2)}) collective-permute-start(bf16[192,1664]{1,0:T(8,128)(2,1)} %collective-permute-done.7.high_a), channel_id=1, source_target_pairs={{0,4},{4,0},{8,12},{12,8},{1,5},{5,1},{9,13},{13,9},{2,6},{6,2},{1... | collective-permute-start | bytes 1916936 | tf_op jit(solution)/shard_map/ppermute | solution.py:489
  114.3 1.9 %collective-permute-start.11 = (bf16[192,1664]{1,0:T(8,128)(2,1)}, bf16[192,1664]{1,0:T(8,128)(2,1)}, u32[]{:S(2)}, u32[]{:S(2)}) collective-permute-start(bf16[192,1664]{1,0:T(8,128)(2,1)} %collective-permute-done.6.low_a), channel_id=1, source_target_pairs={{0,4},{4,0},{8,12},{12,8},{1,5},{5,1},{9,13},{13,9},{2,6},{6,2},{1... | collective-permute-start | bytes 1916936 | tf_op jit(solution)/shard_map/ppermute | solution.py:489
  117.6 2.4 %collective-permute-start.14 = (bf16[96,1664]{1,0:T(8,128)(2,1)S(1)}, bf16[96,1664]{1,0:T(8,128)(2,1)}, u32[]{:S(2)}, u32[]{:S(2)}) collective-permute-start(bf16[96,1664]{1,0:T(8,128)(2,1)S(1)} %collective-permute-done.9.bot_a), channel_id=1, source_target_pairs={{0,4},{4,0},{8,12},{12,8},{1,5},{5,1},{9,13},{13,9},{2,6},{6,2},{1... | collective-permute-start | bytes 958472 | tf_op jit(solution)/shard_map/ppermute | solution.py:489
  120.3 3.7 %collective-permute-start.13 = (bf16[96,1664]{1,0:T(8,128)(2,1)S(1)}, bf16[96,1664]{1,0:T(8,128)(2,1)}, u32[]{:S(2)}, u32[]{:S(2)}) collective-permute-start(bf16[96,1664]{1,0:T(8,128)(2,1)S(1)} %collective-permute-done.8.top_a), channel_id=1, source_target_pairs={{0,4},{4,0},{8,12},{12,8},{1,5},{5,1},{9,13},{13,9},{2,6},{6,2},{1... | collective-permute-start | bytes 958472 | tf_op jit(solution)/shard_map/ppermute | solution.py:489
  126.2 1.7 pad.12
  128.0 1.5 slice.150
  129.6 1.5 reshape.74
  131.1 2.3 %pad_maximum_fusion.1 = bf16[12,40,768]{2,1,0:T(8,128)(2,1)} fusion(bf16[12,4,768]{2,1,0:T(4,128)(2,1)} %reshape.75, bf16[4,32,768]{2,1,0:T(8,128)(2,1)} %copy-done.10, bf16[4,32,768]{2,1,0:T(8,128)(2,1)S(1)} %get-tuple-element.25, bf16[4,32,768]{2,1,0:T(8,128)(2,1)} %copy-done.9, bf16[12,4,768]{2,1,0:T(4,128)(2,1)} %reshape.74), kind=kLoop, calls=%fused_computation.2 | loop fusion | flops 3686400 | bytes 1474560 | tf_op jit(solution)/shard_map/concatenate | solution.py:455
  133.4 2.0 %prep.1 = (bf16[864,768]{1,0:T(8,128)(2,1)S(1)}, bf16[480,768]{1,0:T(8,128)(2,1)S(1)}) custom-call(bf16[864,768]{1,0:T(8,128)(2,1)S(1)} %bitcast.29, bf16[480,768]{1,0:T(8,128)(2,1)S(1)} %bitcast.30, f32[1,768]{1,0:T(1,128)S(1)} %broadcast_in_dim.42.gain_ref, bf16[768,768]{1,0:T(8,128)(2,1)S(1)} %copy-done.2), custom_call_target="tpu_custom_call" | custom-call | flops 1585446912 | bytes 6000000 | tf_op jit(solution)/shard_map/prep/pallas_call | solution.py:348
  135.4 1.1 copy-done.3
  137.5 42.4 %denoise_decode.1 = (bf16[128,768]{1,0:T(8,128)(2,1)}, f32[3,1024]{1,0:T(4,128)}) custom-call(s32[3]{0:T(128)S(1)} %pad_add_fusion.place_ref, bf16[864,768]{1,0:T(8,128)(2,1)} %copy-done.3, bf16[480,768]{1,0:T(8,128)(2,1)} %copy-done.4, bf16[480,768]{1,0:T(8,128)(2,1)} %bitcast.31, bf16[480,768]{1,0:T(8,128)(2,1)} %bitcast.36, ...), custom_call_target="tpu_custom_call" | custom-call | flops 16000000000 | bytes 14000000 | tf_op jit(solution)/shard_map/denoise_decode/pallas_call | solution.py:366
  (116 shorter events, 13.9 us)
Async XLA Ops:
  0.6 22.6 %copy-start.6 = (bf16[4,32,768]{2,1,0:T(8,128)(2,1)S(1)}, bf16[4,32,768]{2,1,0:T(8,128)(2,1)}, u32[]{:S(2)}) copy-start(bf16[4,32,768]{2,1,0:T(8,128)(2,1)} %param.15) | copy-start | bytes 589828
  2.4 33.5 %copy-start.25 = (bf16[6,3]{0,1:T(4,128)(2,1)S(1)}, bf16[6,3]{0,1:T(4,128)(2,1)}, u32[]{:S(2)}) copy-start(bf16[6,3]{0,1:T(4,128)(2,1)} %param.21) | copy-start | bytes 112
  2.4 33.6 %copy-start.20 = (bf16[6,2304]{1,0:T(8,128)(2,1)S(1)}, bf16[6,2304]{1,0:T(8,128)(2,1)}, u32[]{:S(2)}) copy-start(bf16[6,2304]{1,0:T(8,128)(2,1)} %param.18) | copy-start | bytes 82948
  2.4 33.6 %copy-start.24 = (bf16[1,768]{1,0:T(2,128)(2,1)S(1)}, bf16[1,768]{1,0:T(2,128)(2,1)}, u32[]{:S(2)}) copy-start(bf16[1,768]{1,0:T(2,128)(2,1)} %param.20) | copy-start | bytes 4612
  2.4 33.7 %copy-start.21 = (bf16[6,768]{1,0:T(8,128)(2,1)S(1)}, bf16[6,768]{1,0:T(8,128)(2,1)}, u32[]{:S(2)}) copy-start(bf16[6,768]{1,0:T(8,128)(2,1)} %param.19) | copy-start | bytes 27652
  2.4 63.9 %collective-permute-start.3 = (bf16[3,32,768]{2,1,0:T(8,128)(2,1)}, bf16[3,32,768]{2,1,0:T(8,128)(2,1)}, u32[]{:S(2)}, u32[]{:S(2)}) collective-permute-start(bf16[3,32,768]{2,1,0:T(8,128)(2,1)} %get-tuple-element.26), channel_id=1, source_target_pairs={{0,498},{1,499},{2,0},{3,1},{16,2},{17,3},{18,16},{19,17},{32,18},... | collective-permute-start | bytes 442376 | tf_op jit(solution)/shard_map/ppermute | solution.py:426
  19.4 22.5 %collective-permute-start = (bf16[3,32,768]{2,1,0:T(8,128)(2,1)S(1)}, bf16[3,32,768]{2,1,0:T(8,128)(2,1)S(1)}, u32[]{:S(2)}, u32[]{:S(2)}) collective-permute-start(bf16[3,32,768]{2,1,0:T(8,128)(2,1)S(1)} %get-tuple-element.27), channel_id=1, source_target_pairs={{0,2},{1,3},{2,16},{3,17},{16,18},{17,19},{18,32},{19,33},{32,34},... | collective-permute-start | bytes 442376 | tf_op jit(solution)/shard_map/ppermute | solution.py:425
  24.2 39.5 %collective-permute-start.1 = (bf16[9,32,768]{2,1,0:T(8,128)(2,1)}, bf16[9,32,768]{2,1,0:T(8,128)(2,1)S(1)}, u32[]{:S(2)}, u32[]{:S(2)}) collective-permute-start(bf16[9,32,768]{2,1,0:T(8,128)(2,1)} %get-tuple-element.20), channel_id=1, source_target_pairs={{0,1},{1,2},{2,3},{3,16},{16,17},{17,18},{18,19},{19,32},{32,33},{... | collective-permute-start | bytes 1327112 | tf_op jit(solution)/shard_map/ppermute | solution.py:423
  26.4 37.3 %collective-permute-start.2 = (bf16[9,32,768]{2,1,0:T(8,128)(2,1)}, bf16[9,32,768]{2,1,0:T(8,128)(2,1)S(1)}, u32[]{:S(2)}, u32[]{:S(2)}) collective-permute-start(bf16[9,32,768]{2,1,0:T(8,128)(2,1)} %get-tuple-element.21), channel_id=1, source_target_pairs={{0,499},{1,0},{2,1},{3,2},{16,3},{17,16},{18,17},{19,18},{32,19},{... | collective-permute-start | bytes 1327112 | tf_op jit(solution)/shard_map/ppermute | solution.py:424
  37.1 47.2 %all-to-all-start = ((bf16[32,6,1664]{2,1,0:T(8,128)(2,1)}), bf16[32,6,1664]{2,1,0:T(8,128)(2,1)S(1)}, u32[]{:S(2)}, u32[]{:S(2)}) async-start(bf16[32,6,1664]{2,1,0:T(8,128)(2,1)} %broadcast_in_dim.50), calls=%async_computation | async-start | bytes 1703936 | tf_op jit(solution)/shard_map/all_to_all | solution.py:481
  41.8 25.6 %copy-start.7 = (bf16[1,4,32,768]{3,1,2,0:T(4,128)(2,1)}, bf16[1,4,32,768]{3,1,2,0:T(4,128)(2,1)S(1)}, u32[]{:S(2)}) copy-start(bf16[1,4,32,768]{3,1,2,0:T(4,128)(2,1)S(1)} %copy.67) | copy-start | bytes 589828
  63.7 33.7 %copy-start.9 = (bf16[4,32,768]{2,1,0:T(8,128)(2,1)}, bf16[4,32,768]{2,1,0:T(8,128)(2,1)S(1)}, u32[]{:S(2)}) copy-start(bf16[4,32,768]{2,1,0:T(8,128)(2,1)S(1)} %get-tuple-element.17) | copy-start | bytes 589828
  64.6 34.2 %copy-start.10 = (bf16[4,32,768]{2,1,0:T(8,128)(2,1)}, bf16[4,32,768]{2,1,0:T(8,128)(2,1)S(1)}, u32[]{:S(2)}) copy-start(bf16[4,32,768]{2,1,0:T(8,128)(2,1)S(1)} %get-tuple-element.15) | copy-start | bytes 589828
  67.5 27.8 %copy-start.23 = (f32[768]{0:T(1024)S(1)}, f32[768]{0:T(1024)}, u32[]{:S(2)}) copy-start(f32[768]{0:T(1024)} %param.17) | copy-start | bytes 9220
  67.6 27.8 %copy-start.26 = (f32[128]{0:T(128)S(1)}, f32[128]{0:T(128)}, u32[]{:S(2)}) copy-start(f32[128]{0:T(128)} %constant.51) | copy-start | bytes 1540
  67.6 27.8 %copy-start.27 = (f32[128]{0:T(128)S(1)}, f32[128]{0:T(128)}, u32[]{:S(2)}) copy-start(f32[128]{0:T(128)} %constant.50) | copy-start | bytes 1540
  67.6 27.8 %copy-start.28 = (pred[128]{0:T(512)(128)(4,1)S(1)}, pred[128]{0:T(512)(128)(4,1)}, u32[]{:S(2)}) copy-start(pred[128]{0:T(512)(128)(4,1)} %constant.49) | copy-start | bytes 388
  69.2 28.2 %collective-permute-start.5 = (bf16[180,768]{1,0:T(8,128)(2,1)}, bf16[180,768]{1,0:T(8,128)(2,1)S(1)}, u32[]{:S(2)}, u32[]{:S(2)}) collective-permute-start(bf16[180,768]{1,0:T(8,128)(2,1)} %pad_maximum_fusion.6), channel_id=1, source_target_pairs={{0,12},{4,0},{8,4},{12,8},{1,13},{5,1},{9,5},{13,9},{2,14},{6,2},{... | collective-permute-start | bytes 829448 | tf_op jit(solution)/shard_map/ppermute | solution.py:447
  85.3 18.2 %collective-permute-start.7 = (bf16[192,1664]{1,0:T(8,128)(2,1)}, bf16[192,1664]{1,0:T(8,128)(2,1)}, u32[]{:S(2)}, u32[]{:S(2)}) collective-permute-start(bf16[192,1664]{1,0:T(8,128)(2,1)} %reshape.81.own_a), channel_id=1, source_target_pairs={{0,3},{1,0},{2,1},{3,2},{4,7},{5,4},{6,5},{7,6},{8,11},{9,8},{10,9... | collective-permute-start | bytes 1916936 | tf_op jit(solution)/shard_map/ppermute | solution.py:485
  87.3 20.6 %collective-permute-start.6 = (bf16[192,1664]{1,0:T(8,128)(2,1)}, bf16[192,1664]{1,0:T(8,128)(2,1)}, u32[]{:S(2)}, u32[]{:S(2)}) collective-permute-start(bf16[192,1664]{1,0:T(8,128)(2,1)} %reshape.81.own_a), channel_id=1, source_target_pairs={{0,1},{1,2},{2,3},{3,0},{4,5},{5,6},{6,7},{7,4},{8,9},{9,10},{10,1... | collective-permute-start | bytes 1916936 | tf_op jit(solution)/shard_map/ppermute | solution.py:484
  90.7 8.1 %collective-permute-start.4 = (bf16[180,768]{1,0:T(8,128)(2,1)S(1)}, bf16[180,768]{1,0:T(8,128)(2,1)S(1)}, u32[]{:S(2)}, u32[]{:S(2)}) collective-permute-start(bf16[180,768]{1,0:T(8,128)(2,1)S(1)} %pad_maximum_fusion.5), channel_id=1, source_target_pairs={{0,4},{4,8},{8,12},{12,0},{1,5},{5,9},{9,13},{13,1},{2,6},{6,10},{... | collective-permute-start | bytes 829448 | tf_op jit(solution)/shard_map/ppermute | solution.py:446
  99.5 16.7 %copy-start.15 = (bf16[18,7,768]{2,1,0:T(8,128)(2,1)S(1)}, bf16[18,7,768]{2,1,0:T(8,128)(2,1)}, u32[]{:S(2)}) copy-start(bf16[18,7,768]{2,1,0:T(8,128)(2,1)} %reshape.71) | copy-start | bytes 580612
  99.5 16.7 %copy-start.16 = (bf16[18,7,768]{2,1,0:T(8,128)(2,1)S(1)}, bf16[18,7,768]{2,1,0:T(8,128)(2,1)}, u32[]{:S(2)}) copy-start(bf16[18,7,768]{2,1,0:T(8,128)(2,1)} %reshape.67) | copy-start | bytes 580612
  99.5 37.9 %collective-permute-start.10 = (bf16[192,1664]{1,0:T(8,128)(2,1)}, bf16[192,1664]{1,0:T(8,128)(2,1)}, u32[]{:S(2)}, u32[]{:S(2)}) collective-permute-start(bf16[192,1664]{1,0:T(8,128)(2,1)} %reshape.81.own_a), channel_id=1, source_target_pairs={{0,4},{4,0},{8,12},{12,8},{1,5},{5,1},{9,13},{13,9},{2,6},{6,2},{1... | collective-permute-start | bytes 1916936 | tf_op jit(solution)/shard_map/ppermute | solution.py:489
  104.5 13.1 %collective-permute-start.9 = (bf16[96,1664]{1,0:T(8,128)(2,1)S(1)}, bf16[96,1664]{1,0:T(8,128)(2,1)S(1)}, u32[]{:S(2)}, u32[]{:S(2)}) collective-permute-start(bf16[96,1664]{1,0:T(8,128)(2,1)S(1)} %slice.155), channel_id=1, source_target_pairs={{0,3},{1,0},{2,1},{3,2},{4,7},{5,4},{6,5},{7,6},{8,11},{9,8},{10,9... | collective-permute-start | bytes 958472 | tf_op jit(solution)/shard_map/ppermute | solution.py:487
  108.9 15.1 %copy-start.8 = (bf16[1,4,32,768]{3,1,2,0:T(4,128)(2,1)S(1)}, bf16[1,4,32,768]{3,1,2,0:T(4,128)(2,1)}, u32[]{:S(2)}) copy-start(bf16[1,4,32,768]{3,1,2,0:T(4,128)(2,1)} %copy-done.7) | copy-start | bytes 589828
  108.9 15.1 %copy-start.12 = (bf16[1,32,768]{2,0,1:T(2,128)(2,1)S(1)}, bf16[1,32,768]{2,0,1:T(2,128)(2,1)}, u32[]{:S(2)}) copy-start(bf16[1,32,768]{2,0,1:T(2,128)(2,1)} %copy-done.11) | copy-start | bytes 147460
  108.9 11.4 %collective-permute-start.8 = (bf16[96,1664]{1,0:T(8,128)(2,1)S(1)}, bf16[96,1664]{1,0:T(8,128)(2,1)S(1)}, u32[]{:S(2)}, u32[]{:S(2)}) collective-permute-start(bf16[96,1664]{1,0:T(8,128)(2,1)S(1)} %slice.154), channel_id=1, source_target_pairs={{0,1},{1,2},{2,3},{3,0},{4,5},{5,6},{6,7},{7,4},{8,9},{9,10},{10,1... | collective-permute-start | bytes 958472 | tf_op jit(solution)/shard_map/ppermute | solution.py:486
  111.0 26.4 %collective-permute-start.12 = (bf16[192,1664]{1,0:T(8,128)(2,1)}, bf16[192,1664]{1,0:T(8,128)(2,1)}, u32[]{:S(2)}, u32[]{:S(2)}) collective-permute-start(bf16[192,1664]{1,0:T(8,128)(2,1)} %collective-permute-done.7.high_a), channel_id=1, source_target_pairs={{0,4},{4,0},{8,12},{12,8},{1,5},{5,1},{9,13},{13,9},{2,6},{6,2},{1... | collective-permute-start | bytes 1916936 | tf_op jit(solution)/shard_map/ppermute | solution.py:489
  114.3 23.2 %collective-permute-start.11 = (bf16[192,1664]{1,0:T(8,128)(2,1)}, bf16[192,1664]{1,0:T(8,128)(2,1)}, u32[]{:S(2)}, u32[]{:S(2)}) collective-permute-start(bf16[192,1664]{1,0:T(8,128)(2,1)} %collective-permute-done.6.low_a), channel_id=1, source_target_pairs={{0,4},{4,0},{8,12},{12,8},{1,5},{5,1},{9,13},{13,9},{2,6},{6,2},{1... | collective-permute-start | bytes 1916936 | tf_op jit(solution)/shard_map/ppermute | solution.py:489
  117.6 19.8 %collective-permute-start.14 = (bf16[96,1664]{1,0:T(8,128)(2,1)S(1)}, bf16[96,1664]{1,0:T(8,128)(2,1)}, u32[]{:S(2)}, u32[]{:S(2)}) collective-permute-start(bf16[96,1664]{1,0:T(8,128)(2,1)S(1)} %collective-permute-done.9.bot_a), channel_id=1, source_target_pairs={{0,4},{4,0},{8,12},{12,8},{1,5},{5,1},{9,13},{13,9},{2,6},{6,2},{1... | collective-permute-start | bytes 958472 | tf_op jit(solution)/shard_map/ppermute | solution.py:489
  120.3 17.1 %collective-permute-start.13 = (bf16[96,1664]{1,0:T(8,128)(2,1)S(1)}, bf16[96,1664]{1,0:T(8,128)(2,1)}, u32[]{:S(2)}, u32[]{:S(2)}) collective-permute-start(bf16[96,1664]{1,0:T(8,128)(2,1)S(1)} %collective-permute-done.8.top_a), channel_id=1, source_target_pairs={{0,4},{4,0},{8,12},{12,8},{1,5},{5,1},{9,13},{13,9},{2,6},{6,2},{1... | collective-permute-start | bytes 958472 | tf_op jit(solution)/shard_map/ppermute | solution.py:489
  (13 other events, 67.4 us)

commit v2 on v1

v2 whole, which is shorter than its diff:
```python
import math

import jax
import jax.numpy as jnp
import numpy as np
from jax import lax
from jax.experimental import pallas as pl
from jax.experimental.pallas import tpu as pltpu
from jax.sharding import PartitionSpec as P

HEADS = 12
FQ = 128
CH = 3
RAD = 3
STEPS = 2
EPS = 1e-06
NOISE_COEF = 0.3

WIDTH = 768
ROWS = 4
COLS = 32
HALO0 = 2 * RAD + 1
HALO1 = RAD + 1
KEY_ROWS = ROWS + 2 * HALO0
EDGE = 8
PITCH0 = COLS + 2 * EDGE
N_EDGE = EDGE * (KEY_ROWS + ROWS + 2 * HALO1 + ROWS + 2)
MID_ROWS = ROWS + 2 * HALO1
PITCH1 = COLS + 2 * HALO1
END_ROWS = ROWS + 2
N_KEY0 = KEY_ROWS * PITCH0
N_MID = MID_ROWS * PITCH1
N_END = END_ROWS * PITCH1
PAIR = 2 * PITCH1
KEYS = 384
A_HALF = 1152
B_HALF = 512
N_PAD = 544
BLOCK = 128
SWAP = [(0, 1), (1, 0), (2, 3), (3, 2)]
NEG = -1e30
SCALE = math.log2(math.e) / 8.0

BF = jnp.bfloat16
F32 = jnp.float32


def permutation_tables():
    target = np.arange(WIDTH)
    lane, rest = target // 192, target % 192
    source = (rest // 6) * 24 + lane * 6 + rest % 6
    perm = np.zeros((WIDTH, WIDTH), np.float32)
    perm[source, target] = 1.0
    pick = np.zeros((WIDTH, WIDTH), np.float32)
    out = np.arange(WIDTH)
    pick[out, (out % 128) * 6 + out // 128] = 1.0
    return perm, pick


def rms(values, gain):
    factor = lax.rsqrt(jnp.mean(values * values, axis=-1, keepdims=True) + EPS)
    return (values * factor * gain).astype(BF)


def row_lists(far_low, low, own, noise, high, far_high):
    lat = [far_low[r] for r in range(RAD)] + [low[r] for r in range(ROWS)]
    lat += [own[r] for r in range(ROWS)] + [high[1 + r] for r in range(ROWS)]
    lat += [far_high[r] for r in range(RAD)]
    first = [low[ROWS + r] for r in range(ROWS)] + [noise[0, r] for r in range(ROWS)]
    first += [high[1 + ROWS + r] for r in range(ROWS)]
    second = [low[2 * ROWS]] + [noise[1, r] for r in range(ROWS)] + [high[0]]
    return lat, first, second


def pack_kernel(far_low, low, own, noise, high, far_high, to_high, to_low, high_wide, low_wide):
    lists = row_lists(far_low, low, own, noise, high, far_high)
    for i, row in enumerate(lists[0] + lists[1] + lists[2]):
        wide = row.astype(F32)
        high_wide[EDGE * i : EDGE * i + EDGE] = wide[COLS - EDGE :]
        low_wide[EDGE * i : EDGE * i + EDGE] = wide[:EDGE]
    to_high[...] = high_wide[...].astype(BF)
    to_low[...] = low_wide[...].astype(BF)


def prep_kernel(
    far_low,
    low,
    own,
    noise,
    high,
    far_high,
    left_ref,
    right_ref,
    gain_ref,
    perm_ref,
    nk_ref,
    nq_ref,
    base_ref,
    tail_ref,
    left,
    right,
    normed_keys,
    normed_queries,
):
    gain = gain_ref[...]
    lists = row_lists(far_low, low, own, noise, high, far_high)
    left[...] = left_ref[...].astype(F32)
    right[...] = right_ref[...].astype(F32)
    cut = slice(EDGE - HALO1, EDGE + COLS + HALO1)

    def full(i, row):
        span = slice(EDGE * i, EDGE * i + EDGE)
        return jnp.concatenate([left[span], row.astype(F32), right[span]], axis=0)

    for r in range(KEY_ROWS):
        values = full(r, lists[0][r])
        normed = rms(values, gain)
        normed_keys[PITCH0 * r : PITCH0 * r + PITCH0] = normed
        m = r - RAD
        if 0 <= m < MID_ROWS:
            at = slice(PITCH1 * m, PITCH1 * m + PITCH1)
            normed_queries[at] = normed.astype(F32)[cut]
            fresh = full(KEY_ROWS + m, lists[1][m])
            base_ref[at] = (values + NOISE_COEF * fresh)[cut]
    for m in range(END_ROWS):
        fresh = full(KEY_ROWS + MID_ROWS + m, lists[2][m])
        tail_ref[PITCH1 * m : PITCH1 * m + PITCH1] = (NOISE_COEF * fresh)[cut]
    perm = perm_ref[...]
    nk_ref[...] = jnp.dot(normed_keys[...], perm, preferred_element_type=F32).astype(BF)
    nq_ref[...] = jnp.dot(
        normed_queries[...].astype(BF), perm, preferred_element_type=F32
    ).astype(BF)


def stair(index, step, count):
    total = jnp.zeros(index.shape, jnp.int32)
    for i in range(1, count):
        total = total + (index >= step * i).astype(jnp.int32)
    return total


def window_mask(pitch, rows_of_keys):
    row = lax.broadcasted_iota(jnp.int32, (PAIR, KEYS), 0)
    lane = lax.broadcasted_iota(jnp.int32, (PAIR, KEYS), 1)
    q_row = stair(row, PITCH1, 2)
    q_col = row - PITCH1 * q_row
    k_row = stair(lane, pitch, rows_of_keys)
    k_col = lane - pitch * k_row
    return q_row, q_col, k_row, k_col


def attend(queries, keys, values, mask):
    rows = queries.shape[0]
    lane_head = stair(lax.broadcasted_iota(jnp.int32, (rows, 256), 1), 64, 4)
    zero = jnp.zeros((), BF)
    stacked = jnp.concatenate(
        [jnp.where(lane_head == h, queries, zero) for h in range(4)], axis=0
    )
    scores = lax.dot_general(
        stacked, keys, (((1,), (1,)), ((), ())), preferred_element_type=F32
    )
    parts = []
    for h in range(4):
        part = scores[h * rows : (h + 1) * rows] + mask
        top = jnp.max(part, axis=1, keepdims=True)
        weight = jnp.exp2(part - top)
        total = jnp.sum(weight, axis=1, keepdims=True)
        parts.append((weight.astype(BF), 1.0 / total))
    mixed = jnp.dot(
        jnp.concatenate([p[0] for p in parts], axis=0), values, preferred_element_type=F32
    )
    result = mixed[0:rows] * parts[0][1]
    for h in range(1, 4):
        result = jnp.where(
            lane_head == h, mixed[h * rows : (h + 1) * rows] * parts[h][1], result
        )
    return result.astype(BF)


def start_copies(core, pieces, target, sems, width):
    def copy_of(slot, ref, at):
        start = pl.multiple_of(at * width, 128)
        return pltpu.make_async_copy(ref, target.at[:, pl.ds(start, width)], sems.at[slot])

    copy_of(0, pieces[0], core).start()
    copy_of(1, pieces[1], 1 - core).start()

    def wait():
        copy_of(0, pieces[0], core).wait()
        copy_of(1, pieces[1], 1 - core).wait()

    return wait


def project(source, weights, column, target, rows, scale=None):
    for t in range(0, WIDTH, 256):
        product = jnp.dot(
            source[...],
            weights[:, column + t : column + t + 256],
            preferred_element_type=F32,
        )
        if scale is not None:
            product = product * scale
        target[0:rows, t : t + 256] = product.astype(BF).astype(target.dtype)


def first_kernel(
    place_ref, nk_ref, nq_ref, perm_ref, mine, other, att_ref, weights, keys, values, queries, att, sems
):
    wait = start_copies(place_ref[0], (mine, other), weights, sems, A_HALF)
    q_row, q_col, k_row, k_col = window_mask(PITCH0, 8)
    inside = (
        (k_row >= q_row)
        & (k_row <= q_row + 2 * RAD)
        & (k_col >= q_col + EDGE - HALO1 - RAD)
        & (k_col <= q_col + EDGE - HALO1 + RAD)
    )
    mask = jnp.where(inside, 0.0, NEG).astype(F32)
    wait()
    project(nk_ref, weights, 0, keys, N_KEY0)
    project(nk_ref, weights, WIDTH, values, N_KEY0)
    project(nq_ref, weights, 2 * WIDTH, queries, N_MID, SCALE)

    def attend0(j, carry):
        q_at = pl.multiple_of(j * PAIR, PAIR)
        k_at = pl.multiple_of(j * 2 * PITCH0, 2 * PITCH0)
        for g in range(3):
            cols = slice(256 * g, 256 * g + 256)
            att[pl.ds(q_at, PAIR), cols] = attend(
                queries[pl.ds(q_at, PAIR), cols],
                keys[pl.ds(k_at, KEYS), cols],
                values[pl.ds(k_at, KEYS), cols],
                mask,
            )
        return carry

    lax.fori_loop(0, MID_ROWS // 2, attend0, 0)
    att_ref[...] = jnp.dot(
        att[...], perm_ref[...], preferred_element_type=F32
    ).astype(BF)


def second_kernel(
    place_ref,
    att0_ref,
    base_ref,
    noise_ref,
    gain_ref,
    feat_ref,
    cell_ref,
    perm_ref,
    pick_ref,
    mine_a,
    other_a,
    mine_b,
    other_b,
    latent_ref,
    probe_ref,
    weights,
    tail,
    keys,
    values,
    queries,
    att,
    att_perm,
    lat_mid,
    mid_perm,
    lat_end,
    end_low,
    probe_query,
    sems_a,
    sems_b,
):
    live = place_ref[1]
    wait_b = start_copies(place_ref[0], (mine_b, other_b), tail, sems_b, B_HALF)
    wait_a = start_copies(place_ref[0], (mine_a, other_a), weights, sems_a, A_HALF)
    wait_b()

    for t in range(3):
        cols = slice(256 * t, 256 * t + 256)
        update = jnp.dot(att0_ref[...], tail[:, cols], preferred_element_type=F32)
        fresh = base_ref[:, cols] + update / STEPS
        lat_mid[:, cols] = fresh.astype(BF).astype(F32)

    mid_perm[...] = jnp.dot(
        rms(lat_mid[...], gain_ref[...]), perm_ref[...], preferred_element_type=F32
    ).astype(BF)
    keys[N_MID:] = jnp.zeros((N_PAD - N_MID, WIDTH), BF)
    values[N_MID:] = jnp.zeros((N_PAD - N_MID, WIDTH), BF)
    wait_a()
    project(mid_perm, weights, 0, keys, N_MID)
    project(mid_perm, weights, WIDTH, values, N_MID)
    project(mid_perm.at[112:368], weights, 2 * WIDTH, queries, 256, SCALE)

    q_row, q_col, k_row, k_col = window_mask(PITCH1, 10)
    inside = (
        (k_row >= q_row)
        & (k_row <= q_row + 2 * RAD)
        & (k_col >= q_col - RAD)
        & (k_col <= q_col + RAD)
    )
    mask = jnp.where(inside, 0.0, NEG).astype(F32)

    def attend1(j, carry):
        at = pl.multiple_of(j * PAIR, PAIR)
        for g in range(3):
            cols = slice(256 * g, 256 * g + 256)
            att[pl.ds(at, PAIR), cols] = attend(
                queries[pl.ds(pl.multiple_of(at + 8, 8), PAIR), cols].astype(BF),
                keys[pl.ds(at, KEYS), cols],
                values[pl.ds(at, KEYS), cols],
                mask,
            )
        return carry

    lax.fori_loop(0, END_ROWS // 2, attend1, 0)
    att_perm[...] = jnp.dot(att[...], perm_ref[...], preferred_element_type=F32).astype(BF)

    lat_end[N_END:] = jnp.zeros((256 - N_END, WIDTH), F32)
    for t in range(3):
        cols = slice(256 * t, 256 * t + 256)
        update = jnp.dot(att_perm[...], tail[:, cols], preferred_element_type=F32)
        fresh = (
            lat_mid[RAD * PITCH1 : RAD * PITCH1 + N_END, cols]
            + update / STEPS
            + noise_ref[:, cols]
        )
        lat_end[0:N_END, cols] = fresh.astype(BF).astype(F32)
    for r in range(ROWS):
        start = PITCH1 * (r + 1) + HALO1
        latent_ref[COLS * r : COLS * r + COLS] = lat_end[start : start + COLS].astype(BF)

    end_low[...] = lat_end[...].astype(BF)
    query_rows = jnp.dot(
        pick_ref[...], tail[:, 768:896], preferred_element_type=F32
    ).astype(BF)
    for i in range(6):
        probe_query[:, 128 * i : 128 * i + 128] = (
            jnp.dot(
                feat_ref[...], query_rows[128 * i : 128 * i + 128], preferred_element_type=F32
            )
            * SCALE
        ).astype(BF)
    head_rows = jnp.dot(perm_ref[...], tail[:, 896:1024], preferred_element_type=F32)
    head_turned = head_rows.T[0:8].astype(BF)

    spot = lax.broadcasted_iota(jnp.int32, (BLOCK, 256), 1)
    spot_row = stair(spot, PITCH1, 7)
    spot_col = spot - PITCH1 * spot_row

    def decode(b, carry):
        at = pl.multiple_of(b * BLOCK, BLOCK)
        cell = cell_ref[pl.ds(at, BLOCK)]
        cell_row = lax.shift_right_logical(cell, 5)
        cell_col = lax.bitwise_and(cell, 31) + HALO1 - 1
        near = (
            (spot_row >= cell_row)
            & (spot_row <= cell_row + 2)
            & (spot_col >= cell_col)
            & (spot_col <= cell_col + 2)
        )
        near_mask = jnp.where(near, 0.0, NEG).astype(F32)
        mixed = []
        for g in range(3):
            cols = slice(256 * g, 256 * g + 256)
            mixed.append(
                attend(
                    probe_query[pl.ds(at, BLOCK), cols], end_low[:, cols], end_low[:, cols], near_mask
                )
            )
        decoded = lax.dot_general(
            head_turned,
            jnp.concatenate(mixed, axis=1),
            (((1,), (1,)), ((), ())),
            preferred_element_type=F32,
        )
        slot = lax.broadcasted_iota(jnp.int32, (8, BLOCK), 1) + at
        probe_ref[:, pl.ds(at, BLOCK)] = jnp.where(slot < live, decoded, 0.0)[0:CH]
        return carry

    lax.fori_loop(0, feat_ref.shape[0] // BLOCK, decode, 0)


def run_pack(rows):
    vmem = pl.BlockSpec(memory_space=pltpu.VMEM)
    return pl.pallas_call(
        pack_kernel,
        out_shape=(jax.ShapeDtypeStruct((N_EDGE, WIDTH), BF),) * 2,
        in_specs=[vmem] * 6,
        out_specs=(vmem,) * 2,
        scratch_shapes=[pltpu.VMEM((N_EDGE, WIDTH), F32)] * 2,
        compiler_params=pltpu.CompilerParams(vmem_limit_bytes=12 * 1024 * 1024),
        cost_estimate=pl.CostEstimate(flops=0, bytes_accessed=3_000_000, transcendentals=0),
        name="pack",
    )(*rows)


def run_prep(rows, left, right, gain, perm):
    vmem = pl.BlockSpec(memory_space=pltpu.VMEM)
    return pl.pallas_call(
        prep_kernel,
        out_shape=(
            jax.ShapeDtypeStruct((N_KEY0, WIDTH), BF),
            jax.ShapeDtypeStruct((N_MID, WIDTH), BF),
            jax.ShapeDtypeStruct((N_MID, WIDTH), F32),
            jax.ShapeDtypeStruct((N_END, WIDTH), F32),
        ),
        in_specs=[vmem] * 10,
        out_specs=(vmem,) * 4,
        scratch_shapes=[
            pltpu.VMEM((N_EDGE, WIDTH), F32),
            pltpu.VMEM((N_EDGE, WIDTH), F32),
            pltpu.VMEM((N_KEY0, WIDTH), BF),
            pltpu.VMEM((N_MID, WIDTH), F32),
        ],
        compiler_params=pltpu.CompilerParams(vmem_limit_bytes=20 * 1024 * 1024),
        cost_estimate=pl.CostEstimate(
            flops=2 * (N_KEY0 + N_MID) * WIDTH * WIDTH, bytes_accessed=8_000_000, transcendentals=0
        ),
        name="prep",
    )(*rows, left, right, gain, perm)


def run_first(place, nk, nq, perm, mine, other):
    vmem = pl.BlockSpec(memory_space=pltpu.VMEM)
    anywhere = pl.BlockSpec(memory_space=pl.ANY)
    return pl.pallas_call(
        first_kernel,
        out_shape=jax.ShapeDtypeStruct((N_MID, WIDTH), BF),
        in_specs=[pl.BlockSpec(memory_space=pltpu.SMEM), vmem, vmem, vmem, anywhere, anywhere],
        out_specs=vmem,
        scratch_shapes=[
            pltpu.VMEM((WIDTH, 3 * WIDTH), BF),
            pltpu.VMEM((N_KEY0, WIDTH), BF),
            pltpu.VMEM((N_KEY0, WIDTH), BF),
            pltpu.VMEM((N_MID, WIDTH), BF),
            pltpu.VMEM((N_MID, WIDTH), BF),
            pltpu.SemaphoreType.DMA((2,)),
        ],
        compiler_params=pltpu.CompilerParams(vmem_limit_bytes=22 * 1024 * 1024),
        cost_estimate=pl.CostEstimate(
            flops=8_000_000_000, bytes_accessed=8_000_000, transcendentals=2_500_000
        ),
        name="first_step",
    )(place, nk, nq, perm, mine, other)


def run_second(place, att, base, noise, gain, feat, cell, perm, pick, pieces):
    vmem = pl.BlockSpec(memory_space=pltpu.VMEM)
    return pl.pallas_call(
        second_kernel,
        out_shape=(
            jax.ShapeDtypeStruct((ROWS * COLS, WIDTH), BF),
            jax.ShapeDtypeStruct((CH, cell.shape[0]), F32),
        ),
        in_specs=[pl.BlockSpec(memory_space=pltpu.SMEM)]
        + [vmem] * 8
        + [pl.BlockSpec(memory_space=pl.ANY)] * 4,
        out_specs=(vmem, vmem),
        scratch_shapes=[
            pltpu.VMEM((WIDTH, 3 * WIDTH), BF),
            pltpu.VMEM((WIDTH, 2 * B_HALF), BF),
            pltpu.VMEM((N_PAD, WIDTH), BF),
            pltpu.VMEM((N_PAD, WIDTH), BF),
            pltpu.VMEM((256, WIDTH), F32),
            pltpu.VMEM((N_END, WIDTH), BF),
            pltpu.VMEM((N_END, WIDTH), BF),
            pltpu.VMEM((N_MID, WIDTH), F32),
            pltpu.VMEM((N_MID, WIDTH), BF),
            pltpu.VMEM((256, WIDTH), F32),
            pltpu.VMEM((256, WIDTH), BF),
            pltpu.VMEM((cell.shape[0], WIDTH), BF),
            pltpu.SemaphoreType.DMA((2,)),
            pltpu.SemaphoreType.DMA((2,)),
        ],
        compiler_params=pltpu.CompilerParams(vmem_limit_bytes=26 * 1024 * 1024),
        cost_estimate=pl.CostEstimate(
            flops=8_000_000_000, bytes_accessed=14_000_000, transcendentals=4_500_000
        ),
        name="second_step",
    )(place, att, base, noise, gain, feat, cell, perm, pick, *pieces)


def features_of(offsets):
    row = np.arange(FQ)
    index = (row % 32) * 4 + row // 32
    kind = index // (FQ // 4)
    freq = (index % (FQ // 4) + 1).astype(np.float32)
    use_y = jnp.asarray((kind >= 2)[None, :])
    shift = jnp.asarray(np.where(kind % 2 == 1, math.pi / 2, 0.0).astype(np.float32)[None, :])
    position = jnp.where(use_y, offsets[1][:, None], offsets[0][:, None])
    cycles = position * jnp.asarray(freq[None, :])
    cycles = cycles - jnp.round(cycles)
    return jnp.sin(2.0 * math.pi * cycles + shift).astype(BF)


def ring(size, shift):
    return [(i, (i + shift) % size) for i in range(size)]


def halo_rows(latents, noise):
    axes = ("gx", "pa")
    size = lax.axis_size(axes)
    n0, n1 = noise[0], noise[1]
    base = jnp.concatenate([n1[:1], latents, n0, n1[ROWS - 1 :]], axis=0)
    return (
        lax.ppermute(latents[1:], axes, ring(size, 2)),
        lax.ppermute(base[1:], axes, ring(size, 1)),
        latents,
        noise,
        lax.ppermute(base[:-1], axes, ring(size, -1)),
        lax.ppermute(latents[:RAD], axes, ring(size, -2)),
    )


def pack_weights(w_qkv, w_out, w_query, w_head, core):
    head = [w_qkv[:, WIDTH:], w_qkv[:, :WIDTH]]
    tail = [w_out, w_query.reshape(6, 128), jnp.pad(w_head, ((0, 0), (0, 128 - CH)))]
    a = jnp.concatenate(head, axis=1)
    b = jnp.concatenate(tail, axis=1)
    mine = jnp.concatenate(
        [
            lax.dynamic_slice_in_dim(a, core * A_HALF, A_HALF, 1),
            lax.dynamic_slice_in_dim(b, core * B_HALF, B_HALF, 1),
        ],
        axis=1,
    )
    return jnp.broadcast_to(mine[None], (lax.axis_size("gx"),) + mine.shape)


def gather_long(shares):
    return lax.all_to_all(shares, "gx", 0, 0).reshape(192, A_HALF + B_HALF)


def gather_short(block):
    count = lax.axis_size("pa")
    wide = lax.all_to_all(jnp.broadcast_to(block[None], (count,) + block.shape), "pa", 0, 0)
    return wide.reshape(WIDTH, block.shape[1])


def local(
    latents, noise, proc_gain, w_qkv, w_out, w_query, w_head, probe_cell, probe_offset, probe_count
):
    barrier = lax.optimization_barrier
    cols = lax.axis_size("gy")
    perm_table, pick_table = permutation_tables()
    perm, pick = jnp.asarray(perm_table, BF), jnp.asarray(pick_table, BF)
    gain = proc_gain[None, :]
    core = lax.rem(lax.axis_index("gy"), 2)
    place = jnp.stack([core, probe_count[0]]).astype(jnp.int32)

    shares = pack_weights(w_qkv, w_out, w_query, w_head, core)
    shares, latents, noise = barrier((shares, latents, noise))
    rows = halo_rows(latents, noise)
    block, rows = barrier((gather_long(shares), rows))
    wide_a = gather_short(block[:, :A_HALF])
    to_high, to_low = run_pack(rows)
    left = lax.ppermute(to_high, "gy", ring(cols, 1))
    right = lax.ppermute(to_low, "gy", ring(cols, -1))
    nk, nq, base, tail_noise = run_prep(rows, left, right, gain, perm)
    feat = features_of(probe_offset)
    cell = probe_cell[:, None]
    wide_a, nk, nq, base, tail_noise, feat, cell, block = barrier(
        (wide_a, nk, nq, base, tail_noise, feat, cell, block)
    )
    other_a = lax.ppermute(wide_a, "gy", SWAP)
    wide_b = gather_short(block[:, A_HALF:])
    att = run_first(place, nk, nq, perm, wide_a, other_a)
    wide_b, att = barrier((wide_b, att))
    other_b = lax.ppermute(wide_b, "gy", SWAP)
    latent, probes = run_second(
        place, att, base, tail_noise, gain, feat, cell, perm, pick,
        (wide_a, other_a, wide_b, other_b),
    )
    return latent.reshape(latents.shape), probes


def solution(mesh):
    return jax.shard_map(
        local,
        mesh=mesh,
        in_specs=(
            P(("gx", "pa"), "gy", None),
            P(None, ("gx", "pa"), "gy", None),
            P(),
            P(("gx", "pa"), None),
            P(("gx", "pa"), None),
            P(("gx", "pa"), None),
            P(("gx", "pa"), None),
            P(("gx", "gy", "pa")),
            P(None, ("gx", "gy", "pa")),
            P(("gx", "gy", "pa")),
        ),
        out_specs=(P(("gx", "pa"), "gy", None), P(None, ("gx", "gy", "pa"))),
        check_vma=False,
    )
```

time: 181 us -> 160 us (0.88)
  starting transfers between devices: 78.7 us -> 64.4 us
  Pallas kernels: 44.4 us -> 35.6 us
  waiting for transfers between devices: 23.9 us -> 27.9 us
  other arithmetic: 8.2 us -> 4.69 us
    ppermute x15 -> x8, starting transfers between devices: 74.8 us -> 34.7 us  [the longest x1 9.98 us: halo_rows(): lax.ppermute(latents[:RAD], axes, ring(size, -2))]
    all_to_all x1 -> x3, starting transfers between devices: 3.92 us -> 29.7 us  [the longest x1 16.5 us: gather_long(): return lax.all_to_all(shares, 'gx', 0, 0).reshape(192, A_HALF + B_HALF)]
    unnamed x71 -> x55, local copies, waits for them, and re-layouts: 3.41 us -> 17.3 us
    pallas_call x1 -> x3, Pallas kernels: 42.4 us -> 33.1 us  [the longest x1 20.7 us: run_second(): pl.pallas_call(second_kernel, out_shape=(jax.ShapeDtypeStruct((ROWS * COL...]
    reshape x11 -> x1, local copies, waits for them, and re-layouts: 6.37 us -> 0.21 us  [gather_long(): return lax.all_to_all(shares, 'gx', 0, 0).reshape(192, A_HALF + B_HALF)]
    slice x14 -> x7, local copies, waits for them, and re-layouts: 9.18 us -> 3.17 us  [the longest x2 1.5 us: pack_weights(): head = [w_qkv[:, WIDTH:], w_qkv[:, :WIDTH]]]
    concatenate x6 -> x4, other arithmetic: 5.93 us -> 1.79 us  [the longest x1 0.99 us: halo_rows(): base = jnp.concatenate([n1[:1], latents, n0, n1[ROWS - 1:]], axis=0)]
    ppermute x15 -> x8, waiting for transfers between devices: 23.9 us -> 27.9 us  [the longest x1 7.86 us: halo_rows(): lax.ppermute(latents[1:], axes, ring(size, 2))]
  transfers between devices with their start and end apart: 16 -> 11, of which waited for: 4 -> 6; matrix products, arithmetic and copies ran while one was open for 15% -> 4% of each run, Pallas kernels for 1% -> 9%
where the time goes in v2:
time: 160 us; the launch traced here: 159 us
  starting transfers between devices  64.4 us (40%)
  Pallas kernels  35.6 us (22%)
  waiting for transfers between devices  27.9 us (17%)
  local copies, waits for them, and re-layouts  24.3 us (15%)
  other arithmetic  4.69 us (3%)
  between operations  1.79 us (1%)
    pallas_call x1, Pallas kernels, run_second(): pl.pallas_call(second_kernel, out_shape=(jax.ShapeDtypeStruct((ROWS * COL...  20.7 us
    unnamed x55, local copies, waits for them, and re-layouts  17.3 us
    all_to_all x1, starting transfers between devices, gather_long(): return lax.all_to_all(shares, 'gx', 0, 0).reshape(192, A_HALF + B_HALF)  16.5 us
    all_to_all x2, starting transfers between devices, gather_short(): lax.all_to_all(jnp.broadcast_to(block[None], (count,) + block.shape), 'pa...  13.2 us
    pallas_call x1, Pallas kernels, run_first(): pl.pallas_call(first_kernel, out_shape=jax.ShapeDtypeStruct((N_MID, WIDTH...  12.4 us
    ppermute x1, starting transfers between devices, halo_rows(): lax.ppermute(latents[:RAD], axes, ring(size, -2))  9.98 us
    ppermute x1, starting transfers between devices, halo_rows(): lax.ppermute(base[:-1], axes, ring(size, -1))  8.49 us
    ppermute x1, waiting for transfers between devices, halo_rows(): lax.ppermute(latents[1:], axes, ring(size, 2))  7.86 us
  transfers between devices with their start and end apart: 11, of which 6 were waited for; matrix products, arithmetic and copies ran while one was open for 4% of the time, Pallas kernels for 9%

profile of v2, /device:TPU:1, one launch (start us, length us, event | category | flops | bytes accessed | tf_op | source)
XLA Modules:
  0.0 158.7 jit_solution(5559162279705281102)
XLA Ops:
  5.4 16.5 %all-to-all-start = ((bf16[32,6,1664]{2,1,0:T(8,128)(2,1)}), bf16[32,6,1664]{2,1,0:T(8,128)(2,1)S(1)}, u32[]{:S(2)}, u32[]{:S(2)}) async-start(bf16[32,6,1664]{2,1,0:T(8,128)(2,1)} %broadcast_in_dim.54), calls=%async_computation | async-start | bytes 1703936 | tf_op jit(solution)/shard_map/all_to_all | solution.py:532
  23.0 3.1 %collective-permute-start.1 = (bf16[9,32,768]{2,1,0:T(8,128)(2,1)}, bf16[9,32,768]{2,1,0:T(8,128)(2,1)S(1)}, u32[]{:S(2)}, u32[]{:S(2)}) collective-permute-start(bf16[9,32,768]{2,1,0:T(8,128)(2,1)} %get-tuple-element.59), channel_id=1, source_target_pairs={{0,1},{1,2},{2,3},{3,16},{16,17},{17,18},{18,19},{19,32},{32,33},{... | collective-permute-start | bytes 1327112 | tf_op jit(solution)/shard_map/ppermute | solution.py:508
  26.1 8.5 %collective-permute-start.2 = (bf16[9,32,768]{2,1,0:T(8,128)(2,1)}, bf16[9,32,768]{2,1,0:T(8,128)(2,1)S(1)}, u32[]{:S(2)}, u32[]{:S(2)}) collective-permute-start(bf16[9,32,768]{2,1,0:T(8,128)(2,1)} %get-tuple-element.58), channel_id=1, source_target_pairs={{0,499},{1,0},{2,1},{3,2},{16,3},{17,16},{18,17},{19,18},{32,19},{... | collective-permute-start | bytes 1327112 | tf_op jit(solution)/shard_map/ppermute | solution.py:511
  35.3 1.9 %collective-permute-start = (bf16[3,32,768]{2,1,0:T(8,128)(2,1)}, bf16[3,32,768]{2,1,0:T(8,128)(2,1)S(1)}, u32[]{:S(2)}, u32[]{:S(2)}) collective-permute-start(bf16[3,32,768]{2,1,0:T(8,128)(2,1)} %get-tuple-element.63), channel_id=1, source_target_pairs={{0,2},{1,3},{2,16},{3,17},{16,18},{17,19},{18,32},{19,33},{32,34},... | collective-permute-start | bytes 442376 | tf_op jit(solution)/shard_map/ppermute | solution.py:507
  37.2 10.0 %collective-permute-start.3 = (bf16[3,32,768]{2,1,0:T(8,128)(2,1)S(1)}, bf16[3,32,768]{2,1,0:T(8,128)(2,1)S(1)}, u32[]{:S(2)}, u32[]{:S(2)}) collective-permute-start(bf16[3,32,768]{2,1,0:T(8,128)(2,1)S(1)} %get-tuple-element.62), channel_id=1, source_target_pairs={{0,498},{1,499},{2,0},{3,1},{16,2},{17,3},{18,16},{19,17},{32,18},... | collective-permute-start | bytes 442376 | tf_op jit(solution)/shard_map/ppermute | solution.py:512
  47.4 7.9 %collective-permute-done.far_low = bf16[3,32,768]{2,1,0:T(8,128)(2,1)S(1)} collective-permute-done((bf16[3,32,768]{2,1,0:T(8,128)(2,1)}, bf16[3,32,768]{2,1,0:T(8,128)(2,1)S(1)}, u32[]{:S(2)}, u32[]{:S(2)}) %collective-permute-start) | collective-permute-done | bytes 147488 | tf_op jit(solution)/shard_map/ppermute | solution.py:507
  55.3 6.0 %collective-permute-done.3.far_high = bf16[3,32,768]{2,1,0:T(8,128)(2,1)S(1)} collective-permute-done((bf16[3,32,768]{2,1,0:T(8,128)(2,1)S(1)}, bf16[3,32,768]{2,1,0:T(8,128)(2,1)S(1)}, u32[]{:S(2)}, u32[]{:S(2)}) %collective-permute-start.3) | collective-permute-done | bytes 147488 | tf_op jit(solution)/shard_map/ppermute | solution.py:512
  61.3 5.0 %collective-permute-done.1.low = bf16[9,32,768]{2,1,0:T(8,128)(2,1)S(1)} collective-permute-done((bf16[9,32,768]{2,1,0:T(8,128)(2,1)}, bf16[9,32,768]{2,1,0:T(8,128)(2,1)S(1)}, u32[]{:S(2)}, u32[]{:S(2)}) %collective-permute-start.1) | collective-permute-done | bytes 442400 | tf_op jit(solution)/shard_map/ppermute | solution.py:508
  66.4 1.4 broadcast_in_dim.55
  67.8 8.4 %all-to-all-start.1 = ((bf16[4,192,1152]{2,1,0:T(8,128)(2,1)}), bf16[4,192,1152]{2,1,0:T(8,128)(2,1)S(1)}, u32[]{:S(2)}, u32[]{:S(2)}) async-start(bf16[4,192,1152]{2,1,0:T(8,128)(2,1)} %broadcast_in_dim.55), calls=%async_computation.1 | async-start | bytes 3538944 | tf_op jit(solution)/shard_map/all_to_all | solution.py:537
  76.3 4.6 %collective-permute-start.4 = (bf16[288,768]{1,0:T(8,128)(2,1)S(1)}, bf16[288,768]{1,0:T(8,128)(2,1)S(1)}, u32[]{:S(2)}, u32[]{:S(2)}) collective-permute-start(bf16[288,768]{1,0:T(8,128)(2,1)S(1)} %get-tuple-element.40), channel_id=1, source_target_pairs={{0,4},{4,8},{8,12},{12,0},{1,5},{5,9},{9,13},{13,1},{2,6},{6,10},{... | collective-permute-start | bytes 1327112 | tf_op jit(solution)/shard_map/ppermute | solution.py:558
  80.9 1.9 %collective-permute-start.5 = (bf16[288,768]{1,0:T(8,128)(2,1)S(1)}, bf16[288,768]{1,0:T(8,128)(2,1)S(1)}, u32[]{:S(2)}, u32[]{:S(2)}) collective-permute-start(bf16[288,768]{1,0:T(8,128)(2,1)S(1)} %get-tuple-element.41), channel_id=1, source_target_pairs={{0,12},{4,0},{8,4},{12,8},{1,13},{5,1},{9,5},{13,9},{2,14},{6,2},{... | collective-permute-start | bytes 1327112 | tf_op jit(solution)/shard_map/ppermute | solution.py:559
  82.9 2.1 %fusion.3.feat_ref = bf16[1024,128]{1,0:T(8,128)(2,1)S(1)} fusion(f32[128]{0:T(128)S(1)} %copy-done.26, f32[128]{0:T(128)S(1)} %copy-done.25, f32[1024]{0:T(1024)S(1)} %bitcast.20, f32[1024]{0:T(1024)S(1)} %bitcast.19, pred[128]{0:T(512)(128)(4,1)S(1)} %copy-done.24), kind=kLoop, calls=%fused_computation.4 | loop fusion | flops 917504 | bytes 271488 | tf_op jit(solution)/shard_map/convert_element_type | solution.py:494
  85.0 2.2 %collective-permute-done.4.left_ref = bf16[288,768]{1,0:T(8,128)(2,1)S(1)} collective-permute-done((bf16[288,768]{1,0:T(8,128)(2,1)S(1)}, bf16[288,768]{1,0:T(8,128)(2,1)S(1)}, u32[]{:S(2)}, u32[]{:S(2)}) %collective-permute-start.4) | collective-permute-done | bytes 442400 | tf_op jit(solution)/shard_map/ppermute | solution.py:558
  87.2 5.2 %collective-permute-done.5.right_ref = bf16[288,768]{1,0:T(8,128)(2,1)S(1)} collective-permute-done((bf16[288,768]{1,0:T(8,128)(2,1)S(1)}, bf16[288,768]{1,0:T(8,128)(2,1)S(1)}, u32[]{:S(2)}, u32[]{:S(2)}) %collective-permute-start.5) | collective-permute-done | bytes 442400 | tf_op jit(solution)/shard_map/ppermute | solution.py:559
  94.2 2.5 %prep.1 = (bf16[864,768]{1,0:T(8,128)(2,1)S(1)}, bf16[480,768]{1,0:T(8,128)(2,1)S(1)}, f32[480,768]{1,0:T(8,128)S(1)}, f32[240,768]{1,0:T(8,128)S(1)}) custom-call(bf16[3,32,768]{2,1,0:T(8,128)(2,1)S(1)} %copy-done.3, bf16[9,32,768]{2,1,0:T(8,128)(2,1)S(1)} %collective-permute-done.1.low, bf16[4,32,768]{2,1,0:T(8,128)(2,1)S(1)} %copy-done, ...), custom_call_target="tpu_custom_call" | custom-call | flops 1585446912 | bytes 8000000 | tf_op jit(solution)/shard_map/prep/pallas_call | solution.py:400
  96.7 1.1 copy-done.10
  97.8 1.1 copy-done.12
  100.6 1.9 %collective-permute-start.6 = (bf16[768,1152]{1,0:T(8,128)(2,1)S(1)}, bf16[768,1152]{1,0:T(8,128)(2,1)}, u32[]{:S(2)}, u32[]{:S(2)}) collective-permute-start(bf16[768,1152]{1,0:T(8,128)(2,1)S(1)} %bitcast.14), channel_id=1, source_target_pairs={{0,4},{4,0},{8,12},{12,8},{1,5},{5,1},{9,13},{13,9},{2,6},{6,2},{1... | collective-permute-start | bytes 5308424 | tf_op jit(solution)/shard_map/ppermute | solution.py:566
  105.2 4.8 %all-to-all-start.2 = ((bf16[4,192,512]{2,1,0:T(8,128)(2,1)}), bf16[4,192,512]{2,1,0:T(8,128)(2,1)S(1)}, u32[]{:S(2)}, u32[]{:S(2)}) async-start(bf16[4,192,512]{2,1,0:T(8,128)(2,1)} %broadcast_in_dim.64), calls=%async_computation.2 | async-start | bytes 1572864 | tf_op jit(solution)/shard_map/all_to_all | solution.py:537
  110.0 1.3 copy-done.7
  111.3 1.3 copy-done.13
  112.6 1.1 copy-done.17
  113.7 12.4 %first_step.1.att0_ref = bf16[480,768]{1,0:T(8,128)(2,1)S(1)} custom-call(s32[2]{0:T(128)S(1)} %pad_add_fusion.place_ref, bf16[864,768]{1,0:T(8,128)(2,1)S(1)} %copy-done.13, bf16[480,768]{1,0:T(8,128)(2,1)S(1)} %copy-done.17, bf16[768,768]{1,0:T(8,128)(2,1)S(1)} %copy-done.7, bf16[768,1152]{1,0:T(8,128)(2,1)S(1)} %bitcast.15, ...), custom_call_target="tpu_custom_call" | custom-call | flops 8000000000 | bytes 8000000 | tf_op jit(solution)/shard_map/first_step/pallas_call | solution.py:427
  127.0 2.9 %collective-permute-start.7 = (bf16[768,512]{1,0:T(8,128)(2,1)S(1)}, bf16[768,512]{1,0:T(8,128)(2,1)}, u32[]{:S(2)}, u32[]{:S(2)}) collective-permute-start(bf16[768,512]{1,0:T(8,128)(2,1)S(1)} %bitcast.17), channel_id=1, source_target_pairs={{0,4},{4,0},{8,12},{12,8},{1,5},{5,1},{9,13},{13,9},{2,6},{6,2},{1... | collective-permute-start | bytes 2359304 | tf_op jit(solution)/shard_map/ppermute | solution.py:570
  130.1 1.6 %collective-permute-done.7.other_b = bf16[768,512]{1,0:T(8,128)(2,1)} collective-permute-done((bf16[768,512]{1,0:T(8,128)(2,1)S(1)}, bf16[768,512]{1,0:T(8,128)(2,1)}, u32[]{:S(2)}, u32[]{:S(2)}) %collective-permute-start.7) | collective-permute-done | bytes 786464 | tf_op jit(solution)/shard_map/ppermute | solution.py:570
  131.7 1.3 copy-done.8
  133.0 1.3 copy-done.9
  134.2 1.4 copy-done.11
  135.6 1.1 copy-done.15
  136.7 1.1 copy-done.19
  137.8 20.7 %second_step.1 = (bf16[128,768]{1,0:T(8,128)(2,1)}, f32[3,1024]{1,0:T(4,128)}) custom-call(s32[2]{0:T(128)S(1)} %pad_add_fusion.place_ref, bf16[480,768]{1,0:T(8,128)(2,1)S(1)} %copy-done.19, f32[480,768]{1,0:T(8,128)S(1)} %copy-done.11, f32[240,768]{1,0:T(8,128)S(1)} %copy-done.15, f32[1,768]{1,0:T(1,128)S(1)} %broadcast_in_dim.56.gain_ref, ...), custom_call_target="tpu_custom_call" | custom-call | flops 8000000000 | bytes 14000000 | tf_op jit(solution)/shard_map/second_step/pallas_call | solution.py:450
  (70 shorter events, 13.5 us)
Async XLA Ops:
  0.6 21.3 %copy-start.1 = (bf16[2,4,32,768]{3,2,1,0:T(8,128)(2,1)S(1)}, bf16[2,4,32,768]{3,2,1,0:T(8,128)(2,1)}, u32[]{:S(2)}) copy-start(bf16[2,4,32,768]{3,2,1,0:T(8,128)(2,1)} %noise.1) | copy-start | bytes 1179652
  4.4 17.6 %copy-start = (bf16[4,32,768]{2,1,0:T(8,128)(2,1)S(1)}, bf16[4,32,768]{2,1,0:T(8,128)(2,1)}, u32[]{:S(2)}) copy-start(bf16[4,32,768]{2,1,0:T(8,128)(2,1)} %own.1) | copy-start | bytes 589828
  5.4 41.8 %all-to-all-start = ((bf16[32,6,1664]{2,1,0:T(8,128)(2,1)}), bf16[32,6,1664]{2,1,0:T(8,128)(2,1)S(1)}, u32[]{:S(2)}, u32[]{:S(2)}) async-start(bf16[32,6,1664]{2,1,0:T(8,128)(2,1)} %broadcast_in_dim.54), calls=%async_computation | async-start | bytes 1703936 | tf_op jit(solution)/shard_map/all_to_all | solution.py:532
  23.0 43.4 %collective-permute-start.1 = (bf16[9,32,768]{2,1,0:T(8,128)(2,1)}, bf16[9,32,768]{2,1,0:T(8,128)(2,1)S(1)}, u32[]{:S(2)}, u32[]{:S(2)}) collective-permute-start(bf16[9,32,768]{2,1,0:T(8,128)(2,1)} %get-tuple-element.59), channel_id=1, source_target_pairs={{0,1},{1,2},{2,3},{3,16},{16,17},{17,18},{18,19},{19,32},{32,33},{... | collective-permute-start | bytes 1327112 | tf_op jit(solution)/shard_map/ppermute | solution.py:508
  26.1 40.2 %collective-permute-start.2 = (bf16[9,32,768]{2,1,0:T(8,128)(2,1)}, bf16[9,32,768]{2,1,0:T(8,128)(2,1)S(1)}, u32[]{:S(2)}, u32[]{:S(2)}) collective-permute-start(bf16[9,32,768]{2,1,0:T(8,128)(2,1)} %get-tuple-element.58), channel_id=1, source_target_pairs={{0,499},{1,0},{2,1},{3,2},{16,3},{17,16},{18,17},{19,18},{32,19},{... | collective-permute-start | bytes 1327112 | tf_op jit(solution)/shard_map/ppermute | solution.py:511
  35.3 20.0 %collective-permute-start = (bf16[3,32,768]{2,1,0:T(8,128)(2,1)}, bf16[3,32,768]{2,1,0:T(8,128)(2,1)S(1)}, u32[]{:S(2)}, u32[]{:S(2)}) collective-permute-start(bf16[3,32,768]{2,1,0:T(8,128)(2,1)} %get-tuple-element.63), channel_id=1, source_target_pairs={{0,2},{1,3},{2,16},{3,17},{16,18},{17,19},{18,32},{19,33},{32,34},... | collective-permute-start | bytes 442376 | tf_op jit(solution)/shard_map/ppermute | solution.py:507
  37.2 24.1 %collective-permute-start.3 = (bf16[3,32,768]{2,1,0:T(8,128)(2,1)S(1)}, bf16[3,32,768]{2,1,0:T(8,128)(2,1)S(1)}, u32[]{:S(2)}, u32[]{:S(2)}) collective-permute-start(bf16[3,32,768]{2,1,0:T(8,128)(2,1)S(1)} %get-tuple-element.62), channel_id=1, source_target_pairs={{0,498},{1,499},{2,0},{3,1},{16,2},{17,3},{18,16},{19,17},{32,18},... | collective-permute-start | bytes 442376 | tf_op jit(solution)/shard_map/ppermute | solution.py:512
  47.4 20.3 %copy-start.20 = (bf16[192,1664]{1,0:T(8,128)(2,1)}, bf16[192,1664]{1,0:T(8,128)(2,1)S(1)}, u32[]{:S(2)}) copy-start(bf16[192,1664]{1,0:T(8,128)(2,1)S(1)} %reshape.27) | copy-start | bytes 1916932
  55.3 20.9 %copy-start.2 = (bf16[3,32,768]{2,1,0:T(8,128)(2,1)}, bf16[3,32,768]{2,1,0:T(8,128)(2,1)S(1)}, u32[]{:S(2)}) copy-start(bf16[3,32,768]{2,1,0:T(8,128)(2,1)S(1)} %collective-permute-done.far_low) | copy-start | bytes 442372
  61.3 14.9 %copy-start.4 = (bf16[3,32,768]{2,1,0:T(8,128)(2,1)}, bf16[3,32,768]{2,1,0:T(8,128)(2,1)S(1)}, u32[]{:S(2)}) copy-start(bf16[3,32,768]{2,1,0:T(8,128)(2,1)S(1)} %collective-permute-done.3.far_high) | copy-start | bytes 442372
  67.8 8.4 %copy-start.23 = (f32[768]{0:T(1024)S(1)}, f32[768]{0:T(1024)}, u32[]{:S(2)}) copy-start(f32[768]{0:T(1024)} %param.17) | copy-start | bytes 9220
  67.8 32.9 %all-to-all-start.1 = ((bf16[4,192,1152]{2,1,0:T(8,128)(2,1)}), bf16[4,192,1152]{2,1,0:T(8,128)(2,1)S(1)}, u32[]{:S(2)}, u32[]{:S(2)}) async-start(bf16[4,192,1152]{2,1,0:T(8,128)(2,1)} %broadcast_in_dim.55), calls=%async_computation.1 | async-start | bytes 3538944 | tf_op jit(solution)/shard_map/all_to_all | solution.py:537
  76.2 6.6 %copy-start.21 = (f32[2,1024]{1,0:T(2,128)S(1)}, f32[2,1024]{1,0:T(2,128)}, u32[]{:S(2)}) copy-start(f32[2,1024]{1,0:T(2,128)} %param.23) | copy-start | bytes 24580
  76.2 6.7 %copy-start.24 = (pred[128]{0:T(512)(128)(4,1)S(1)}, pred[128]{0:T(512)(128)(4,1)}, u32[]{:S(2)}) copy-start(pred[128]{0:T(512)(128)(4,1)} %constant.47) | copy-start | bytes 388
  76.2 6.7 %copy-start.25 = (f32[128]{0:T(128)S(1)}, f32[128]{0:T(128)}, u32[]{:S(2)}) copy-start(f32[128]{0:T(128)} %constant.48) | copy-start | bytes 1540
  76.2 6.7 %copy-start.26 = (f32[128]{0:T(128)S(1)}, f32[128]{0:T(128)}, u32[]{:S(2)}) copy-start(f32[128]{0:T(128)} %constant.49) | copy-start | bytes 1540
  76.2 16.2 %copy-start.6 = (bf16[768,768]{1,0:T(8,128)(2,1)S(1)}, bf16[768,768]{1,0:T(8,128)(2,1)}, u32[]{:S(2)}) copy-start(bf16[768,768]{1,0:T(8,128)(2,1)} %constant.33.clone.perm_ref) | copy-start | bytes 3538948
  76.3 10.9 %collective-permute-start.4 = (bf16[288,768]{1,0:T(8,128)(2,1)S(1)}, bf16[288,768]{1,0:T(8,128)(2,1)S(1)}, u32[]{:S(2)}, u32[]{:S(2)}) collective-permute-start(bf16[288,768]{1,0:T(8,128)(2,1)S(1)} %get-tuple-element.40), channel_id=1, source_target_pairs={{0,4},{4,8},{8,12},{12,0},{1,5},{5,9},{9,13},{13,1},{2,6},{6,10},{... | collective-permute-start | bytes 1327112 | tf_op jit(solution)/shard_map/ppermute | solution.py:558
  80.9 11.5 %collective-permute-start.5 = (bf16[288,768]{1,0:T(8,128)(2,1)S(1)}, bf16[288,768]{1,0:T(8,128)(2,1)S(1)}, u32[]{:S(2)}, u32[]{:S(2)}) collective-permute-start(bf16[288,768]{1,0:T(8,128)(2,1)S(1)} %get-tuple-element.41), channel_id=1, source_target_pairs={{0,12},{4,0},{8,4},{12,8},{1,13},{5,1},{9,5},{13,9},{2,14},{6,2},{... | collective-permute-start | bytes 1327112 | tf_op jit(solution)/shard_map/ppermute | solution.py:559
  96.7 1.1 copy-start.10
  100.6 9.4 %collective-permute-start.6 = (bf16[768,1152]{1,0:T(8,128)(2,1)S(1)}, bf16[768,1152]{1,0:T(8,128)(2,1)}, u32[]{:S(2)}, u32[]{:S(2)}) collective-permute-start(bf16[768,1152]{1,0:T(8,128)(2,1)S(1)} %bitcast.14), channel_id=1, source_target_pairs={{0,4},{4,0},{8,12},{12,8},{1,5},{5,1},{9,13},{13,9},{2,6},{6,2},{1... | collective-permute-start | bytes 5308424 | tf_op jit(solution)/shard_map/ppermute | solution.py:566
  105.2 21.8 %all-to-all-start.2 = ((bf16[4,192,512]{2,1,0:T(8,128)(2,1)}), bf16[4,192,512]{2,1,0:T(8,128)(2,1)S(1)}, u32[]{:S(2)}, u32[]{:S(2)}) async-start(bf16[4,192,512]{2,1,0:T(8,128)(2,1)} %broadcast_in_dim.64), calls=%async_computation.2 | async-start | bytes 1572864 | tf_op jit(solution)/shard_map/all_to_all | solution.py:537
  110.0 1.3 copy-start.7
  111.3 1.3 copy-start.13
  112.6 1.1 copy-start.17
  113.7 16.1 %copy-start.22 = (s32[1024]{0:T(1024)S(1)}, s32[1024]{0:T(1024)}, u32[]{:S(2)}) copy-start(s32[1024]{0:T(1024)} %param.22) | copy-start | bytes 12292
  127.0 4.7 %collective-permute-start.7 = (bf16[768,512]{1,0:T(8,128)(2,1)S(1)}, bf16[768,512]{1,0:T(8,128)(2,1)}, u32[]{:S(2)}, u32[]{:S(2)}) collective-permute-start(bf16[768,512]{1,0:T(8,128)(2,1)S(1)} %bitcast.17), channel_id=1, source_target_pairs={{0,4},{4,0},{8,12},{12,8},{1,5},{5,1},{9,13},{13,9},{2,6},{6,2},{1... | collective-permute-start | bytes 2359304 | tf_op jit(solution)/shard_map/ppermute | solution.py:570
  131.7 1.3 copy-start.8
  133.0 1.3 copy-start.9
  134.2 1.4 copy-start.11
  135.6 1.1 copy-start.15
  136.7 1.1 copy-start.19
  (6 other events, 5.5 us)

commit v3 on v2

--- a/solution.py
+++ b/solution.py
@@ -33,9 +33,8 @@
 N_END = END_ROWS * PITCH1
 PAIR = 2 * PITCH1
 KEYS = 384
-A_HALF = 1152
-B_HALF = 512
-N_PAD = 544
+HALF = 1664
+TAIL = 3 * WIDTH
 BLOCK = 128
 SWAP = [(0, 1), (1, 0), (2, 3), (3, 2)]
 NEG = -1e30
@@ -177,21 +176,6 @@
     return result.astype(BF)
 
 
-def start_copies(core, pieces, target, sems, width):
-    def copy_of(slot, ref, at):
-        start = pl.multiple_of(at * width, 128)
-        return pltpu.make_async_copy(ref, target.at[:, pl.ds(start, width)], sems.at[slot])
-
-    copy_of(0, pieces[0], core).start()
-    copy_of(1, pieces[1], 1 - core).start()
-
-    def wait():
-        copy_of(0, pieces[0], core).wait()
-        copy_of(1, pieces[1], 1 - core).wait()
-
-    return wait
-
-
 def project(source, weights, column, target, rows, scale=None):
     for t in range(0, WIDTH, 256):
         product = jnp.dot(
@@ -204,62 +188,33 @@
         target[0:rows, t : t + 256] = product.astype(BF).astype(target.dtype)
 
 
-def first_kernel(
-    place_ref, nk_ref, nq_ref, perm_ref, mine, other, att_ref, weights, keys, values, queries, att, sems
-):
-    wait = start_copies(place_ref[0], (mine, other), weights, sems, A_HALF)
-    q_row, q_col, k_row, k_col = window_mask(PITCH0, 8)
-    inside = (
-        (k_row >= q_row)
-        & (k_row <= q_row + 2 * RAD)
-        & (k_col >= q_col + EDGE - HALO1 - RAD)
-        & (k_col <= q_col + EDGE - HALO1 + RAD)
-    )
-    mask = jnp.where(inside, 0.0, NEG).astype(F32)
-    wait()
-    project(nk_ref, weights, 0, keys, N_KEY0)
-    project(nk_ref, weights, WIDTH, values, N_KEY0)
-    project(nq_ref, weights, 2 * WIDTH, queries, N_MID, SCALE)
-
-    def attend0(j, carry):
-        q_at = pl.multiple_of(j * PAIR, PAIR)
-        k_at = pl.multiple_of(j * 2 * PITCH0, 2 * PITCH0)
-        for g in range(3):
-            cols = slice(256 * g, 256 * g + 256)
-            att[pl.ds(q_at, PAIR), cols] = attend(
-                queries[pl.ds(q_at, PAIR), cols],
-                keys[pl.ds(k_at, KEYS), cols],
-                values[pl.ds(k_at, KEYS), cols],
-                mask,
-            )
-        return carry
-
-    lax.fori_loop(0, MID_ROWS // 2, attend0, 0)
-    att_ref[...] = jnp.dot(
-        att[...], perm_ref[...], preferred_element_type=F32
-    ).astype(BF)
-
-
-def second_kernel(
+def main_kernel(
     place_ref,
-    att0_ref,
+    gain_ref,
+    nk_any,
+    nq_any,
+    base_any,
+    noise_any,
+    feat_any,
+    cell_any,
+    perm_any,
+    pick_any,
+    mine,
+    other,
+    latent_ref,
+    probe_ref,
+    weights,
+    nk_ref,
+    nq_ref,
     base_ref,
     noise_ref,
-    gain_ref,
     feat_ref,
     cell_ref,
     perm_ref,
     pick_ref,
-    mine_a,
-    other_a,
-    mine_b,
-    other_b,
-    latent_ref,
-    probe_ref,
-    weights,
-    tail,
     keys,
     values,
+    q_low,
     queries,
     att,
     att_perm,
@@ -268,26 +223,81 @@
     lat_end,
     end_low,
     probe_query,
-    sems_a,
-    sems_b,
+    half_sems,
+    sems,
 ):
+    core = place_ref[0]
     live = place_ref[1]
-    wait_b = start_copies(place_ref[0], (mine_b, other_b), tail, sems_b, B_HALF)
-    wait_a = start_copies(place_ref[0], (mine_a, other_a), weights, sems_a, A_HALF)
-    wait_b()
-
+
+    def half(ref, slot):
+        start = pl.multiple_of(slot * HALF, 128)
+        return pltpu.make_async_copy(
+            ref, weights.at[:, pl.ds(start, HALF)], half_sems.at[slot]
+        )
+
+    pairs = (
+        (nk_any, nk_ref),
+        (nq_any, nq_ref),
+        (perm_any, perm_ref),
+        (base_any, base_ref),
+        (noise_any, noise_ref),
+        (pick_any, pick_ref),
+        (feat_any, feat_ref),
+        (cell_any, cell_ref),
+    )
+    loads = [pltpu.make_async_copy(a, b, sems.at[n]) for n, (a, b) in enumerate(pairs)]
+    loads[0].start()
+    half(mine, core).start()
+    half(other, 1 - core).start()
+    for load in loads[1:]:
+        load.start()
+
+    q_row, q_col, k_row, k_col = window_mask(PITCH0, 8)
+    inside = (
+        (k_row >= q_row)
+        & (k_row <= q_row + 2 * RAD)
+        & (k_col >= q_col + EDGE - HALO1 - RAD)
+        & (k_col <= q_col + EDGE - HALO1 + RAD)
+    )
+    mask = jnp.where(inside, 0.0, NEG).astype(F32)
+    loads[0].wait()
+    half(mine, 0).wait()
+    project(nk_ref, weights, 0, keys, N_KEY0)
+    project(nk_ref, weights, WIDTH, values, N_KEY0)
+    loads[1].wait()
+    half(mine, 1).wait()
+    project(nq_ref, weights, 2 * WIDTH, q_low, N_MID, SCALE)
+
+    def attend0(j, carry):
+        q_at = pl.multiple_of(j * PAIR, PAIR)
+        k_at = pl.multiple_of(j * 2 * PITCH0, 2 * PITCH0)
+        for g in range(3):
+            cols = slice(256 * g, 256 * g + 256)
+            att[pl.ds(q_at, PAIR), cols] = attend(
+                q_low[pl.ds(q_at, PAIR), cols],
+                keys[pl.ds(k_at, KEYS), cols],
+                values[pl.ds(k_at, KEYS), cols],
+                mask,
+            )
+        return carry
+
+    lax.fori_loop(0, MID_ROWS // 2, attend0, 0)
+    for load in loads[2:]:
+        load.wait()
+    att_perm[...] = jnp.dot(att[...], perm_ref[...], preferred_element_type=F32).astype(BF)
     for t in range(3):
         cols = slice(256 * t, 256 * t + 256)
-        update = jnp.dot(att0_ref[...], tail[:, cols], preferred_element_type=F32)
+        update = jnp.dot(
+            att_perm[...],
+            weights[:, TAIL + 256 * t : TAIL + 256 * t + 256],
+            preferred_element_type=F32,
+        )
         fresh = base_ref[:, cols] + update / STEPS
         lat_mid[:, cols] = fresh.astype(BF).astype(F32)
 
     mid_perm[...] = jnp.dot(
         rms(lat_mid[...], gain_ref[...]), perm_ref[...], preferred_element_type=F32
     ).astype(BF)
-    keys[N_MID:] = jnp.zeros((N_PAD - N_MID, WIDTH), BF)
-    values[N_MID:] = jnp.zeros((N_PAD - N_MID, WIDTH), BF)
-    wait_a()
     project(mid_perm, weights, 0, keys, N_MID)
     project(mid_perm, weights, WIDTH, values, N_MID)
     project(mid_perm.at[112:368], weights, 2 * WIDTH, queries, 256, SCALE)
@@ -314,12 +324,18 @@
         return carry
 
     lax.fori_loop(0, END_ROWS // 2, attend1, 0)
-    att_perm[...] = jnp.dot(att[...], perm_ref[...], preferred_element_type=F32).astype(BF)
+    att_perm[0:N_END] = jnp.dot(
+        att[0:N_END], perm_ref[...], preferred_element_type=F32
+    ).astype(BF)
 
     lat_end[N_END:] = jnp.zeros((256 - N_END, WIDTH), F32)
     for t in range(3):
         cols = slice(256 * t, 256 * t + 256)
-        update = jnp.dot(att_perm[...], tail[:, cols], preferred_element_type=F32)
+        update = jnp.dot(
+            att_perm[0:N_END],
+            weights[:, TAIL + 256 * t : TAIL + 256 * t + 256],
+            preferred_element_type=F32,
+        )
         fresh = (
             lat_mid[RAD * PITCH1 : RAD * PITCH1 + N_END, cols]
             + update / STEPS
@@ -332,7 +348,7 @@
 
     end_low[...] = lat_end[...].astype(BF)
     query_rows = jnp.dot(
-        pick_ref[...], tail[:, 768:896], preferred_element_type=F32
+        pick_ref[...], weights[:, TAIL + 768 : TAIL + 896], preferred_element_type=F32
     ).astype(BF)
     for i in range(6):
         probe_query[:, 128 * i : 128 * i + 128] = (
@@ -341,7 +357,7 @@
             )
             * SCALE
         ).astype(BF)
-    head_rows = jnp.dot(perm_ref[...], tail[:, 896:1024], preferred_element_type=F32)
+    head_rows = jnp.dot(perm_ref[...], weights[:, TAIL + 896 : TAIL + 1024], preferred_element_type=F32)
     head_turned = head_rows.T[0:8].astype(BF)
 
     spot = lax.broadcasted_iota(jnp.int32, (BLOCK, 256), 1)
@@ -389,7 +405,7 @@
         in_specs=[vmem] * 6,
         out_specs=(vmem,) * 2,
         scratch_shapes=[pltpu.VMEM((N_EDGE, WIDTH), F32)] * 2,
-        compiler_params=pltpu.CompilerParams(vmem_limit_bytes=12 * 1024 * 1024),
+        compiler_params=pltpu.CompilerParams(vmem_limit_bytes=60 * 1024 * 1024),
         cost_estimate=pl.CostEstimate(flops=0, bytes_accessed=3_000_000, transcendentals=0),
         name="pack",
     )(*rows)
@@ -413,7 +429,7 @@
             pltpu.VMEM((N_KEY0, WIDTH), BF),
             pltpu.VMEM((N_MID, WIDTH), F32),
         ],
-        compiler_params=pltpu.CompilerParams(vmem_limit_bytes=20 * 1024 * 1024),
+        compiler_params=pltpu.CompilerParams(vmem_limit_bytes=60 * 1024 * 1024),
         cost_estimate=pl.CostEstimate(
             flops=2 * (N_KEY0 + N_MID) * WIDTH * WIDTH, bytes_accessed=8_000_000, transcendentals=0
         ),
@@ -421,64 +437,41 @@
     )(*rows, left, right, gain, perm)
 
 
-def run_first(place, nk, nq, perm, mine, other):
+def run_main(place, gain, arrays, mine, other):
     vmem = pl.BlockSpec(memory_space=pltpu.VMEM)
-    anywhere = pl.BlockSpec(memory_space=pl.ANY)
+    probes = arrays[5].shape[0]
     return pl.pallas_call(
-        first_kernel,
-        out_shape=jax.ShapeDtypeStruct((N_MID, WIDTH), BF),
-        in_specs=[pl.BlockSpec(memory_space=pltpu.SMEM), vmem, vmem, vmem, anywhere, anywhere],
-        out_specs=vmem,
-        scratch_shapes=[
-            pltpu.VMEM((WIDTH, 3 * WIDTH), BF),
+        main_kernel,
+        out_shape=(
+            jax.ShapeDtypeStruct((ROWS * COLS, WIDTH), BF),
+            jax.ShapeDtypeStruct((CH, probes), F32),
+        ),
+        in_specs=[pl.BlockSpec(memory_space=pltpu.SMEM), vmem]
+        + [pl.BlockSpec(memory_space=pl.ANY)] * (len(arrays) + 2),
+        out_specs=(vmem, vmem),
+        scratch_shapes=[pltpu.VMEM((WIDTH, 2 * HALF), BF)]
+        + [pltpu.VMEM(a.shape, a.dtype) for a in arrays]
+        + [
             pltpu.VMEM((N_KEY0, WIDTH), BF),
             pltpu.VMEM((N_KEY0, WIDTH), BF),
             pltpu.VMEM((N_MID, WIDTH), BF),
+            pltpu.VMEM((256, WIDTH), F32),
             pltpu.VMEM((N_MID, WIDTH), BF),
-            pltpu.SemaphoreType.DMA((2,)),
-        ],
-        compiler_params=pltpu.CompilerParams(vmem_limit_bytes=22 * 1024 * 1024),
-        cost_estimate=pl.CostEstimate(
-            flops=8_000_000_000, bytes_accessed=8_000_000, transcendentals=2_500_000
-        ),
-        name="first_step",
-    )(place, nk, nq, perm, mine, other)
-
-
-def run_second(place, att, base, noise, gain, feat, cell, perm, pick, pieces):
-    vmem = pl.BlockSpec(memory_space=pltpu.VMEM)
-    return pl.pallas_call(
-        second_kernel,
-        out_shape=(
-            jax.ShapeDtypeStruct((ROWS * COLS, WIDTH), BF),
-            jax.ShapeDtypeStruct((CH, cell.shape[0]), F32),
-        ),
-        in_specs=[pl.BlockSpec(memory_space=pltpu.SMEM)]
-        + [vmem] * 8
-        + [pl.BlockSpec(memory_space=pl.ANY)] * 4,
-        out_specs=(vmem, vmem),
-        scratch_shapes=[
-            pltpu.VMEM((WIDTH, 3 * WIDTH), BF),
-            pltpu.VMEM((WIDTH, 2 * B_HALF), BF),
-            pltpu.VMEM((N_PAD, WIDTH), BF),
-            pltpu.VMEM((N_PAD, WIDTH), BF),
-            pltpu.VMEM((256, WIDTH), F32),
-            pltpu.VMEM((N_END, WIDTH), BF),
-            pltpu.VMEM((N_END, WIDTH), BF),
+            pltpu.VMEM((N_MID, WIDTH), BF),
             pltpu.VMEM((N_MID, WIDTH), F32),
             pltpu.VMEM((N_MID, WIDTH), BF),
             pltpu.VMEM((256, WIDTH), F32),
             pltpu.VMEM((256, WIDTH), BF),
-            pltpu.VMEM((cell.shape[0], WIDTH), BF),
+            pltpu.VMEM((probes, WIDTH), BF),
             pltpu.SemaphoreType.DMA((2,)),
-            pltpu.SemaphoreType.DMA((2,)),
+            pltpu.SemaphoreType.DMA((len(arrays),)),
         ],
-        compiler_params=pltpu.CompilerParams(vmem_limit_bytes=26 * 1024 * 1024),
+        compiler_params=pltpu.CompilerParams(vmem_limit_bytes=60 * 1024 * 1024),
         cost_estimate=pl.CostEstimate(
-            flops=8_000_000_000, bytes_accessed=14_000_000, transcendentals=4_500_000
+            flops=16_000_000_000, bytes_accessed=16_000_000, transcendentals=7_000_000
         ),
-        name="second_step",
-    )(place, att, base, noise, gain, feat, cell, perm, pick, *pieces)
+        name="denoise_decode",
+    )(place, gain, *arrays, mine, other)
 
 
 def features_of(offsets):
@@ -514,22 +507,22 @@
 
 
 def pack_weights(w_qkv, w_out, w_query, w_head, core):
-    head = [w_qkv[:, WIDTH:], w_qkv[:, :WIDTH]]
-    tail = [w_out, w_query.reshape(6, 128), jnp.pad(w_head, ((0, 0), (0, 128 - CH)))]
-    a = jnp.concatenate(head, axis=1)
-    b = jnp.concatenate(tail, axis=1)
-    mine = jnp.concatenate(
+    pack = jnp.concatenate(
         [
-            lax.dynamic_slice_in_dim(a, core * A_HALF, A_HALF, 1),
-            lax.dynamic_slice_in_dim(b, core * B_HALF, B_HALF, 1),
+            w_qkv[:, WIDTH:],
+            w_qkv[:, :WIDTH],
+            w_out,
+            w_query.reshape(6, 128),
+            jnp.pad(w_head, ((0, 0), (0, 128 - CH))),
         ],
         axis=1,
     )
+    mine = lax.dynamic_slice_in_dim(pack, core * HALF, HALF, 1)
     return jnp.broadcast_to(mine[None], (lax.axis_size("gx"),) + mine.shape)
 
 
 def gather_long(shares):
-    return lax.all_to_all(shares, "gx", 0, 0).reshape(192, A_HALF + B_HALF)
+    return lax.all_to_all(shares, "gx", 0, 0).reshape(192, HALF)
 
 
 def gather_short(block):
@@ -553,25 +546,15 @@
     shares, latents, noise = barrier((shares, latents, noise))
     rows = halo_rows(latents, noise)
     block, rows = barrier((gather_long(shares), rows))
-    wide_a = gather_short(block[:, :A_HALF])
+    wide = gather_short(block)
     to_high, to_low = run_pack(rows)
     left = lax.ppermute(to_high, "gy", ring(cols, 1))
     right = lax.ppermute(to_low, "gy", ring(cols, -1))
-    nk, nq, base, tail_noise = run_prep(rows, left, right, gain, perm)
-    feat = features_of(probe_offset)
-    cell = probe_cell[:, None]
-    wide_a, nk, nq, base, tail_noise, feat, cell, block = barrier(
-        (wide_a, nk, nq, base, tail_noise, feat, cell, block)
-    )
-    other_a = lax.ppermute(wide_a, "gy", SWAP)
-    wide_b = gather_short(block[:, A_HALF:])
-    att = run_first(place, nk, nq, perm, wide_a, other_a)
-    wide_b, att = barrier((wide_b, att))
-    other_b = lax.ppermute(wide_b, "gy", SWAP)
-    latent, probes = run_second(
-        place, att, base, tail_noise, gain, feat, cell, perm, pick,
-        (wide_a, other_a, wide_b, other_b),
-    )
+    nk, nq, base, fresh = run_prep(rows, left, right, gain, perm)
+    arrays = (nk, nq, base, fresh, features_of(probe_offset), probe_cell[:, None], perm, pick)
+    wide, arrays = barrier((wide, arrays))
+    other = lax.ppermute(wide, "gy", SWAP)
+    latent, probes = run_main(place, gain, arrays, wide, other)
     return latent.reshape(latents.shape), probes
 
 

time: 160 us -> 150 us (0.938)
  local copies, waits for them, and re-layouts: 24.3 us -> 8.35 us
  starting transfers between devices: 64.4 us -> 54.9 us
  waiting for transfers between devices: 27.9 us -> 36.8 us
  Pallas kernels: 35.6 us -> 42.8 us
    unnamed x55 -> x35, local copies, waits for them, and re-layouts: 17.3 us -> 3.83 us
    ppermute x1, waiting for transfers between devices: 6.04 us -> 16.3 us  [halo_rows(): lax.ppermute(latents[:RAD], axes, ring(size, -2))]
    ppermute x1, waiting for transfers between devices: 7.86 us -> 0.01 us  [halo_rows(): lax.ppermute(latents[1:], axes, ring(size, 2))]
    ppermute x1, starting transfers between devices: 9.98 us -> 3.63 us  [halo_rows(): lax.ppermute(latents[:RAD], axes, ring(size, -2))]
    all_to_all x2 -> x1, starting transfers between devices: 13.2 us -> 8.41 us  [gather_short(): lax.all_to_all(jnp.broadcast_to(block[None], (count,) + block.shape), 'pa...]
    pallas_call x1, Pallas kernels: 2.47 us -> 6.15 us  [run_prep(): pl.pallas_call(prep_kernel, out_shape=(jax.ShapeDtypeStruct((N_KEY0, WIDT...]
    all_to_all x1, waiting for transfers between devices: 0.01 us -> 3.62 us  [gather_long(): return lax.all_to_all(shares, 'gx', 0, 0).reshape(192, HALF)]
    all_to_all x2 -> x1, waiting for transfers between devices: 0.01 us -> 2.69 us  [gather_short(): lax.all_to_all(jnp.broadcast_to(block[None], (count,) + block.shape), 'pa...]
  transfers between devices with their start and end apart: 11 -> 9, of which waited for: 6 -> 7; matrix products, arithmetic and copies ran while one was open for 4% -> 4% of each run, Pallas kernels for 9% -> 6%
where the time goes in v3:
time: 150 us; the launch traced here: 149 us
  starting transfers between devices  54.9 us (37%)
  Pallas kernels  42.8 us (29%)
  waiting for transfers between devices  36.8 us (25%)
  local copies, waits for them, and re-layouts  8.35 us (6%)
  other arithmetic  4.95 us (3%)
  between operations  1.68 us (1%)
    pallas_call x1, Pallas kernels, run_main(): pl.pallas_call(main_kernel, out_shape=(jax.ShapeDtypeStruct((ROWS * COLS,...  34.3 us
    all_to_all x1, starting transfers between devices, gather_long(): return lax.all_to_all(shares, 'gx', 0, 0).reshape(192, HALF)  16.5 us
    ppermute x1, waiting for transfers between devices, halo_rows(): lax.ppermute(latents[:RAD], axes, ring(size, -2))  16.3 us
    ppermute x1, starting transfers between devices, halo_rows(): lax.ppermute(base[:-1], axes, ring(size, -1))  9.63 us
    all_to_all x1, starting transfers between devices, gather_short(): lax.all_to_all(jnp.broadcast_to(block[None], (count,) + block.shape), 'pa...  8.41 us
    pallas_call x1, Pallas kernels, run_prep(): pl.pallas_call(prep_kernel, out_shape=(jax.ShapeDtypeStruct((N_KEY0, WIDT...  6.15 us
    ppermute x1, waiting for transfers between devices, local(): right = lax.ppermute(to_low, 'gy', ring(cols, -1))  5.34 us
    ppermute x1, starting transfers between devices, local(): other = lax.ppermute(wide, 'gy', SWAP)  5.27 us
  transfers between devices with their start and end apart: 9, of which 7 were waited for; matrix products, arithmetic and copies ran while one was open for 4% of the time, Pallas kernels for 6%

profile of v3, /device:TPU:1, one launch (start us, length us, event | category | flops | bytes accessed | tf_op | source)
XLA Modules:
  0.0 149.5 jit_solution(11729198122590622696)
XLA Ops:
  0.7 0.8 copy.20
  1.5 0.7 slice_dynamic-update-slice_fusion
  2.2 0.7 slice_dynamic-update-slice_fusion.1
  2.9 0.7 reduce
  3.6 0.7 constant_dynamic-update-slice_fusion.2
  4.4 1.0 broadcast_in_dim.49
  5.4 16.5 %all-to-all-start = ((bf16[32,6,1664]{2,1,0:T(8,128)(2,1)}), bf16[32,6,1664]{2,1,0:T(8,128)(2,1)S(1)}, u32[]{:S(2)}, u32[]{:S(2)}) async-start(bf16[32,6,1664]{2,1,0:T(8,128)(2,1)} %broadcast_in_dim.49), calls=%async_computation | async-start | bytes 1703936 | tf_op jit(solution)/shard_map/all_to_all | solution.py:525
  21.9 0.9 pad_maximum_fusion.1
  22.8 9.6 %collective-permute-start.2 = (bf16[9,32,768]{2,1,0:T(8,128)(2,1)}, bf16[9,32,768]{2,1,0:T(8,128)(2,1)S(1)}, u32[]{:S(2)}, u32[]{:S(2)}) collective-permute-start(bf16[9,32,768]{2,1,0:T(8,128)(2,1)} %get-tuple-element.56), channel_id=1, source_target_pairs={{0,499},{1,0},{2,1},{3,2},{16,3},{17,16},{18,17},{19,18},{32,19},{... | collective-permute-start | bytes 1327112 | tf_op jit(solution)/shard_map/ppermute | solution.py:504
  32.4 1.9 %collective-permute-start.1 = (bf16[9,32,768]{2,1,0:T(8,128)(2,1)S(1)}, bf16[9,32,768]{2,1,0:T(8,128)(2,1)S(1)}, u32[]{:S(2)}, u32[]{:S(2)}) collective-permute-start(bf16[9,32,768]{2,1,0:T(8,128)(2,1)S(1)} %get-tuple-element.57), channel_id=1, source_target_pairs={{0,1},{1,2},{2,3},{3,16},{16,17},{17,18},{18,19},{19,32},{32,33},{... | collective-permute-start | bytes 1327112 | tf_op jit(solution)/shard_map/ppermute | solution.py:501
  34.4 3.6 %collective-permute-start.3 = (bf16[3,32,768]{2,1,0:T(8,128)(2,1)S(1)}, bf16[3,32,768]{2,1,0:T(8,128)(2,1)S(1)}, u32[]{:S(2)}, u32[]{:S(2)}) collective-permute-start(bf16[3,32,768]{2,1,0:T(8,128)(2,1)S(1)} %get-tuple-element.60), channel_id=1, source_target_pairs={{0,498},{1,499},{2,0},{3,1},{16,2},{17,3},{18,16},{19,17},{32,18},... | collective-permute-start | bytes 442376 | tf_op jit(solution)/shard_map/ppermute | solution.py:505
  38.0 3.2 %collective-permute-start = (bf16[3,32,768]{2,1,0:T(8,128)(2,1)S(1)}, bf16[3,32,768]{2,1,0:T(8,128)(2,1)S(1)}, u32[]{:S(2)}, u32[]{:S(2)}) collective-permute-start(bf16[3,32,768]{2,1,0:T(8,128)(2,1)S(1)} %get-tuple-element.61), channel_id=1, source_target_pairs={{0,2},{1,3},{2,16},{3,17},{16,18},{17,19},{18,32},{19,33},{32,34},... | collective-permute-start | bytes 442376 | tf_op jit(solution)/shard_map/ppermute | solution.py:500
  41.2 3.6 %all-to-all-done = bf16[32,6,1664]{2,1,0:T(8,128)(2,1)S(1)} async-done(((bf16[32,6,1664]{2,1,0:T(8,128)(2,1)}), bf16[32,6,1664]{2,1,0:T(8,128)(2,1)S(1)}, u32[]{:S(2)}, u32[]{:S(2)}) %all-to-all-start) | async-done | bytes 639008 | tf_op jit(solution)/shard_map/all_to_all | solution.py:525
  45.0 16.3 %collective-permute-done.3.far_high = bf16[3,32,768]{2,1,0:T(8,128)(2,1)S(1)} collective-permute-done((bf16[3,32,768]{2,1,0:T(8,128)(2,1)S(1)}, bf16[3,32,768]{2,1,0:T(8,128)(2,1)S(1)}, u32[]{:S(2)}, u32[]{:S(2)}) %collective-permute-start.3) | collective-permute-done | bytes 147488 | tf_op jit(solution)/shard_map/ppermute | solution.py:505
  61.3 4.9 %collective-permute-done.1.low = bf16[9,32,768]{2,1,0:T(8,128)(2,1)S(1)} collective-permute-done((bf16[9,32,768]{2,1,0:T(8,128)(2,1)S(1)}, bf16[9,32,768]{2,1,0:T(8,128)(2,1)S(1)}, u32[]{:S(2)}, u32[]{:S(2)}) %collective-permute-start.1) | collective-permute-done | bytes 442400 | tf_op jit(solution)/shard_map/ppermute | solution.py:501
  66.3 1.7 %broadcast_in_dim.50 = bf16[4,192,1664]{2,1,0:T(8,128)(2,1)} broadcast(bf16[192,1664]{1,0:T(8,128)(2,1)S(1)} %reshape.23), dimensions={1,2} | broadcast | bytes 3194880 | tf_op jit(solution)/shard_map/broadcast_in_dim | solution.py:530
  67.9 8.4 %all-to-all-start.1 = ((bf16[4,192,1664]{2,1,0:T(8,128)(2,1)}), bf16[4,192,1664]{2,1,0:T(8,128)(2,1)S(1)}, u32[]{:S(2)}, u32[]{:S(2)}) async-start(bf16[4,192,1664]{2,1,0:T(8,128)(2,1)} %broadcast_in_dim.50), calls=%async_computation.1 | async-start | bytes 5111808 | tf_op jit(solution)/shard_map/all_to_all | solution.py:530
  76.4 0.6 broadcast_in_dim.48.gain_ref
  77.0 2.3 %pack.1 = (bf16[288,768]{1,0:T(8,128)(2,1)}, bf16[288,768]{1,0:T(8,128)(2,1)}) custom-call(bf16[3,32,768]{2,1,0:T(8,128)(2,1)} %copy-done.6, bf16[9,32,768]{2,1,0:T(8,128)(2,1)} %copy-done.4, bf16[4,32,768]{2,1,0:T(8,128)(2,1)} %own.1, bf16[2,4,32,768]{3,2,1,0:T(8,128)(2,1)} %noise.1, bf16[9,32,768]{2,1,0:T(8,128)(2,1)} %copy-done.3, ...), custom_call_target="tpu_custom_call" | custom-call | bytes 3000000 | tf_op jit(solution)/shard_map/pack/pallas_call | solution.py:402
  79.3 4.4 %collective-permute-start.4 = (bf16[288,768]{1,0:T(8,128)(2,1)}, bf16[288,768]{1,0:T(8,128)(2,1)S(1)}, u32[]{:S(2)}, u32[]{:S(2)}) collective-permute-start(bf16[288,768]{1,0:T(8,128)(2,1)} %get-tuple-element.39), channel_id=1, source_target_pairs={{0,4},{4,8},{8,12},{12,0},{1,5},{5,9},{9,13},{13,1},{2,6},{6,10},{... | collective-permute-start | bytes 1327112 | tf_op jit(solution)/shard_map/ppermute | solution.py:551
  83.7 1.9 %collective-permute-start.5 = (bf16[288,768]{1,0:T(8,128)(2,1)}, bf16[288,768]{1,0:T(8,128)(2,1)S(1)}, u32[]{:S(2)}, u32[]{:S(2)}) collective-permute-start(bf16[288,768]{1,0:T(8,128)(2,1)} %get-tuple-element.40), channel_id=1, source_target_pairs={{0,12},{4,0},{8,4},{12,8},{1,13},{5,1},{9,5},{13,9},{2,14},{6,2},{... | collective-permute-start | bytes 1327112 | tf_op jit(solution)/shard_map/ppermute | solution.py:552
  85.7 2.8 %fusion.3.feat_any = bf16[1024,128]{1,0:T(8,128)(2,1)} fusion(f32[128]{0:T(128)S(1)} %copy-done.10, f32[128]{0:T(128)S(1)} %copy-done.11, f32[1024]{0:T(1024)S(1)} %bitcast.17, f32[1024]{0:T(1024)S(1)} %bitcast.16, pred[128]{0:T(512)(128)(4,1)S(1)} %copy-done.12), kind=kLoop, calls=%fused_computation.4 | loop fusion | flops 917504 | bytes 271488 | tf_op jit(solution)/shard_map/convert_element_type | solution.py:487
  88.5 1.9 %collective-permute-done.4.left_ref = bf16[288,768]{1,0:T(8,128)(2,1)S(1)} collective-permute-done((bf16[288,768]{1,0:T(8,128)(2,1)}, bf16[288,768]{1,0:T(8,128)(2,1)S(1)}, u32[]{:S(2)}, u32[]{:S(2)}) %collective-permute-start.4) | collective-permute-done | bytes 442400 | tf_op jit(solution)/shard_map/ppermute | solution.py:551
  90.4 5.3 %collective-permute-done.5.right_ref = bf16[288,768]{1,0:T(8,128)(2,1)S(1)} collective-permute-done((bf16[288,768]{1,0:T(8,128)(2,1)}, bf16[288,768]{1,0:T(8,128)(2,1)S(1)}, u32[]{:S(2)}, u32[]{:S(2)}) %collective-permute-start.5) | collective-permute-done | bytes 442400 | tf_op jit(solution)/shard_map/ppermute | solution.py:552
  95.7 0.8 copy-done.14
  96.5 6.2 %prep.1 = (bf16[864,768]{1,0:T(8,128)(2,1)}, bf16[480,768]{1,0:T(8,128)(2,1)}, f32[480,768]{1,0:T(8,128)}, f32[240,768]{1,0:T(8,128)}) custom-call(bf16[3,32,768]{2,1,0:T(8,128)(2,1)} %copy-done.6, bf16[9,32,768]{2,1,0:T(8,128)(2,1)} %copy-done.4, bf16[4,32,768]{2,1,0:T(8,128)(2,1)} %own.1, bf16[2,4,32,768]{3,2,1,0:T(8,128)(2,1)} %noise.1, ...), custom_call_target="tpu_custom_call" | custom-call | flops 1585446912 | bytes 8000000 | tf_op jit(solution)/shard_map/prep/pallas_call | solution.py:416
  102.7 2.7 %all-to-all-done.1 = bf16[4,192,1664]{2,1,0:T(8,128)(2,1)S(1)} async-done(((bf16[4,192,1664]{2,1,0:T(8,128)(2,1)}), bf16[4,192,1664]{2,1,0:T(8,128)(2,1)S(1)}, u32[]{:S(2)}, u32[]{:S(2)}) %all-to-all-start.1) | async-done | bytes 2555936 | tf_op jit(solution)/shard_map/all_to_all | solution.py:530
  105.4 5.3 %collective-permute-start.6 = (bf16[768,1664]{1,0:T(8,128)(2,1)S(1)}, bf16[768,1664]{1,0:T(8,128)(2,1)}, u32[]{:S(2)}, u32[]{:S(2)}) collective-permute-start(bf16[768,1664]{1,0:T(8,128)(2,1)S(1)} %bitcast.14), channel_id=1, source_target_pairs={{0,4},{4,0},{8,12},{12,8},{1,5},{5,1},{9,13},{13,9},{2,6},{6,2},{1... | collective-permute-start | bytes 7667720 | tf_op jit(solution)/shard_map/ppermute | solution.py:556
  111.3 0.6 pad_add_fusion.place_ref
  111.9 1.0 copy.19.cell_any
  112.9 2.1 %collective-permute-done.6.other = bf16[768,1664]{1,0:T(8,128)(2,1)} collective-permute-done((bf16[768,1664]{1,0:T(8,128)(2,1)S(1)}, bf16[768,1664]{1,0:T(8,128)(2,1)}, u32[]{:S(2)}, u32[]{:S(2)}) %collective-permute-start.6) | collective-permute-done | bytes 2555936 | tf_op jit(solution)/shard_map/ppermute | solution.py:556
  115.0 34.3 %denoise_decode.1 = (bf16[128,768]{1,0:T(8,128)(2,1)}, f32[3,1024]{1,0:T(4,128)}) custom-call(s32[2]{0:T(128)} %pad_add_fusion.place_ref, f32[1,768]{1,0:T(1,128)} %broadcast_in_dim.48.gain_ref, bf16[864,768]{1,0:T(8,128)(2,1)} %get-tuple-element.45.nk_any, bf16[480,768]{1,0:T(8,128)(2,1)} %get-tuple-element.46.nq_any, ...), custom_call_target="tpu_custom_call" | custom-call | flops 16000000000 | bytes 16000000 | tf_op jit(solution)/shard_map/denoise_decode/pallas_call | solution.py:443
  (39 shorter events, 0.4 us)
Async XLA Ops:
  0.6 21.3 %copy-start.2 = (bf16[2,4,32,768]{3,2,1,0:T(8,128)(2,1)S(1)}, bf16[2,4,32,768]{3,2,1,0:T(8,128)(2,1)}, u32[]{:S(2)}) copy-start(bf16[2,4,32,768]{3,2,1,0:T(8,128)(2,1)} %noise.1) | copy-start | bytes 1179652
  4.4 17.6 %copy-start.1 = (bf16[4,32,768]{2,1,0:T(8,128)(2,1)S(1)}, bf16[4,32,768]{2,1,0:T(8,128)(2,1)}, u32[]{:S(2)}) copy-start(bf16[4,32,768]{2,1,0:T(8,128)(2,1)} %own.1) | copy-start | bytes 589828
  5.4 39.5 %all-to-all-start = ((bf16[32,6,1664]{2,1,0:T(8,128)(2,1)}), bf16[32,6,1664]{2,1,0:T(8,128)(2,1)S(1)}, u32[]{:S(2)}, u32[]{:S(2)}) async-start(bf16[32,6,1664]{2,1,0:T(8,128)(2,1)} %broadcast_in_dim.49), calls=%async_computation | async-start | bytes 1703936 | tf_op jit(solution)/shard_map/all_to_all | solution.py:525
  22.8 38.5 %collective-permute-start.2 = (bf16[9,32,768]{2,1,0:T(8,128)(2,1)}, bf16[9,32,768]{2,1,0:T(8,128)(2,1)S(1)}, u32[]{:S(2)}, u32[]{:S(2)}) collective-permute-start(bf16[9,32,768]{2,1,0:T(8,128)(2,1)} %get-tuple-element.56), channel_id=1, source_target_pairs={{0,499},{1,0},{2,1},{3,2},{16,3},{17,16},{18,17},{19,18},{32,19},{... | collective-permute-start | bytes 1327112 | tf_op jit(solution)/shard_map/ppermute | solution.py:504
  32.4 33.8 %collective-permute-start.1 = (bf16[9,32,768]{2,1,0:T(8,128)(2,1)S(1)}, bf16[9,32,768]{2,1,0:T(8,128)(2,1)S(1)}, u32[]{:S(2)}, u32[]{:S(2)}) collective-permute-start(bf16[9,32,768]{2,1,0:T(8,128)(2,1)S(1)} %get-tuple-element.57), channel_id=1, source_target_pairs={{0,1},{1,2},{2,3},{3,16},{16,17},{17,18},{18,19},{19,32},{32,33},{... | collective-permute-start | bytes 1327112 | tf_op jit(solution)/shard_map/ppermute | solution.py:501
  34.4 26.9 %collective-permute-start.3 = (bf16[3,32,768]{2,1,0:T(8,128)(2,1)S(1)}, bf16[3,32,768]{2,1,0:T(8,128)(2,1)S(1)}, u32[]{:S(2)}, u32[]{:S(2)}) collective-permute-start(bf16[3,32,768]{2,1,0:T(8,128)(2,1)S(1)} %get-tuple-element.60), channel_id=1, source_target_pairs={{0,498},{1,499},{2,0},{3,1},{16,2},{17,3},{18,16},{19,17},{32,18},... | collective-permute-start | bytes 442376 | tf_op jit(solution)/shard_map/ppermute | solution.py:505
  38.0 23.3 %collective-permute-start = (bf16[3,32,768]{2,1,0:T(8,128)(2,1)S(1)}, bf16[3,32,768]{2,1,0:T(8,128)(2,1)S(1)}, u32[]{:S(2)}, u32[]{:S(2)}) collective-permute-start(bf16[3,32,768]{2,1,0:T(8,128)(2,1)S(1)} %get-tuple-element.61), channel_id=1, source_target_pairs={{0,2},{1,3},{2,16},{3,17},{16,18},{17,19},{18,32},{19,33},{32,34},... | collective-permute-start | bytes 442376 | tf_op jit(solution)/shard_map/ppermute | solution.py:500
  61.3 6.6 %copy-start.5 = (bf16[3,32,768]{2,1,0:T(8,128)(2,1)}, bf16[3,32,768]{2,1,0:T(8,128)(2,1)S(1)}, u32[]{:S(2)}) copy-start(bf16[3,32,768]{2,1,0:T(8,128)(2,1)S(1)} %collective-permute-done.3.far_high) | copy-start | bytes 442372
  61.3 6.6 %copy-start.6 = (bf16[3,32,768]{2,1,0:T(8,128)(2,1)}, bf16[3,32,768]{2,1,0:T(8,128)(2,1)S(1)}, u32[]{:S(2)}) copy-start(bf16[3,32,768]{2,1,0:T(8,128)(2,1)S(1)} %collective-permute-done.far_low) | copy-start | bytes 442372
  61.3 6.6 %copy-start.3 = (bf16[9,32,768]{2,1,0:T(8,128)(2,1)}, bf16[9,32,768]{2,1,0:T(8,128)(2,1)S(1)}, u32[]{:S(2)}) copy-start(bf16[9,32,768]{2,1,0:T(8,128)(2,1)S(1)} %collective-permute-done.2.high) | copy-start | bytes 1327108
  66.3 1.7 %copy-start.4 = (bf16[9,32,768]{2,1,0:T(8,128)(2,1)}, bf16[9,32,768]{2,1,0:T(8,128)(2,1)S(1)}, u32[]{:S(2)}) copy-start(bf16[9,32,768]{2,1,0:T(8,128)(2,1)S(1)} %collective-permute-done.1.low) | copy-start | bytes 1327108
  67.9 8.4 %copy-start.9 = (f32[768]{0:T(1024)S(1)}, f32[768]{0:T(1024)}, u32[]{:S(2)}) copy-start(f32[768]{0:T(1024)} %param.17) | copy-start | bytes 9220
  67.9 37.4 %all-to-all-start.1 = ((bf16[4,192,1664]{2,1,0:T(8,128)(2,1)}), bf16[4,192,1664]{2,1,0:T(8,128)(2,1)S(1)}, u32[]{:S(2)}, u32[]{:S(2)}) async-start(bf16[4,192,1664]{2,1,0:T(8,128)(2,1)} %broadcast_in_dim.50), calls=%async_computation.1 | async-start | bytes 5111808 | tf_op jit(solution)/shard_map/all_to_all | solution.py:530
  76.4 9.3 %copy-start.7 = (f32[2,1024]{1,0:T(2,128)S(1)}, f32[2,1024]{1,0:T(2,128)}, u32[]{:S(2)}) copy-start(f32[2,1024]{1,0:T(2,128)} %param.23) | copy-start | bytes 24580
  76.4 9.4 %copy-start.10 = (f32[128]{0:T(128)S(1)}, f32[128]{0:T(128)}, u32[]{:S(2)}) copy-start(f32[128]{0:T(128)} %constant.45) | copy-start | bytes 1540
  76.4 9.4 %copy-start.11 = (f32[128]{0:T(128)S(1)}, f32[128]{0:T(128)}, u32[]{:S(2)}) copy-start(f32[128]{0:T(128)} %constant.44) | copy-start | bytes 1540
  76.4 9.4 %copy-start.12 = (pred[128]{0:T(512)(128)(4,1)S(1)}, pred[128]{0:T(512)(128)(4,1)}, u32[]{:S(2)}) copy-start(pred[128]{0:T(512)(128)(4,1)} %constant.43) | copy-start | bytes 388
  79.3 11.1 %collective-permute-start.4 = (bf16[288,768]{1,0:T(8,128)(2,1)}, bf16[288,768]{1,0:T(8,128)(2,1)S(1)}, u32[]{:S(2)}, u32[]{:S(2)}) collective-permute-start(bf16[288,768]{1,0:T(8,128)(2,1)} %get-tuple-element.39), channel_id=1, source_target_pairs={{0,4},{4,8},{8,12},{12,0},{1,5},{5,9},{9,13},{13,1},{2,6},{6,10},{... | collective-permute-start | bytes 1327112 | tf_op jit(solution)/shard_map/ppermute | solution.py:551
  83.7 12.0 %collective-permute-start.5 = (bf16[288,768]{1,0:T(8,128)(2,1)}, bf16[288,768]{1,0:T(8,128)(2,1)S(1)}, u32[]{:S(2)}, u32[]{:S(2)}) collective-permute-start(bf16[288,768]{1,0:T(8,128)(2,1)} %get-tuple-element.40), channel_id=1, source_target_pairs={{0,12},{4,0},{8,4},{12,8},{1,13},{5,1},{9,5},{13,9},{2,14},{6,2},{... | collective-permute-start | bytes 1327112 | tf_op jit(solution)/shard_map/ppermute | solution.py:552
  88.5 23.4 %copy-start.8 = (s32[1024]{0:T(1024)S(1)}, s32[1024]{0:T(1024)}, u32[]{:S(2)}) copy-start(s32[1024]{0:T(1024)} %param.22) | copy-start | bytes 12292
  90.4 5.3 %copy-start.13 = (bf16[288,768]{1,0:T(8,128)(2,1)}, bf16[288,768]{1,0:T(8,128)(2,1)S(1)}, u32[]{:S(2)}) copy-start(bf16[288,768]{1,0:T(8,128)(2,1)S(1)} %collective-permute-done.4.left_ref) | copy-start | bytes 1327108
  95.7 0.8 copy-start.14
  105.4 9.7 %copy-start = (bf16[4,192,1664]{2,1,0:T(8,128)(2,1)}, bf16[4,192,1664]{2,1,0:T(8,128)(2,1)S(1)}, u32[]{:S(2)}) copy-start(bf16[4,192,1664]{2,1,0:T(8,128)(2,1)S(1)} %all-to-all-done.1) | copy-start | bytes 7667716
  105.4 9.7 %collective-permute-start.6 = (bf16[768,1664]{1,0:T(8,128)(2,1)S(1)}, bf16[768,1664]{1,0:T(8,128)(2,1)}, u32[]{:S(2)}, u32[]{:S(2)}) collective-permute-start(bf16[768,1664]{1,0:T(8,128)(2,1)S(1)} %bitcast.14), channel_id=1, source_target_pairs={{0,4},{4,0},{8,12},{12,8},{1,5},{5,1},{9,13},{13,9},{2,6},{6,2},{1... | collective-permute-start | bytes 7667720 | tf_op jit(solution)/shard_map/ppermute | solution.py:556

commit v4 on v3

--- a/solution.py
+++ b/solution.py
@@ -35,6 +35,7 @@
 KEYS = 384
 HALF = 1664
 TAIL = 3 * WIDTH
+PARTS = ((0, 0, 768), (0, 768, 768), (0, 1536, 128), (1, 0, 640), (1, 640, 1024))
 BLOCK = 128
 SWAP = [(0, 1), (1, 0), (2, 3), (3, 2)]
 NEG = -1e30
@@ -223,17 +224,24 @@
     lat_end,
     end_low,
     probe_query,
-    half_sems,
+    part_sems,
     sems,
 ):
     core = place_ref[0]
     live = place_ref[1]
 
-    def half(ref, slot):
-        start = pl.multiple_of(slot * HALF, 128)
+    def part(ref, n):
+        slot, start, width = PARTS[n]
+        first = slot * HALF + start
         return pltpu.make_async_copy(
-            ref, weights.at[:, pl.ds(start, HALF)], half_sems.at[slot]
-        )
+            ref.at[:, start : start + width],
+            weights.at[:, first : first + width],
+            part_sems.at[n],
+        )
+
+    def start_parts(low, high):
+        for n, (slot, _, _) in enumerate(PARTS):
+            part((low, high)[slot], n).start()
 
     pairs = (
         (nk_any, nk_ref),
@@ -247,8 +255,8 @@
     )
     loads = [pltpu.make_async_copy(a, b, sems.at[n]) for n, (a, b) in enumerate(pairs)]
     loads[0].start()
-    half(mine, core).start()
-    half(other, 1 - core).start()
+    pl.when(core == 0)(lambda: start_parts(mine, other))
+    pl.when(core != 0)(lambda: start_parts(other, mine))
     for load in loads[1:]:
         load.start()
 
@@ -261,11 +269,13 @@
     )
     mask = jnp.where(inside, 0.0, NEG).astype(F32)
     loads[0].wait()
-    half(mine, 0).wait()
+    part(mine, 0).wait()
     project(nk_ref, weights, 0, keys, N_KEY0)
+    part(mine, 1).wait()
     project(nk_ref, weights, WIDTH, values, N_KEY0)
     loads[1].wait()
-    half(mine, 1).wait()
+    part(mine, 2).wait()
+    part(mine, 3).wait()
     project(nq_ref, weights, 2 * WIDTH, q_low, N_MID, SCALE)
 
     def attend0(j, carry):
@@ -284,6 +294,7 @@
     lax.fori_loop(0, MID_ROWS // 2, attend0, 0)
     for load in loads[2:]:
         load.wait()
+    part(mine, 4).wait()
     att_perm[...] = jnp.dot(att[...], perm_ref[...], preferred_element_type=F32).astype(BF)
     for t in range(3):
         cols = slice(256 * t, 256 * t + 256)
@@ -394,7 +405,9 @@
         probe_ref[:, pl.ds(at, BLOCK)] = jnp.where(slot < live, decoded, 0.0)[0:CH]
         return carry
 
-    lax.fori_loop(0, feat_ref.shape[0] // BLOCK, decode, 0)
+    probe_ref[...] = jnp.zeros(probe_ref.shape, F32)
+    blocks = lax.div(jnp.clip(live, 0, feat_ref.shape[0]) + BLOCK - 1, BLOCK)
+    lax.fori_loop(0, blocks, decode, 0)
 
 
 def run_pack(rows):
@@ -463,7 +476,7 @@
             pltpu.VMEM((256, WIDTH), F32),
             pltpu.VMEM((256, WIDTH), BF),
             pltpu.VMEM((probes, WIDTH), BF),
-            pltpu.SemaphoreType.DMA((2,)),
+            pltpu.SemaphoreType.DMA((len(PARTS),)),
             pltpu.SemaphoreType.DMA((len(arrays),)),
         ],
         compiler_params=pltpu.CompilerParams(vmem_limit_bytes=60 * 1024 * 1024),

time: 150 us -> 146 us (0.973)
  Pallas kernels: 42.8 us -> 38.8 us
    pallas_call x1, Pallas kernels: 34.3 us -> 30.3 us  [run_main(): pl.pallas_call(main_kernel, out_shape=(jax.ShapeDtypeStruct((ROWS * COLS,...]
where the time goes in v4:
time: 146 us; the launch traced here: 145 us
  starting transfers between devices  54.9 us (38%)
  Pallas kernels  38.8 us (27%)
  waiting for transfers between devices  36.8 us (25%)
  local copies, waits for them, and re-layouts  8.35 us (6%)
  other arithmetic  4.95 us (3%)
  between operations  1.68 us (1%)
    pallas_call x1, Pallas kernels, run_main(): pl.pallas_call(main_kernel, out_shape=(jax.ShapeDtypeStruct((ROWS * COLS,...  30.3 us
    all_to_all x1, starting transfers between devices, gather_long(): return lax.all_to_all(shares, 'gx', 0, 0).reshape(192, HALF)  16.5 us
    ppermute x1, waiting for transfers between devices, halo_rows(): lax.ppermute(latents[:RAD], axes, ring(size, -2))  16.3 us
    ppermute x1, starting transfers between devices, halo_rows(): lax.ppermute(base[:-1], axes, ring(size, -1))  9.63 us
    all_to_all x1, starting transfers between devices, gather_short(): lax.all_to_all(jnp.broadcast_to(block[None], (count,) + block.shape), 'pa...  8.41 us
    pallas_call x1, Pallas kernels, run_prep(): pl.pallas_call(prep_kernel, out_shape=(jax.ShapeDtypeStruct((N_KEY0, WIDT...  6.15 us
    ppermute x1, waiting for transfers between devices, local(): right = lax.ppermute(to_low, 'gy', ring(cols, -1))  5.34 us
    ppermute x1, starting transfers between devices, local(): other = lax.ppermute(wide, 'gy', SWAP)  5.27 us
  transfers between devices with their start and end apart: 9, of which 7 were waited for; matrix products, arithmetic and copies ran while one was open for 4% of the time, Pallas kernels for 6%

profile of v4, /device:TPU:1, one launch (start us, length us, event | category | flops | bytes accessed | tf_op | source)
XLA Modules:
  0.0 145.5 jit_solution(14885327980379861826)
XLA Ops:
  0.7 0.8 copy.20
  1.5 0.7 slice_dynamic-update-slice_fusion
  2.2 0.7 slice_dynamic-update-slice_fusion.1
  2.9 0.7 reduce
  3.6 0.7 constant_dynamic-update-slice_fusion.2
  4.4 1.0 broadcast_in_dim.49
  5.4 16.5 %all-to-all-start = ((bf16[32,6,1664]{2,1,0:T(8,128)(2,1)}), bf16[32,6,1664]{2,1,0:T(8,128)(2,1)S(1)}, u32[]{:S(2)}, u32[]{:S(2)}) async-start(bf16[32,6,1664]{2,1,0:T(8,128)(2,1)} %broadcast_in_dim.49), calls=%async_computation | async-start | bytes 1703936 | tf_op jit(solution)/shard_map/all_to_all | solution.py:538
  21.9 0.9 pad_maximum_fusion.1
  22.8 9.6 %collective-permute-start.2 = (bf16[9,32,768]{2,1,0:T(8,128)(2,1)}, bf16[9,32,768]{2,1,0:T(8,128)(2,1)S(1)}, u32[]{:S(2)}, u32[]{:S(2)}) collective-permute-start(bf16[9,32,768]{2,1,0:T(8,128)(2,1)} %get-tuple-element.56), channel_id=1, source_target_pairs={{0,499},{1,0},{2,1},{3,2},{16,3},{17,16},{18,17},{19,18},{32,19},{... | collective-permute-start | bytes 1327112 | tf_op jit(solution)/shard_map/ppermute | solution.py:517
  32.4 1.9 %collective-permute-start.1 = (bf16[9,32,768]{2,1,0:T(8,128)(2,1)S(1)}, bf16[9,32,768]{2,1,0:T(8,128)(2,1)S(1)}, u32[]{:S(2)}, u32[]{:S(2)}) collective-permute-start(bf16[9,32,768]{2,1,0:T(8,128)(2,1)S(1)} %get-tuple-element.57), channel_id=1, source_target_pairs={{0,1},{1,2},{2,3},{3,16},{16,17},{17,18},{18,19},{19,32},{32,33},{... | collective-permute-start | bytes 1327112 | tf_op jit(solution)/shard_map/ppermute | solution.py:514
  34.4 3.6 %collective-permute-start.3 = (bf16[3,32,768]{2,1,0:T(8,128)(2,1)S(1)}, bf16[3,32,768]{2,1,0:T(8,128)(2,1)S(1)}, u32[]{:S(2)}, u32[]{:S(2)}) collective-permute-start(bf16[3,32,768]{2,1,0:T(8,128)(2,1)S(1)} %get-tuple-element.60), channel_id=1, source_target_pairs={{0,498},{1,499},{2,0},{3,1},{16,2},{17,3},{18,16},{19,17},{32,18},... | collective-permute-start | bytes 442376 | tf_op jit(solution)/shard_map/ppermute | solution.py:518
  38.0 3.2 %collective-permute-start = (bf16[3,32,768]{2,1,0:T(8,128)(2,1)S(1)}, bf16[3,32,768]{2,1,0:T(8,128)(2,1)S(1)}, u32[]{:S(2)}, u32[]{:S(2)}) collective-permute-start(bf16[3,32,768]{2,1,0:T(8,128)(2,1)S(1)} %get-tuple-element.61), channel_id=1, source_target_pairs={{0,2},{1,3},{2,16},{3,17},{16,18},{17,19},{18,32},{19,33},{32,34},... | collective-permute-start | bytes 442376 | tf_op jit(solution)/shard_map/ppermute | solution.py:513
  41.2 3.6 %all-to-all-done = bf16[32,6,1664]{2,1,0:T(8,128)(2,1)S(1)} async-done(((bf16[32,6,1664]{2,1,0:T(8,128)(2,1)}), bf16[32,6,1664]{2,1,0:T(8,128)(2,1)S(1)}, u32[]{:S(2)}, u32[]{:S(2)}) %all-to-all-start) | async-done | bytes 639008 | tf_op jit(solution)/shard_map/all_to_all | solution.py:538
  45.0 16.3 %collective-permute-done.3.far_high = bf16[3,32,768]{2,1,0:T(8,128)(2,1)S(1)} collective-permute-done((bf16[3,32,768]{2,1,0:T(8,128)(2,1)S(1)}, bf16[3,32,768]{2,1,0:T(8,128)(2,1)S(1)}, u32[]{:S(2)}, u32[]{:S(2)}) %collective-permute-start.3) | collective-permute-done | bytes 147488 | tf_op jit(solution)/shard_map/ppermute | solution.py:518
  61.3 4.9 %collective-permute-done.1.low = bf16[9,32,768]{2,1,0:T(8,128)(2,1)S(1)} collective-permute-done((bf16[9,32,768]{2,1,0:T(8,128)(2,1)S(1)}, bf16[9,32,768]{2,1,0:T(8,128)(2,1)S(1)}, u32[]{:S(2)}, u32[]{:S(2)}) %collective-permute-start.1) | collective-permute-done | bytes 442400 | tf_op jit(solution)/shard_map/ppermute | solution.py:514
  66.3 1.7 %broadcast_in_dim.50 = bf16[4,192,1664]{2,1,0:T(8,128)(2,1)} broadcast(bf16[192,1664]{1,0:T(8,128)(2,1)S(1)} %reshape.23), dimensions={1,2} | broadcast | bytes 3194880 | tf_op jit(solution)/shard_map/broadcast_in_dim | solution.py:543
  67.9 8.4 %all-to-all-start.1 = ((bf16[4,192,1664]{2,1,0:T(8,128)(2,1)}), bf16[4,192,1664]{2,1,0:T(8,128)(2,1)S(1)}, u32[]{:S(2)}, u32[]{:S(2)}) async-start(bf16[4,192,1664]{2,1,0:T(8,128)(2,1)} %broadcast_in_dim.50), calls=%async_computation.1 | async-start | bytes 5111808 | tf_op jit(solution)/shard_map/all_to_all | solution.py:543
  76.4 0.6 broadcast_in_dim.48.gain_ref
  77.0 2.3 %pack.1 = (bf16[288,768]{1,0:T(8,128)(2,1)}, bf16[288,768]{1,0:T(8,128)(2,1)}) custom-call(bf16[3,32,768]{2,1,0:T(8,128)(2,1)} %copy-done.6, bf16[9,32,768]{2,1,0:T(8,128)(2,1)} %copy-done.4, bf16[4,32,768]{2,1,0:T(8,128)(2,1)} %own.1, bf16[2,4,32,768]{3,2,1,0:T(8,128)(2,1)} %noise.1, bf16[9,32,768]{2,1,0:T(8,128)(2,1)} %copy-done.3, ...), custom_call_target="tpu_custom_call" | custom-call | bytes 3000000 | tf_op jit(solution)/shard_map/pack/pallas_call | solution.py:415
  79.3 4.4 %collective-permute-start.4 = (bf16[288,768]{1,0:T(8,128)(2,1)}, bf16[288,768]{1,0:T(8,128)(2,1)S(1)}, u32[]{:S(2)}, u32[]{:S(2)}) collective-permute-start(bf16[288,768]{1,0:T(8,128)(2,1)} %get-tuple-element.39), channel_id=1, source_target_pairs={{0,4},{4,8},{8,12},{12,0},{1,5},{5,9},{9,13},{13,1},{2,6},{6,10},{... | collective-permute-start | bytes 1327112 | tf_op jit(solution)/shard_map/ppermute | solution.py:564
  83.7 1.9 %collective-permute-start.5 = (bf16[288,768]{1,0:T(8,128)(2,1)}, bf16[288,768]{1,0:T(8,128)(2,1)S(1)}, u32[]{:S(2)}, u32[]{:S(2)}) collective-permute-start(bf16[288,768]{1,0:T(8,128)(2,1)} %get-tuple-element.40), channel_id=1, source_target_pairs={{0,12},{4,0},{8,4},{12,8},{1,13},{5,1},{9,5},{13,9},{2,14},{6,2},{... | collective-permute-start | bytes 1327112 | tf_op jit(solution)/shard_map/ppermute | solution.py:565
  85.7 2.8 %fusion.3.feat_any = bf16[1024,128]{1,0:T(8,128)(2,1)} fusion(f32[128]{0:T(128)S(1)} %copy-done.10, f32[128]{0:T(128)S(1)} %copy-done.11, f32[1024]{0:T(1024)S(1)} %bitcast.17, f32[1024]{0:T(1024)S(1)} %bitcast.16, pred[128]{0:T(512)(128)(4,1)S(1)} %copy-done.12), kind=kLoop, calls=%fused_computation.4 | loop fusion | flops 917504 | bytes 271488 | tf_op jit(solution)/shard_map/convert_element_type | solution.py:500
  88.5 1.9 %collective-permute-done.4.left_ref = bf16[288,768]{1,0:T(8,128)(2,1)S(1)} collective-permute-done((bf16[288,768]{1,0:T(8,128)(2,1)}, bf16[288,768]{1,0:T(8,128)(2,1)S(1)}, u32[]{:S(2)}, u32[]{:S(2)}) %collective-permute-start.4) | collective-permute-done | bytes 442400 | tf_op jit(solution)/shard_map/ppermute | solution.py:564
  90.4 5.3 %collective-permute-done.5.right_ref = bf16[288,768]{1,0:T(8,128)(2,1)S(1)} collective-permute-done((bf16[288,768]{1,0:T(8,128)(2,1)}, bf16[288,768]{1,0:T(8,128)(2,1)S(1)}, u32[]{:S(2)}, u32[]{:S(2)}) %collective-permute-start.5) | collective-permute-done | bytes 442400 | tf_op jit(solution)/shard_map/ppermute | solution.py:565
  95.7 0.8 copy-done.14
  96.5 6.2 %prep.1 = (bf16[864,768]{1,0:T(8,128)(2,1)}, bf16[480,768]{1,0:T(8,128)(2,1)}, f32[480,768]{1,0:T(8,128)}, f32[240,768]{1,0:T(8,128)}) custom-call(bf16[3,32,768]{2,1,0:T(8,128)(2,1)} %copy-done.6, bf16[9,32,768]{2,1,0:T(8,128)(2,1)} %copy-done.4, bf16[4,32,768]{2,1,0:T(8,128)(2,1)} %own.1, bf16[2,4,32,768]{3,2,1,0:T(8,128)(2,1)} %noise.1, ...), custom_call_target="tpu_custom_call" | custom-call | flops 1585446912 | bytes 8000000 | tf_op jit(solution)/shard_map/prep/pallas_call | solution.py:429
  102.7 2.7 %all-to-all-done.1 = bf16[4,192,1664]{2,1,0:T(8,128)(2,1)S(1)} async-done(((bf16[4,192,1664]{2,1,0:T(8,128)(2,1)}), bf16[4,192,1664]{2,1,0:T(8,128)(2,1)S(1)}, u32[]{:S(2)}, u32[]{:S(2)}) %all-to-all-start.1) | async-done | bytes 2555936 | tf_op jit(solution)/shard_map/all_to_all | solution.py:543
  105.4 5.3 %collective-permute-start.6 = (bf16[768,1664]{1,0:T(8,128)(2,1)S(1)}, bf16[768,1664]{1,0:T(8,128)(2,1)}, u32[]{:S(2)}, u32[]{:S(2)}) collective-permute-start(bf16[768,1664]{1,0:T(8,128)(2,1)S(1)} %bitcast.14), channel_id=1, source_target_pairs={{0,4},{4,0},{8,12},{12,8},{1,5},{5,1},{9,13},{13,9},{2,6},{6,2},{1... | collective-permute-start | bytes 7667720 | tf_op jit(solution)/shard_map/ppermute | solution.py:569
  111.3 0.6 pad_add_fusion.place_ref
  111.9 1.0 copy.19.cell_any
  112.9 2.1 %collective-permute-done.6.other = bf16[768,1664]{1,0:T(8,128)(2,1)} collective-permute-done((bf16[768,1664]{1,0:T(8,128)(2,1)S(1)}, bf16[768,1664]{1,0:T(8,128)(2,1)}, u32[]{:S(2)}, u32[]{:S(2)}) %collective-permute-start.6) | collective-permute-done | bytes 2555936 | tf_op jit(solution)/shard_map/ppermute | solution.py:569
  115.0 30.3 %denoise_decode.1 = (bf16[128,768]{1,0:T(8,128)(2,1)}, f32[3,1024]{1,0:T(4,128)}) custom-call(s32[2]{0:T(128)} %pad_add_fusion.place_ref, f32[1,768]{1,0:T(1,128)} %broadcast_in_dim.48.gain_ref, bf16[864,768]{1,0:T(8,128)(2,1)} %get-tuple-element.45.nk_any, bf16[480,768]{1,0:T(8,128)(2,1)} %get-tuple-element.46.nq_any, ...), custom_call_target="tpu_custom_call" | custom-call | flops 16000000000 | bytes 16000000 | tf_op jit(solution)/shard_map/denoise_decode/pallas_call | solution.py:456
  (39 shorter events, 0.4 us)
Async XLA Ops:
  0.6 21.3 %copy-start.2 = (bf16[2,4,32,768]{3,2,1,0:T(8,128)(2,1)S(1)}, bf16[2,4,32,768]{3,2,1,0:T(8,128)(2,1)}, u32[]{:S(2)}) copy-start(bf16[2,4,32,768]{3,2,1,0:T(8,128)(2,1)} %noise.1) | copy-start | bytes 1179652
  4.4 17.6 %copy-start.1 = (bf16[4,32,768]{2,1,0:T(8,128)(2,1)S(1)}, bf16[4,32,768]{2,1,0:T(8,128)(2,1)}, u32[]{:S(2)}) copy-start(bf16[4,32,768]{2,1,0:T(8,128)(2,1)} %own.1) | copy-start | bytes 589828
  5.4 39.5 %all-to-all-start = ((bf16[32,6,1664]{2,1,0:T(8,128)(2,1)}), bf16[32,6,1664]{2,1,0:T(8,128)(2,1)S(1)}, u32[]{:S(2)}, u32[]{:S(2)}) async-start(bf16[32,6,1664]{2,1,0:T(8,128)(2,1)} %broadcast_in_dim.49), calls=%async_computation | async-start | bytes 1703936 | tf_op jit(solution)/shard_map/all_to_all | solution.py:538
  22.8 38.5 %collective-permute-start.2 = (bf16[9,32,768]{2,1,0:T(8,128)(2,1)}, bf16[9,32,768]{2,1,0:T(8,128)(2,1)S(1)}, u32[]{:S(2)}, u32[]{:S(2)}) collective-permute-start(bf16[9,32,768]{2,1,0:T(8,128)(2,1)} %get-tuple-element.56), channel_id=1, source_target_pairs={{0,499},{1,0},{2,1},{3,2},{16,3},{17,16},{18,17},{19,18},{32,19},{... | collective-permute-start | bytes 1327112 | tf_op jit(solution)/shard_map/ppermute | solution.py:517
  32.4 33.8 %collective-permute-start.1 = (bf16[9,32,768]{2,1,0:T(8,128)(2,1)S(1)}, bf16[9,32,768]{2,1,0:T(8,128)(2,1)S(1)}, u32[]{:S(2)}, u32[]{:S(2)}) collective-permute-start(bf16[9,32,768]{2,1,0:T(8,128)(2,1)S(1)} %get-tuple-element.57), channel_id=1, source_target_pairs={{0,1},{1,2},{2,3},{3,16},{16,17},{17,18},{18,19},{19,32},{32,33},{... | collective-permute-start | bytes 1327112 | tf_op jit(solution)/shard_map/ppermute | solution.py:514
  34.4 26.9 %collective-permute-start.3 = (bf16[3,32,768]{2,1,0:T(8,128)(2,1)S(1)}, bf16[3,32,768]{2,1,0:T(8,128)(2,1)S(1)}, u32[]{:S(2)}, u32[]{:S(2)}) collective-permute-start(bf16[3,32,768]{2,1,0:T(8,128)(2,1)S(1)} %get-tuple-element.60), channel_id=1, source_target_pairs={{0,498},{1,499},{2,0},{3,1},{16,2},{17,3},{18,16},{19,17},{32,18},... | collective-permute-start | bytes 442376 | tf_op jit(solution)/shard_map/ppermute | solution.py:518
  38.0 23.3 %collective-permute-start = (bf16[3,32,768]{2,1,0:T(8,128)(2,1)S(1)}, bf16[3,32,768]{2,1,0:T(8,128)(2,1)S(1)}, u32[]{:S(2)}, u32[]{:S(2)}) collective-permute-start(bf16[3,32,768]{2,1,0:T(8,128)(2,1)S(1)} %get-tuple-element.61), channel_id=1, source_target_pairs={{0,2},{1,3},{2,16},{3,17},{16,18},{17,19},{18,32},{19,33},{32,34},... | collective-permute-start | bytes 442376 | tf_op jit(solution)/shard_map/ppermute | solution.py:513
  61.3 6.6 %copy-start.5 = (bf16[3,32,768]{2,1,0:T(8,128)(2,1)}, bf16[3,32,768]{2,1,0:T(8,128)(2,1)S(1)}, u32[]{:S(2)}) copy-start(bf16[3,32,768]{2,1,0:T(8,128)(2,1)S(1)} %collective-permute-done.3.far_high) | copy-start | bytes 442372
  61.3 6.6 %copy-start.6 = (bf16[3,32,768]{2,1,0:T(8,128)(2,1)}, bf16[3,32,768]{2,1,0:T(8,128)(2,1)S(1)}, u32[]{:S(2)}) copy-start(bf16[3,32,768]{2,1,0:T(8,128)(2,1)S(1)} %collective-permute-done.far_low) | copy-start | bytes 442372
  61.3 6.6 %copy-start.3 = (bf16[9,32,768]{2,1,0:T(8,128)(2,1)}, bf16[9,32,768]{2,1,0:T(8,128)(2,1)S(1)}, u32[]{:S(2)}) copy-start(bf16[9,32,768]{2,1,0:T(8,128)(2,1)S(1)} %collective-permute-done.2.high) | copy-start | bytes 1327108
  66.3 1.7 %copy-start.4 = (bf16[9,32,768]{2,1,0:T(8,128)(2,1)}, bf16[9,32,768]{2,1,0:T(8,128)(2,1)S(1)}, u32[]{:S(2)}) copy-start(bf16[9,32,768]{2,1,0:T(8,128)(2,1)S(1)} %collective-permute-done.1.low) | copy-start | bytes 1327108
  67.9 8.4 %copy-start.9 = (f32[768]{0:T(1024)S(1)}, f32[768]{0:T(1024)}, u32[]{:S(2)}) copy-start(f32[768]{0:T(1024)} %param.17) | copy-start | bytes 9220
  67.9 37.4 %all-to-all-start.1 = ((bf16[4,192,1664]{2,1,0:T(8,128)(2,1)}), bf16[4,192,1664]{2,1,0:T(8,128)(2,1)S(1)}, u32[]{:S(2)}, u32[]{:S(2)}) async-start(bf16[4,192,1664]{2,1,0:T(8,128)(2,1)} %broadcast_in_dim.50), calls=%async_computation.1 | async-start | bytes 5111808 | tf_op jit(solution)/shard_map/all_to_all | solution.py:543
  76.4 9.3 %copy-start.7 = (f32[2,1024]{1,0:T(2,128)S(1)}, f32[2,1024]{1,0:T(2,128)}, u32[]{:S(2)}) copy-start(f32[2,1024]{1,0:T(2,128)} %param.23) | copy-start | bytes 24580
  76.4 9.4 %copy-start.10 = (f32[128]{0:T(128)S(1)}, f32[128]{0:T(128)}, u32[]{:S(2)}) copy-start(f32[128]{0:T(128)} %constant.45) | copy-start | bytes 1540
  76.4 9.4 %copy-start.11 = (f32[128]{0:T(128)S(1)}, f32[128]{0:T(128)}, u32[]{:S(2)}) copy-start(f32[128]{0:T(128)} %constant.44) | copy-start | bytes 1540
  76.4 9.4 %copy-start.12 = (pred[128]{0:T(512)(128)(4,1)S(1)}, pred[128]{0:T(512)(128)(4,1)}, u32[]{:S(2)}) copy-start(pred[128]{0:T(512)(128)(4,1)} %constant.43) | copy-start | bytes 388
  79.3 11.1 %collective-permute-start.4 = (bf16[288,768]{1,0:T(8,128)(2,1)}, bf16[288,768]{1,0:T(8,128)(2,1)S(1)}, u32[]{:S(2)}, u32[]{:S(2)}) collective-permute-start(bf16[288,768]{1,0:T(8,128)(2,1)} %get-tuple-element.39), channel_id=1, source_target_pairs={{0,4},{4,8},{8,12},{12,0},{1,5},{5,9},{9,13},{13,1},{2,6},{6,10},{... | collective-permute-start | bytes 1327112 | tf_op jit(solution)/shard_map/ppermute | solution.py:564
  83.7 12.0 %collective-permute-start.5 = (bf16[288,768]{1,0:T(8,128)(2,1)}, bf16[288,768]{1,0:T(8,128)(2,1)S(1)}, u32[]{:S(2)}, u32[]{:S(2)}) collective-permute-start(bf16[288,768]{1,0:T(8,128)(2,1)} %get-tuple-element.40), channel_id=1, source_target_pairs={{0,12},{4,0},{8,4},{12,8},{1,13},{5,1},{9,5},{13,9},{2,14},{6,2},{... | collective-permute-start | bytes 1327112 | tf_op jit(solution)/shard_map/ppermute | solution.py:565
  88.5 23.4 %copy-start.8 = (s32[1024]{0:T(1024)S(1)}, s32[1024]{0:T(1024)}, u32[]{:S(2)}) copy-start(s32[1024]{0:T(1024)} %param.22) | copy-start | bytes 12292
  90.4 5.3 %copy-start.13 = (bf16[288,768]{1,0:T(8,128)(2,1)}, bf16[288,768]{1,0:T(8,128)(2,1)S(1)}, u32[]{:S(2)}) copy-start(bf16[288,768]{1,0:T(8,128)(2,1)S(1)} %collective-permute-done.4.left_ref) | copy-start | bytes 1327108
  95.7 0.8 copy-start.14
  105.4 9.7 %copy-start = (bf16[4,192,1664]{2,1,0:T(8,128)(2,1)}, bf16[4,192,1664]{2,1,0:T(8,128)(2,1)S(1)}, u32[]{:S(2)}) copy-start(bf16[4,192,1664]{2,1,0:T(8,128)(2,1)S(1)} %all-to-all-done.1) | copy-start | bytes 7667716
  105.4 9.7 %collective-permute-start.6 = (bf16[768,1664]{1,0:T(8,128)(2,1)S(1)}, bf16[768,1664]{1,0:T(8,128)(2,1)}, u32[]{:S(2)}, u32[]{:S(2)}) collective-permute-start(bf16[768,1664]{1,0:T(8,128)(2,1)S(1)} %bitcast.14), channel_id=1, source_target_pairs={{0,4},{4,0},{8,12},{12,8},{1,5},{5,1},{9,13},{13,9},{2,6},{6,2},{1... | collective-permute-start | bytes 7667720 | tf_op jit(solution)/shard_map/ppermute | solution.py:569

commit v5 on v4

--- a/solution.py
+++ b/solution.py
@@ -36,7 +36,7 @@
 HALF = 1664
 TAIL = 3 * WIDTH
 PARTS = ((0, 0, 768), (0, 768, 768), (0, 1536, 128), (1, 0, 640), (1, 640, 1024))
-BLOCK = 128
+BLOCK = 256
 SWAP = [(0, 1), (1, 0), (2, 3), (3, 2)]
 NEG = -1e30
 SCALE = math.log2(math.e) / 8.0
@@ -291,7 +291,7 @@
             )
         return carry
 
-    lax.fori_loop(0, MID_ROWS // 2, attend0, 0)
+    lax.fori_loop(0, MID_ROWS // 2, attend0, 0, unroll=6)
     for load in loads[2:]:
         load.wait()
     part(mine, 4).wait()
@@ -334,7 +334,7 @@
             )
         return carry
 
-    lax.fori_loop(0, END_ROWS // 2, attend1, 0)
+    lax.fori_loop(0, END_ROWS // 2, attend1, 0, unroll=3)
     att_perm[0:N_END] = jnp.dot(
         att[0:N_END], perm_ref[...], preferred_element_type=F32
     ).astype(BF)

time: 146 us -> 141 us (0.966)
  Pallas kernels: 38.8 us -> 33.9 us
    pallas_call x1, Pallas kernels: 30.3 us -> 25.4 us  [run_main(): pl.pallas_call(main_kernel, out_shape=(jax.ShapeDtypeStruct((ROWS * COLS,...]
where the time goes in v5:
time: 141 us
  starting transfers between devices  54.9 us (39%)
  waiting for transfers between devices  36.8 us (26%)
  Pallas kernels  33.9 us (24%)
  local copies, waits for them, and re-layouts  8.35 us (6%)
  other arithmetic  4.95 us (4%)
  between operations  1.7 us (1%)
    pallas_call x1, Pallas kernels, run_main(): pl.pallas_call(main_kernel, out_shape=(jax.ShapeDtypeStruct((ROWS * COLS,...  25.4 us
    all_to_all x1, starting transfers between devices, gather_long(): return lax.all_to_all(shares, 'gx', 0, 0).reshape(192, HALF)  16.5 us
    ppermute x1, waiting for transfers between devices, halo_rows(): lax.ppermute(latents[:RAD], axes, ring(size, -2))  16.3 us
    ppermute x1, starting transfers between devices, halo_rows(): lax.ppermute(base[:-1], axes, ring(size, -1))  9.63 us
    all_to_all x1, starting transfers between devices, gather_short(): lax.all_to_all(jnp.broadcast_to(block[None], (count,) + block.shape), 'pa...  8.41 us
    pallas_call x1, Pallas kernels, run_prep(): pl.pallas_call(prep_kernel, out_shape=(jax.ShapeDtypeStruct((N_KEY0, WIDT...  6.15 us
    ppermute x1, waiting for transfers between devices, local(): right = lax.ppermute(to_low, 'gy', ring(cols, -1))  5.34 us
    ppermute x1, starting transfers between devices, local(): other = lax.ppermute(wide, 'gy', SWAP)  5.27 us
  transfers between devices with their start and end apart: 9, of which 7 were waited for; matrix products, arithmetic and copies ran while one was open for 4% of the time, Pallas kernels for 6%

profile of v5, /device:TPU:1, one launch (start us, length us, event | category | flops | bytes accessed | tf_op | source)
XLA Modules:
  0.0 140.6 jit_solution(16610746099742523731)
XLA Ops:
  0.7 0.8 copy.20
  1.5 0.7 slice_dynamic-update-slice_fusion
  2.2 0.7 slice_dynamic-update-slice_fusion.1
  2.9 0.7 reduce
  3.6 0.7 constant_dynamic-update-slice_fusion.2
  4.4 1.0 broadcast_in_dim.49
  5.4 16.5 %all-to-all-start = ((bf16[32,6,1664]{2,1,0:T(8,128)(2,1)}), bf16[32,6,1664]{2,1,0:T(8,128)(2,1)S(1)}, u32[]{:S(2)}, u32[]{:S(2)}) async-start(bf16[32,6,1664]{2,1,0:T(8,128)(2,1)} %broadcast_in_dim.49), calls=%async_computation | async-start | bytes 1703936 | tf_op jit(solution)/shard_map/all_to_all | solution.py:538
  21.9 0.9 pad_maximum_fusion.1
  22.8 9.6 %collective-permute-start.2 = (bf16[9,32,768]{2,1,0:T(8,128)(2,1)}, bf16[9,32,768]{2,1,0:T(8,128)(2,1)S(1)}, u32[]{:S(2)}, u32[]{:S(2)}) collective-permute-start(bf16[9,32,768]{2,1,0:T(8,128)(2,1)} %get-tuple-element.56), channel_id=1, source_target_pairs={{0,499},{1,0},{2,1},{3,2},{16,3},{17,16},{18,17},{19,18},{32,19},{... | collective-permute-start | bytes 1327112 | tf_op jit(solution)/shard_map/ppermute | solution.py:517
  32.4 1.9 %collective-permute-start.1 = (bf16[9,32,768]{2,1,0:T(8,128)(2,1)S(1)}, bf16[9,32,768]{2,1,0:T(8,128)(2,1)S(1)}, u32[]{:S(2)}, u32[]{:S(2)}) collective-permute-start(bf16[9,32,768]{2,1,0:T(8,128)(2,1)S(1)} %get-tuple-element.57), channel_id=1, source_target_pairs={{0,1},{1,2},{2,3},{3,16},{16,17},{17,18},{18,19},{19,32},{32,33},{... | collective-permute-start | bytes 1327112 | tf_op jit(solution)/shard_map/ppermute | solution.py:514
  34.4 3.6 %collective-permute-start.3 = (bf16[3,32,768]{2,1,0:T(8,128)(2,1)S(1)}, bf16[3,32,768]{2,1,0:T(8,128)(2,1)S(1)}, u32[]{:S(2)}, u32[]{:S(2)}) collective-permute-start(bf16[3,32,768]{2,1,0:T(8,128)(2,1)S(1)} %get-tuple-element.60), channel_id=1, source_target_pairs={{0,498},{1,499},{2,0},{3,1},{16,2},{17,3},{18,16},{19,17},{32,18},... | collective-permute-start | bytes 442376 | tf_op jit(solution)/shard_map/ppermute | solution.py:518
  38.0 3.2 %collective-permute-start = (bf16[3,32,768]{2,1,0:T(8,128)(2,1)S(1)}, bf16[3,32,768]{2,1,0:T(8,128)(2,1)S(1)}, u32[]{:S(2)}, u32[]{:S(2)}) collective-permute-start(bf16[3,32,768]{2,1,0:T(8,128)(2,1)S(1)} %get-tuple-element.61), channel_id=1, source_target_pairs={{0,2},{1,3},{2,16},{3,17},{16,18},{17,19},{18,32},{19,33},{32,34},... | collective-permute-start | bytes 442376 | tf_op jit(solution)/shard_map/ppermute | solution.py:513
  41.2 3.6 %all-to-all-done = bf16[32,6,1664]{2,1,0:T(8,128)(2,1)S(1)} async-done(((bf16[32,6,1664]{2,1,0:T(8,128)(2,1)}), bf16[32,6,1664]{2,1,0:T(8,128)(2,1)S(1)}, u32[]{:S(2)}, u32[]{:S(2)}) %all-to-all-start) | async-done | bytes 639008 | tf_op jit(solution)/shard_map/all_to_all | solution.py:538
  45.0 16.3 %collective-permute-done.3.far_high = bf16[3,32,768]{2,1,0:T(8,128)(2,1)S(1)} collective-permute-done((bf16[3,32,768]{2,1,0:T(8,128)(2,1)S(1)}, bf16[3,32,768]{2,1,0:T(8,128)(2,1)S(1)}, u32[]{:S(2)}, u32[]{:S(2)}) %collective-permute-start.3) | collective-permute-done | bytes 147488 | tf_op jit(solution)/shard_map/ppermute | solution.py:518
  61.3 4.9 %collective-permute-done.1.low = bf16[9,32,768]{2,1,0:T(8,128)(2,1)S(1)} collective-permute-done((bf16[9,32,768]{2,1,0:T(8,128)(2,1)S(1)}, bf16[9,32,768]{2,1,0:T(8,128)(2,1)S(1)}, u32[]{:S(2)}, u32[]{:S(2)}) %collective-permute-start.1) | collective-permute-done | bytes 442400 | tf_op jit(solution)/shard_map/ppermute | solution.py:514
  66.3 1.7 %broadcast_in_dim.50 = bf16[4,192,1664]{2,1,0:T(8,128)(2,1)} broadcast(bf16[192,1664]{1,0:T(8,128)(2,1)S(1)} %reshape.23), dimensions={1,2} | broadcast | bytes 3194880 | tf_op jit(solution)/shard_map/broadcast_in_dim | solution.py:543
  67.9 8.4 %all-to-all-start.1 = ((bf16[4,192,1664]{2,1,0:T(8,128)(2,1)}), bf16[4,192,1664]{2,1,0:T(8,128)(2,1)S(1)}, u32[]{:S(2)}, u32[]{:S(2)}) async-start(bf16[4,192,1664]{2,1,0:T(8,128)(2,1)} %broadcast_in_dim.50), calls=%async_computation.1 | async-start | bytes 5111808 | tf_op jit(solution)/shard_map/all_to_all | solution.py:543
  76.4 0.6 broadcast_in_dim.48.gain_ref
  77.0 2.3 %pack.1 = (bf16[288,768]{1,0:T(8,128)(2,1)}, bf16[288,768]{1,0:T(8,128)(2,1)}) custom-call(bf16[3,32,768]{2,1,0:T(8,128)(2,1)} %copy-done.6, bf16[9,32,768]{2,1,0:T(8,128)(2,1)} %copy-done.4, bf16[4,32,768]{2,1,0:T(8,128)(2,1)} %own.1, bf16[2,4,32,768]{3,2,1,0:T(8,128)(2,1)} %noise.1, bf16[9,32,768]{2,1,0:T(8,128)(2,1)} %copy-done.3, ...), custom_call_target="tpu_custom_call" | custom-call | bytes 3000000 | tf_op jit(solution)/shard_map/pack/pallas_call | solution.py:415
  79.3 4.4 %collective-permute-start.4 = (bf16[288,768]{1,0:T(8,128)(2,1)}, bf16[288,768]{1,0:T(8,128)(2,1)S(1)}, u32[]{:S(2)}, u32[]{:S(2)}) collective-permute-start(bf16[288,768]{1,0:T(8,128)(2,1)} %get-tuple-element.39), channel_id=1, source_target_pairs={{0,4},{4,8},{8,12},{12,0},{1,5},{5,9},{9,13},{13,1},{2,6},{6,10},{... | collective-permute-start | bytes 1327112 | tf_op jit(solution)/shard_map/ppermute | solution.py:564
  83.7 1.9 %collective-permute-start.5 = (bf16[288,768]{1,0:T(8,128)(2,1)}, bf16[288,768]{1,0:T(8,128)(2,1)S(1)}, u32[]{:S(2)}, u32[]{:S(2)}) collective-permute-start(bf16[288,768]{1,0:T(8,128)(2,1)} %get-tuple-element.40), channel_id=1, source_target_pairs={{0,12},{4,0},{8,4},{12,8},{1,13},{5,1},{9,5},{13,9},{2,14},{6,2},{... | collective-permute-start | bytes 1327112 | tf_op jit(solution)/shard_map/ppermute | solution.py:565
  85.7 2.8 %fusion.3.feat_any = bf16[1024,128]{1,0:T(8,128)(2,1)} fusion(f32[128]{0:T(128)S(1)} %copy-done.10, f32[128]{0:T(128)S(1)} %copy-done.11, f32[1024]{0:T(1024)S(1)} %bitcast.17, f32[1024]{0:T(1024)S(1)} %bitcast.16, pred[128]{0:T(512)(128)(4,1)S(1)} %copy-done.12), kind=kLoop, calls=%fused_computation.4 | loop fusion | flops 917504 | bytes 271488 | tf_op jit(solution)/shard_map/convert_element_type | solution.py:500
  88.5 1.9 %collective-permute-done.4.left_ref = bf16[288,768]{1,0:T(8,128)(2,1)S(1)} collective-permute-done((bf16[288,768]{1,0:T(8,128)(2,1)}, bf16[288,768]{1,0:T(8,128)(2,1)S(1)}, u32[]{:S(2)}, u32[]{:S(2)}) %collective-permute-start.4) | collective-permute-done | bytes 442400 | tf_op jit(solution)/shard_map/ppermute | solution.py:564
  90.4 5.3 %collective-permute-done.5.right_ref = bf16[288,768]{1,0:T(8,128)(2,1)S(1)} collective-permute-done((bf16[288,768]{1,0:T(8,128)(2,1)}, bf16[288,768]{1,0:T(8,128)(2,1)S(1)}, u32[]{:S(2)}, u32[]{:S(2)}) %collective-permute-start.5) | collective-permute-done | bytes 442400 | tf_op jit(solution)/shard_map/ppermute | solution.py:565
  95.7 0.8 copy-done.14
  96.5 6.2 %prep.1 = (bf16[864,768]{1,0:T(8,128)(2,1)}, bf16[480,768]{1,0:T(8,128)(2,1)}, f32[480,768]{1,0:T(8,128)}, f32[240,768]{1,0:T(8,128)}) custom-call(bf16[3,32,768]{2,1,0:T(8,128)(2,1)} %copy-done.6, bf16[9,32,768]{2,1,0:T(8,128)(2,1)} %copy-done.4, bf16[4,32,768]{2,1,0:T(8,128)(2,1)} %own.1, bf16[2,4,32,768]{3,2,1,0:T(8,128)(2,1)} %noise.1, ...), custom_call_target="tpu_custom_call" | custom-call | flops 1585446912 | bytes 8000000 | tf_op jit(solution)/shard_map/prep/pallas_call | solution.py:429
  102.7 2.7 %all-to-all-done.1 = bf16[4,192,1664]{2,1,0:T(8,128)(2,1)S(1)} async-done(((bf16[4,192,1664]{2,1,0:T(8,128)(2,1)}), bf16[4,192,1664]{2,1,0:T(8,128)(2,1)S(1)}, u32[]{:S(2)}, u32[]{:S(2)}) %all-to-all-start.1) | async-done | bytes 2555936 | tf_op jit(solution)/shard_map/all_to_all | solution.py:543
  105.4 5.3 %collective-permute-start.6 = (bf16[768,1664]{1,0:T(8,128)(2,1)S(1)}, bf16[768,1664]{1,0:T(8,128)(2,1)}, u32[]{:S(2)}, u32[]{:S(2)}) collective-permute-start(bf16[768,1664]{1,0:T(8,128)(2,1)S(1)} %bitcast.14), channel_id=1, source_target_pairs={{0,4},{4,0},{8,12},{12,8},{1,5},{5,1},{9,13},{13,9},{2,6},{6,2},{1... | collective-permute-start | bytes 7667720 | tf_op jit(solution)/shard_map/ppermute | solution.py:569
  111.3 0.6 pad_add_fusion.place_ref
  111.9 1.0 copy.19.cell_any
  112.9 2.1 %collective-permute-done.6.other = bf16[768,1664]{1,0:T(8,128)(2,1)} collective-permute-done((bf16[768,1664]{1,0:T(8,128)(2,1)S(1)}, bf16[768,1664]{1,0:T(8,128)(2,1)}, u32[]{:S(2)}, u32[]{:S(2)}) %collective-permute-start.6) | collective-permute-done | bytes 2555936 | tf_op jit(solution)/shard_map/ppermute | solution.py:569
  115.0 25.4 %denoise_decode.1 = (bf16[128,768]{1,0:T(8,128)(2,1)}, f32[3,1024]{1,0:T(4,128)}) custom-call(s32[2]{0:T(128)} %pad_add_fusion.place_ref, f32[1,768]{1,0:T(1,128)} %broadcast_in_dim.48.gain_ref, bf16[864,768]{1,0:T(8,128)(2,1)} %get-tuple-element.45.nk_any, bf16[480,768]{1,0:T(8,128)(2,1)} %get-tuple-element.46.nq_any, ...), custom_call_target="tpu_custom_call" | custom-call | flops 16000000000 | bytes 16000000 | tf_op jit(solution)/shard_map/denoise_decode/pallas_call | solution.py:456
  (39 shorter events, 0.4 us)
Async XLA Ops:
  0.6 21.3 %copy-start.2 = (bf16[2,4,32,768]{3,2,1,0:T(8,128)(2,1)S(1)}, bf16[2,4,32,768]{3,2,1,0:T(8,128)(2,1)}, u32[]{:S(2)}) copy-start(bf16[2,4,32,768]{3,2,1,0:T(8,128)(2,1)} %noise.1) | copy-start | bytes 1179652
  4.4 17.6 %copy-start.1 = (bf16[4,32,768]{2,1,0:T(8,128)(2,1)S(1)}, bf16[4,32,768]{2,1,0:T(8,128)(2,1)}, u32[]{:S(2)}) copy-start(bf16[4,32,768]{2,1,0:T(8,128)(2,1)} %own.1) | copy-start | bytes 589828
  5.4 39.5 %all-to-all-start = ((bf16[32,6,1664]{2,1,0:T(8,128)(2,1)}), bf16[32,6,1664]{2,1,0:T(8,128)(2,1)S(1)}, u32[]{:S(2)}, u32[]{:S(2)}) async-start(bf16[32,6,1664]{2,1,0:T(8,128)(2,1)} %broadcast_in_dim.49), calls=%async_computation | async-start | bytes 1703936 | tf_op jit(solution)/shard_map/all_to_all | solution.py:538
  22.8 38.5 %collective-permute-start.2 = (bf16[9,32,768]{2,1,0:T(8,128)(2,1)}, bf16[9,32,768]{2,1,0:T(8,128)(2,1)S(1)}, u32[]{:S(2)}, u32[]{:S(2)}) collective-permute-start(bf16[9,32,768]{2,1,0:T(8,128)(2,1)} %get-tuple-element.56), channel_id=1, source_target_pairs={{0,499},{1,0},{2,1},{3,2},{16,3},{17,16},{18,17},{19,18},{32,19},{... | collective-permute-start | bytes 1327112 | tf_op jit(solution)/shard_map/ppermute | solution.py:517
  32.4 33.8 %collective-permute-start.1 = (bf16[9,32,768]{2,1,0:T(8,128)(2,1)S(1)}, bf16[9,32,768]{2,1,0:T(8,128)(2,1)S(1)}, u32[]{:S(2)}, u32[]{:S(2)}) collective-permute-start(bf16[9,32,768]{2,1,0:T(8,128)(2,1)S(1)} %get-tuple-element.57), channel_id=1, source_target_pairs={{0,1},{1,2},{2,3},{3,16},{16,17},{17,18},{18,19},{19,32},{32,33},{... | collective-permute-start | bytes 1327112 | tf_op jit(solution)/shard_map/ppermute | solution.py:514
  34.4 26.9 %collective-permute-start.3 = (bf16[3,32,768]{2,1,0:T(8,128)(2,1)S(1)}, bf16[3,32,768]{2,1,0:T(8,128)(2,1)S(1)}, u32[]{:S(2)}, u32[]{:S(2)}) collective-permute-start(bf16[3,32,768]{2,1,0:T(8,128)(2,1)S(1)} %get-tuple-element.60), channel_id=1, source_target_pairs={{0,498},{1,499},{2,0},{3,1},{16,2},{17,3},{18,16},{19,17},{32,18},... | collective-permute-start | bytes 442376 | tf_op jit(solution)/shard_map/ppermute | solution.py:518
  38.0 23.3 %collective-permute-start = (bf16[3,32,768]{2,1,0:T(8,128)(2,1)S(1)}, bf16[3,32,768]{2,1,0:T(8,128)(2,1)S(1)}, u32[]{:S(2)}, u32[]{:S(2)}) collective-permute-start(bf16[3,32,768]{2,1,0:T(8,128)(2,1)S(1)} %get-tuple-element.61), channel_id=1, source_target_pairs={{0,2},{1,3},{2,16},{3,17},{16,18},{17,19},{18,32},{19,33},{32,34},... | collective-permute-start | bytes 442376 | tf_op jit(solution)/shard_map/ppermute | solution.py:513
  61.3 6.6 %copy-start.5 = (bf16[3,32,768]{2,1,0:T(8,128)(2,1)}, bf16[3,32,768]{2,1,0:T(8,128)(2,1)S(1)}, u32[]{:S(2)}) copy-start(bf16[3,32,768]{2,1,0:T(8,128)(2,1)S(1)} %collective-permute-done.3.far_high) | copy-start | bytes 442372
  61.3 6.6 %copy-start.6 = (bf16[3,32,768]{2,1,0:T(8,128)(2,1)}, bf16[3,32,768]{2,1,0:T(8,128)(2,1)S(1)}, u32[]{:S(2)}) copy-start(bf16[3,32,768]{2,1,0:T(8,128)(2,1)S(1)} %collective-permute-done.far_low) | copy-start | bytes 442372
  61.3 6.6 %copy-start.3 = (bf16[9,32,768]{2,1,0:T(8,128)(2,1)}, bf16[9,32,768]{2,1,0:T(8,128)(2,1)S(1)}, u32[]{:S(2)}) copy-start(bf16[9,32,768]{2,1,0:T(8,128)(2,1)S(1)} %collective-permute-done.2.high) | copy-start | bytes 1327108
  66.3 1.7 %copy-start.4 = (bf16[9,32,768]{2,1,0:T(8,128)(2,1)}, bf16[9,32,768]{2,1,0:T(8,128)(2,1)S(1)}, u32[]{:S(2)}) copy-start(bf16[9,32,768]{2,1,0:T(8,128)(2,1)S(1)} %collective-permute-done.1.low) | copy-start | bytes 1327108
  67.9 8.4 %copy-start.9 = (f32[768]{0:T(1024)S(1)}, f32[768]{0:T(1024)}, u32[]{:S(2)}) copy-start(f32[768]{0:T(1024)} %param.17) | copy-start | bytes 9220
  67.9 37.4 %all-to-all-start.1 = ((bf16[4,192,1664]{2,1,0:T(8,128)(2,1)}), bf16[4,192,1664]{2,1,0:T(8,128)(2,1)S(1)}, u32[]{:S(2)}, u32[]{:S(2)}) async-start(bf16[4,192,1664]{2,1,0:T(8,128)(2,1)} %broadcast_in_dim.50), calls=%async_computation.1 | async-start | bytes 5111808 | tf_op jit(solution)/shard_map/all_to_all | solution.py:543
  76.4 9.3 %copy-start.7 = (f32[2,1024]{1,0:T(2,128)S(1)}, f32[2,1024]{1,0:T(2,128)}, u32[]{:S(2)}) copy-start(f32[2,1024]{1,0:T(2,128)} %param.23) | copy-start | bytes 24580
  76.4 9.4 %copy-start.10 = (f32[128]{0:T(128)S(1)}, f32[128]{0:T(128)}, u32[]{:S(2)}) copy-start(f32[128]{0:T(128)} %constant.45) | copy-start | bytes 1540
  76.4 9.4 %copy-start.11 = (f32[128]{0:T(128)S(1)}, f32[128]{0:T(128)}, u32[]{:S(2)}) copy-start(f32[128]{0:T(128)} %constant.44) | copy-start | bytes 1540
  76.4 9.4 %copy-start.12 = (pred[128]{0:T(512)(128)(4,1)S(1)}, pred[128]{0:T(512)(128)(4,1)}, u32[]{:S(2)}) copy-start(pred[128]{0:T(512)(128)(4,1)} %constant.43) | copy-start | bytes 388
  79.3 11.1 %collective-permute-start.4 = (bf16[288,768]{1,0:T(8,128)(2,1)}, bf16[288,768]{1,0:T(8,128)(2,1)S(1)}, u32[]{:S(2)}, u32[]{:S(2)}) collective-permute-start(bf16[288,768]{1,0:T(8,128)(2,1)} %get-tuple-element.39), channel_id=1, source_target_pairs={{0,4},{4,8},{8,12},{12,0},{1,5},{5,9},{9,13},{13,1},{2,6},{6,10},{... | collective-permute-start | bytes 1327112 | tf_op jit(solution)/shard_map/ppermute | solution.py:564
  83.7 12.0 %collective-permute-start.5 = (bf16[288,768]{1,0:T(8,128)(2,1)}, bf16[288,768]{1,0:T(8,128)(2,1)S(1)}, u32[]{:S(2)}, u32[]{:S(2)}) collective-permute-start(bf16[288,768]{1,0:T(8,128)(2,1)} %get-tuple-element.40), channel_id=1, source_target_pairs={{0,12},{4,0},{8,4},{12,8},{1,13},{5,1},{9,5},{13,9},{2,14},{6,2},{... | collective-permute-start | bytes 1327112 | tf_op jit(solution)/shard_map/ppermute | solution.py:565
  88.5 23.4 %copy-start.8 = (s32[1024]{0:T(1024)S(1)}, s32[1024]{0:T(1024)}, u32[]{:S(2)}) copy-start(s32[1024]{0:T(1024)} %param.22) | copy-start | bytes 12292
  90.4 5.3 %copy-start.13 = (bf16[288,768]{1,0:T(8,128)(2,1)}, bf16[288,768]{1,0:T(8,128)(2,1)S(1)}, u32[]{:S(2)}) copy-start(bf16[288,768]{1,0:T(8,128)(2,1)S(1)} %collective-permute-done.4.left_ref) | copy-start | bytes 1327108
  95.7 0.8 copy-start.14
  105.4 9.7 %copy-start = (bf16[4,192,1664]{2,1,0:T(8,128)(2,1)}, bf16[4,192,1664]{2,1,0:T(8,128)(2,1)S(1)}, u32[]{:S(2)}) copy-start(bf16[4,192,1664]{2,1,0:T(8,128)(2,1)S(1)} %all-to-all-done.1) | copy-start | bytes 7667716
  105.4 9.7 %collective-permute-start.6 = (bf16[768,1664]{1,0:T(8,128)(2,1)S(1)}, bf16[768,1664]{1,0:T(8,128)(2,1)}, u32[]{:S(2)}, u32[]{:S(2)}) collective-permute-start(bf16[768,1664]{1,0:T(8,128)(2,1)S(1)} %bitcast.14), channel_id=1, source_target_pairs={{0,4},{4,0},{8,12},{12,8},{1,5},{5,1},{9,13},{13,9},{2,6},{6,2},{1... | collective-permute-start | bytes 7667720 | tf_op jit(solution)/shard_map/ppermute | solution.py:569

commit v6 on v5

--- a/solution.py
+++ b/solution.py
@@ -558,7 +558,8 @@
     shares = pack_weights(w_qkv, w_out, w_query, w_head, core)
     shares, latents, noise = barrier((shares, latents, noise))
     rows = halo_rows(latents, noise)
-    block, rows = barrier((gather_long(shares), rows))
+    rows = list(rows)
+    block, rows[1], rows[4] = barrier((gather_long(shares), rows[1], rows[4]))
     wide = gather_short(block)
     to_high, to_low = run_pack(rows)
     left = lax.ppermute(to_high, "gy", ring(cols, 1))

time: 141 us -> 166 us (1.18); the launches traced: 141 us -> 164 us
  waiting for transfers between devices: 36.8 us -> 69.1 us
  starting transfers between devices: 54.9 us -> 47.8 us
  Pallas kernels: 33.9 us -> 30.6 us
    ppermute x1, waiting for transfers between devices: 16.3 us -> 28 us  [halo_rows(): lax.ppermute(latents[:RAD], axes, ring(size, -2))]
    ppermute x1, waiting for transfers between devices: 0.01 us -> 10.1 us  [halo_rows(): lax.ppermute(base[:-1], axes, ring(size, -1))]
    all_to_all x1, waiting for transfers between devices: 3.62 us -> 10.5 us  [gather_long(): return lax.all_to_all(shares, 'gx', 0, 0).reshape(192, HALF)]
    ppermute x1, waiting for transfers between devices: 4.93 us -> 11.1 us  [halo_rows(): lax.ppermute(base[1:], axes, ring(size, 1))]
    all_to_all x1, starting transfers between devices: 8.41 us -> 3.78 us  [gather_short(): lax.all_to_all(jnp.broadcast_to(block[None], (count,) + block.shape), 'pa...]
    pallas_call x1, Pallas kernels: 25.4 us -> 22.1 us  [run_main(): pl.pallas_call(main_kernel, out_shape=(jax.ShapeDtypeStruct((ROWS * COLS,...]
    ppermute x1, starting transfers between devices: 5.27 us -> 2.1 us  [local(): other = lax.ppermute(wide, 'gy', SWAP)]
    all_to_all x1, waiting for transfers between devices: 2.69 us -> 0.01 us  [gather_short(): lax.all_to_all(jnp.broadcast_to(block[None], (count,) + block.shape), 'pa...]
  transfers between devices with their start and end apart: 9 -> 9, of which waited for: 7 -> 7; matrix products, arithmetic and copies ran while one was open for 4% -> 4% of each run, Pallas kernels for 6% -> 5%
where the time goes in v6:
time: 166 us; the launch traced here: 164 us
  waiting for transfers between devices  69.1 us (42%)
  starting transfers between devices  47.8 us (29%)
  Pallas kernels  30.6 us (18%)
  local copies, waits for them, and re-layouts  9.66 us (6%)
  other arithmetic  4.95 us (3%)
  between operations  1.71 us (1%)
    ppermute x1, waiting for transfers between devices, halo_rows(): lax.ppermute(latents[:RAD], axes, ring(size, -2))  28 us
    pallas_call x1, Pallas kernels, run_main(): pl.pallas_call(main_kernel, out_shape=(jax.ShapeDtypeStruct((ROWS * COLS,...  22.1 us
    all_to_all x1, starting transfers between devices, gather_long(): return lax.all_to_all(shares, 'gx', 0, 0).reshape(192, HALF)  16.5 us
    ppermute x1, waiting for transfers between devices, halo_rows(): lax.ppermute(base[1:], axes, ring(size, 1))  11.1 us
    all_to_all x1, waiting for transfers between devices, gather_long(): return lax.all_to_all(shares, 'gx', 0, 0).reshape(192, HALF)  10.5 us
    ppermute x1, waiting for transfers between devices, halo_rows(): lax.ppermute(base[:-1], axes, ring(size, -1))  10.1 us
    ppermute x1, starting transfers between devices, halo_rows(): lax.ppermute(base[:-1], axes, ring(size, -1))  9.63 us
    pallas_call x1, Pallas kernels, run_prep(): pl.pallas_call(prep_kernel, out_shape=(jax.ShapeDtypeStruct((N_KEY0, WIDT...  6.15 us
  transfers between devices with their start and end apart: 9, of which 7 were waited for; matrix products, arithmetic and copies ran while one was open for 4% of the time, Pallas kernels for 5%

profile of v6, /device:TPU:1, one launch (start us, length us, event | category | flops | bytes accessed | tf_op | source)
XLA Modules:
  0.0 163.8 jit_solution(609141004479263946)
XLA Ops:
  0.7 0.8 copy.20
  1.5 0.7 slice_dynamic-update-slice_fusion
  2.2 0.7 slice_dynamic-update-slice_fusion.1
  2.9 0.7 reduce
  3.6 0.7 constant_dynamic-update-slice_fusion.2
  4.4 1.0 broadcast_in_dim.49
  5.4 16.5 %all-to-all-start = ((bf16[32,6,1664]{2,1,0:T(8,128)(2,1)}), bf16[32,6,1664]{2,1,0:T(8,128)(2,1)S(1)}, u32[]{:S(2)}, u32[]{:S(2)}) async-start(bf16[32,6,1664]{2,1,0:T(8,128)(2,1)} %broadcast_in_dim.49), calls=%async_computation | async-start | bytes 1703936 | tf_op jit(solution)/shard_map/all_to_all | solution.py:538
  21.9 0.9 pad_maximum_fusion.1
  22.8 9.6 %collective-permute-start.1 = (bf16[9,32,768]{2,1,0:T(8,128)(2,1)}, bf16[9,32,768]{2,1,0:T(8,128)(2,1)S(1)}, u32[]{:S(2)}, u32[]{:S(2)}) collective-permute-start(bf16[9,32,768]{2,1,0:T(8,128)(2,1)} %get-tuple-element.48), channel_id=1, source_target_pairs={{0,499},{1,0},{2,1},{3,2},{16,3},{17,16},{18,17},{19,18},{32,19},{... | collective-permute-start | bytes 1327112 | tf_op jit(solution)/shard_map/ppermute | solution.py:517
  32.4 1.9 %collective-permute-start = (bf16[9,32,768]{2,1,0:T(8,128)(2,1)S(1)}, bf16[9,32,768]{2,1,0:T(8,128)(2,1)S(1)}, u32[]{:S(2)}, u32[]{:S(2)}) collective-permute-start(bf16[9,32,768]{2,1,0:T(8,128)(2,1)S(1)} %get-tuple-element.49), channel_id=1, source_target_pairs={{0,1},{1,2},{2,3},{3,16},{16,17},{17,18},{18,19},{19,32},{32,33},{... | collective-permute-start | bytes 1327112 | tf_op jit(solution)/shard_map/ppermute | solution.py:514
  34.4 10.5 %all-to-all-done = bf16[32,6,1664]{2,1,0:T(8,128)(2,1)S(1)} async-done(((bf16[32,6,1664]{2,1,0:T(8,128)(2,1)}), bf16[32,6,1664]{2,1,0:T(8,128)(2,1)S(1)}, u32[]{:S(2)}, u32[]{:S(2)}) %all-to-all-start) | async-done | bytes 639008 | tf_op jit(solution)/shard_map/all_to_all | solution.py:538
  45.0 10.1 %collective-permute-done.1.high = bf16[9,32,768]{2,1,0:T(8,128)(2,1)S(1)} collective-permute-done((bf16[9,32,768]{2,1,0:T(8,128)(2,1)}, bf16[9,32,768]{2,1,0:T(8,128)(2,1)S(1)}, u32[]{:S(2)}, u32[]{:S(2)}) %collective-permute-start.1) | collective-permute-done | bytes 442400 | tf_op jit(solution)/shard_map/ppermute | solution.py:517
  55.2 11.1 %collective-permute-done.low = bf16[9,32,768]{2,1,0:T(8,128)(2,1)S(1)} collective-permute-done((bf16[9,32,768]{2,1,0:T(8,128)(2,1)S(1)}, bf16[9,32,768]{2,1,0:T(8,128)(2,1)S(1)}, u32[]{:S(2)}, u32[]{:S(2)}) %collective-permute-start) | collective-permute-done | bytes 442400 | tf_op jit(solution)/shard_map/ppermute | solution.py:514
  66.3 1.7 %broadcast_in_dim.50 = bf16[4,192,1664]{2,1,0:T(8,128)(2,1)} broadcast(bf16[192,1664]{1,0:T(8,128)(2,1)S(1)} %reshape.23), dimensions={1,2} | broadcast | bytes 3194880 | tf_op jit(solution)/shard_map/broadcast_in_dim | solution.py:543
  67.9 3.8 %all-to-all-start.1 = ((bf16[4,192,1664]{2,1,0:T(8,128)(2,1)}), bf16[4,192,1664]{2,1,0:T(8,128)(2,1)S(1)}, u32[]{:S(2)}, u32[]{:S(2)}) async-start(bf16[4,192,1664]{2,1,0:T(8,128)(2,1)} %broadcast_in_dim.50), calls=%async_computation.1 | async-start | bytes 5111808 | tf_op jit(solution)/shard_map/all_to_all | solution.py:543
  71.8 3.2 %collective-permute-start.3 = (bf16[3,32,768]{2,1,0:T(8,128)(2,1)S(1)}, bf16[3,32,768]{2,1,0:T(8,128)(2,1)S(1)}, u32[]{:S(2)}, u32[]{:S(2)}) collective-permute-start(bf16[3,32,768]{2,1,0:T(8,128)(2,1)S(1)} %get-tuple-element.52), channel_id=1, source_target_pairs={{0,498},{1,499},{2,0},{3,1},{16,2},{17,3},{18,16},{19,17},{32,18},... | collective-permute-start | bytes 442376 | tf_op jit(solution)/shard_map/ppermute | solution.py:518
  75.0 3.6 %collective-permute-start.2 = (bf16[3,32,768]{2,1,0:T(8,128)(2,1)S(1)}, bf16[3,32,768]{2,1,0:T(8,128)(2,1)S(1)}, u32[]{:S(2)}, u32[]{:S(2)}) collective-permute-start(bf16[3,32,768]{2,1,0:T(8,128)(2,1)S(1)} %get-tuple-element.53), channel_id=1, source_target_pairs={{0,2},{1,3},{2,16},{3,17},{16,18},{17,19},{18,32},{19,33},{32,34},... | collective-permute-start | bytes 442376 | tf_op jit(solution)/shard_map/ppermute | solution.py:513
  79.2 28.0 %collective-permute-done.3.far_high = bf16[3,32,768]{2,1,0:T(8,128)(2,1)S(1)} collective-permute-done((bf16[3,32,768]{2,1,0:T(8,128)(2,1)S(1)}, bf16[3,32,768]{2,1,0:T(8,128)(2,1)S(1)}, u32[]{:S(2)}, u32[]{:S(2)}) %collective-permute-start.3) | collective-permute-done | bytes 147488 | tf_op jit(solution)/shard_map/ppermute | solution.py:518
  107.2 0.6 copy-done.5
  107.9 0.7 copy-done.6
  108.5 2.3 %pack.1 = (bf16[288,768]{1,0:T(8,128)(2,1)}, bf16[288,768]{1,0:T(8,128)(2,1)}) custom-call(bf16[3,32,768]{2,1,0:T(8,128)(2,1)} %copy-done.6, bf16[9,32,768]{2,1,0:T(8,128)(2,1)} %copy-done.4, bf16[4,32,768]{2,1,0:T(8,128)(2,1)} %own.1, bf16[2,4,32,768]{3,2,1,0:T(8,128)(2,1)} %noise.1, bf16[9,32,768]{2,1,0:T(8,128)(2,1)} %copy-done.3, ...), custom_call_target="tpu_custom_call" | custom-call | bytes 3000000 | tf_op jit(solution)/shard_map/pack/pallas_call | solution.py:415
  110.9 5.0 %collective-permute-start.4 = (bf16[288,768]{1,0:T(8,128)(2,1)}, bf16[288,768]{1,0:T(8,128)(2,1)S(1)}, u32[]{:S(2)}, u32[]{:S(2)}) collective-permute-start(bf16[288,768]{1,0:T(8,128)(2,1)} %get-tuple-element.31), channel_id=1, source_target_pairs={{0,4},{4,8},{8,12},{12,0},{1,5},{5,9},{9,13},{13,1},{2,6},{6,10},{... | collective-permute-start | bytes 1327112 | tf_op jit(solution)/shard_map/ppermute | solution.py:565
  115.9 1.9 %collective-permute-start.5 = (bf16[288,768]{1,0:T(8,128)(2,1)}, bf16[288,768]{1,0:T(8,128)(2,1)S(1)}, u32[]{:S(2)}, u32[]{:S(2)}) collective-permute-start(bf16[288,768]{1,0:T(8,128)(2,1)} %get-tuple-element.32), channel_id=1, source_target_pairs={{0,12},{4,0},{8,4},{12,8},{1,13},{5,1},{9,5},{13,9},{2,14},{6,2},{... | collective-permute-start | bytes 1327112 | tf_op jit(solution)/shard_map/ppermute | solution.py:566
  117.9 2.8 %fusion.3.feat_any = bf16[1024,128]{1,0:T(8,128)(2,1)} fusion(f32[128]{0:T(128)S(1)} %copy-done.10, f32[128]{0:T(128)S(1)} %copy-done.11, f32[1024]{0:T(1024)S(1)} %bitcast.17, f32[1024]{0:T(1024)S(1)} %bitcast.16, pred[128]{0:T(512)(128)(4,1)S(1)} %copy-done.12), kind=kLoop, calls=%fused_computation.4 | loop fusion | flops 917504 | bytes 271488 | tf_op jit(solution)/shard_map/convert_element_type | solution.py:500
  120.7 1.8 %collective-permute-done.4.left_ref = bf16[288,768]{1,0:T(8,128)(2,1)S(1)} collective-permute-done((bf16[288,768]{1,0:T(8,128)(2,1)}, bf16[288,768]{1,0:T(8,128)(2,1)S(1)}, u32[]{:S(2)}, u32[]{:S(2)}) %collective-permute-start.4) | collective-permute-done | bytes 442400 | tf_op jit(solution)/shard_map/ppermute | solution.py:565
  122.4 5.3 %collective-permute-done.5.right_ref = bf16[288,768]{1,0:T(8,128)(2,1)S(1)} collective-permute-done((bf16[288,768]{1,0:T(8,128)(2,1)}, bf16[288,768]{1,0:T(8,128)(2,1)S(1)}, u32[]{:S(2)}, u32[]{:S(2)}) %collective-permute-start.5) | collective-permute-done | bytes 442400 | tf_op jit(solution)/shard_map/ppermute | solution.py:566
  127.7 0.8 copy-done.14
  128.5 6.2 %prep.1 = (bf16[864,768]{1,0:T(8,128)(2,1)}, bf16[480,768]{1,0:T(8,128)(2,1)}, f32[480,768]{1,0:T(8,128)}, f32[240,768]{1,0:T(8,128)}) custom-call(bf16[3,32,768]{2,1,0:T(8,128)(2,1)} %copy-done.6, bf16[9,32,768]{2,1,0:T(8,128)(2,1)} %copy-done.4, bf16[4,32,768]{2,1,0:T(8,128)(2,1)} %own.1, bf16[2,4,32,768]{3,2,1,0:T(8,128)(2,1)} %noise.1, ...), custom_call_target="tpu_custom_call" | custom-call | flops 1585446912 | bytes 8000000 | tf_op jit(solution)/shard_map/prep/pallas_call | solution.py:429
  134.7 2.1 %collective-permute-start.6 = (bf16[768,1664]{1,0:T(8,128)(2,1)S(1)}, bf16[768,1664]{1,0:T(8,128)(2,1)}, u32[]{:S(2)}, u32[]{:S(2)}) collective-permute-start(bf16[768,1664]{1,0:T(8,128)(2,1)S(1)} %bitcast.14), channel_id=1, source_target_pairs={{0,4},{4,0},{8,12},{12,8},{1,5},{5,1},{9,13},{13,9},{2,6},{6,2},{1... | collective-permute-start | bytes 7667720 | tf_op jit(solution)/shard_map/ppermute | solution.py:570
  138.0 1.0 copy.19.cell_any
  139.1 2.4 %collective-permute-done.6.other = bf16[768,1664]{1,0:T(8,128)(2,1)} collective-permute-done((bf16[768,1664]{1,0:T(8,128)(2,1)S(1)}, bf16[768,1664]{1,0:T(8,128)(2,1)}, u32[]{:S(2)}, u32[]{:S(2)}) %collective-permute-start.6) | collective-permute-done | bytes 2555936 | tf_op jit(solution)/shard_map/ppermute | solution.py:570
  141.5 22.1 %denoise_decode.1 = (bf16[128,768]{1,0:T(8,128)(2,1)}, f32[3,1024]{1,0:T(4,128)}) custom-call(s32[2]{0:T(128)} %pad_add_fusion.place_ref, f32[1,768]{1,0:T(1,128)} %broadcast_in_dim.48.gain_ref, bf16[864,768]{1,0:T(8,128)(2,1)} %get-tuple-element.37.nk_any, bf16[480,768]{1,0:T(8,128)(2,1)} %get-tuple-element.38.nq_any, ...), custom_call_target="tpu_custom_call" | custom-call | flops 16000000000 | bytes 16000000 | tf_op jit(solution)/shard_map/denoise_decode/pallas_call | solution.py:456
  (39 shorter events, 1.5 us)
Async XLA Ops:
  0.6 21.3 %copy-start.2 = (bf16[2,4,32,768]{3,2,1,0:T(8,128)(2,1)S(1)}, bf16[2,4,32,768]{3,2,1,0:T(8,128)(2,1)}, u32[]{:S(2)}) copy-start(bf16[2,4,32,768]{3,2,1,0:T(8,128)(2,1)} %noise.1) | copy-start | bytes 1179652
  4.4 17.6 %copy-start.1 = (bf16[4,32,768]{2,1,0:T(8,128)(2,1)S(1)}, bf16[4,32,768]{2,1,0:T(8,128)(2,1)}, u32[]{:S(2)}) copy-start(bf16[4,32,768]{2,1,0:T(8,128)(2,1)} %own.1) | copy-start | bytes 589828
  5.4 39.5 %all-to-all-start = ((bf16[32,6,1664]{2,1,0:T(8,128)(2,1)}), bf16[32,6,1664]{2,1,0:T(8,128)(2,1)S(1)}, u32[]{:S(2)}, u32[]{:S(2)}) async-start(bf16[32,6,1664]{2,1,0:T(8,128)(2,1)} %broadcast_in_dim.49), calls=%async_computation | async-start | bytes 1703936 | tf_op jit(solution)/shard_map/all_to_all | solution.py:538
  22.8 32.4 %collective-permute-start.1 = (bf16[9,32,768]{2,1,0:T(8,128)(2,1)}, bf16[9,32,768]{2,1,0:T(8,128)(2,1)S(1)}, u32[]{:S(2)}, u32[]{:S(2)}) collective-permute-start(bf16[9,32,768]{2,1,0:T(8,128)(2,1)} %get-tuple-element.48), channel_id=1, source_target_pairs={{0,499},{1,0},{2,1},{3,2},{16,3},{17,16},{18,17},{19,18},{32,19},{... | collective-permute-start | bytes 1327112 | tf_op jit(solution)/shard_map/ppermute | solution.py:517
  32.4 33.8 %collective-permute-start = (bf16[9,32,768]{2,1,0:T(8,128)(2,1)S(1)}, bf16[9,32,768]{2,1,0:T(8,128)(2,1)S(1)}, u32[]{:S(2)}, u32[]{:S(2)}) collective-permute-start(bf16[9,32,768]{2,1,0:T(8,128)(2,1)S(1)} %get-tuple-element.49), channel_id=1, source_target_pairs={{0,1},{1,2},{2,3},{3,16},{16,17},{17,18},{18,19},{19,32},{32,33},{... | collective-permute-start | bytes 1327112 | tf_op jit(solution)/shard_map/ppermute | solution.py:514
  55.2 12.7 %copy-start.3 = (bf16[9,32,768]{2,1,0:T(8,128)(2,1)}, bf16[9,32,768]{2,1,0:T(8,128)(2,1)S(1)}, u32[]{:S(2)}) copy-start(bf16[9,32,768]{2,1,0:T(8,128)(2,1)S(1)} %collective-permute-done.1.high) | copy-start | bytes 1327108
  66.3 1.7 %copy-start.4 = (bf16[9,32,768]{2,1,0:T(8,128)(2,1)}, bf16[9,32,768]{2,1,0:T(8,128)(2,1)S(1)}, u32[]{:S(2)}) copy-start(bf16[9,32,768]{2,1,0:T(8,128)(2,1)S(1)} %collective-permute-done.low) | copy-start | bytes 1327108
  67.9 10.7 %copy-start.9 = (f32[768]{0:T(1024)S(1)}, f32[768]{0:T(1024)}, u32[]{:S(2)}) copy-start(f32[768]{0:T(1024)} %param.17) | copy-start | bytes 9220
  67.9 66.7 %all-to-all-start.1 = ((bf16[4,192,1664]{2,1,0:T(8,128)(2,1)}), bf16[4,192,1664]{2,1,0:T(8,128)(2,1)S(1)}, u32[]{:S(2)}, u32[]{:S(2)}) async-start(bf16[4,192,1664]{2,1,0:T(8,128)(2,1)} %broadcast_in_dim.50), calls=%async_computation.1 | async-start | bytes 5111808 | tf_op jit(solution)/shard_map/all_to_all | solution.py:543
  71.7 46.1 %copy-start.7 = (f32[2,1024]{1,0:T(2,128)S(1)}, f32[2,1024]{1,0:T(2,128)}, u32[]{:S(2)}) copy-start(f32[2,1024]{1,0:T(2,128)} %param.23) | copy-start | bytes 24580
  71.7 46.2 %copy-start.10 = (f32[128]{0:T(128)S(1)}, f32[128]{0:T(128)}, u32[]{:S(2)}) copy-start(f32[128]{0:T(128)} %constant.45) | copy-start | bytes 1540
  71.7 46.1 %copy-start.11 = (f32[128]{0:T(128)S(1)}, f32[128]{0:T(128)}, u32[]{:S(2)}) copy-start(f32[128]{0:T(128)} %constant.44) | copy-start | bytes 1540
  71.7 46.1 %copy-start.12 = (pred[128]{0:T(512)(128)(4,1)S(1)}, pred[128]{0:T(512)(128)(4,1)}, u32[]{:S(2)}) copy-start(pred[128]{0:T(512)(128)(4,1)} %constant.43) | copy-start | bytes 388
  71.8 35.4 %collective-permute-start.3 = (bf16[3,32,768]{2,1,0:T(8,128)(2,1)S(1)}, bf16[3,32,768]{2,1,0:T(8,128)(2,1)S(1)}, u32[]{:S(2)}, u32[]{:S(2)}) collective-permute-start(bf16[3,32,768]{2,1,0:T(8,128)(2,1)S(1)} %get-tuple-element.52), channel_id=1, source_target_pairs={{0,498},{1,499},{2,0},{3,1},{16,2},{17,3},{18,16},{19,17},{32,18},... | collective-permute-start | bytes 442376 | tf_op jit(solution)/shard_map/ppermute | solution.py:518
  75.0 32.2 %collective-permute-start.2 = (bf16[3,32,768]{2,1,0:T(8,128)(2,1)S(1)}, bf16[3,32,768]{2,1,0:T(8,128)(2,1)S(1)}, u32[]{:S(2)}, u32[]{:S(2)}) collective-permute-start(bf16[3,32,768]{2,1,0:T(8,128)(2,1)S(1)} %get-tuple-element.53), channel_id=1, source_target_pairs={{0,2},{1,3},{2,16},{3,17},{16,18},{17,19},{18,32},{19,33},{32,34},... | collective-permute-start | bytes 442376 | tf_op jit(solution)/shard_map/ppermute | solution.py:513
  107.2 0.7 copy-start.5
  107.9 0.7 copy-start.6
  110.9 11.6 %collective-permute-start.4 = (bf16[288,768]{1,0:T(8,128)(2,1)}, bf16[288,768]{1,0:T(8,128)(2,1)S(1)}, u32[]{:S(2)}, u32[]{:S(2)}) collective-permute-start(bf16[288,768]{1,0:T(8,128)(2,1)} %get-tuple-element.31), channel_id=1, source_target_pairs={{0,4},{4,8},{8,12},{12,0},{1,5},{5,9},{9,13},{13,1},{2,6},{6,10},{... | collective-permute-start | bytes 1327112 | tf_op jit(solution)/shard_map/ppermute | solution.py:565
  115.9 11.8 %collective-permute-start.5 = (bf16[288,768]{1,0:T(8,128)(2,1)}, bf16[288,768]{1,0:T(8,128)(2,1)S(1)}, u32[]{:S(2)}, u32[]{:S(2)}) collective-permute-start(bf16[288,768]{1,0:T(8,128)(2,1)} %get-tuple-element.32), channel_id=1, source_target_pairs={{0,12},{4,0},{8,4},{12,8},{1,13},{5,1},{9,5},{13,9},{2,14},{6,2},{... | collective-permute-start | bytes 1327112 | tf_op jit(solution)/shard_map/ppermute | solution.py:566
  120.7 17.4 %copy-start.8 = (s32[1024]{0:T(1024)S(1)}, s32[1024]{0:T(1024)}, u32[]{:S(2)}) copy-start(s32[1024]{0:T(1024)} %param.22) | copy-start | bytes 12292
  122.4 5.3 %copy-start.13 = (bf16[288,768]{1,0:T(8,128)(2,1)}, bf16[288,768]{1,0:T(8,128)(2,1)S(1)}, u32[]{:S(2)}) copy-start(bf16[288,768]{1,0:T(8,128)(2,1)S(1)} %collective-permute-done.4.left_ref) | copy-start | bytes 1327108
  127.7 0.8 copy-start.14
  134.7 6.9 %copy-start = (bf16[4,192,1664]{2,1,0:T(8,128)(2,1)}, bf16[4,192,1664]{2,1,0:T(8,128)(2,1)S(1)}, u32[]{:S(2)}) copy-start(bf16[4,192,1664]{2,1,0:T(8,128)(2,1)S(1)} %all-to-all-done.1) | copy-start | bytes 7667716
  134.7 6.8 %collective-permute-start.6 = (bf16[768,1664]{1,0:T(8,128)(2,1)S(1)}, bf16[768,1664]{1,0:T(8,128)(2,1)}, u32[]{:S(2)}, u32[]{:S(2)}) collective-permute-start(bf16[768,1664]{1,0:T(8,128)(2,1)S(1)} %bitcast.14), channel_id=1, source_target_pairs={{0,4},{4,0},{8,12},{12,8},{1,5},{5,1},{9,13},{13,9},{2,6},{6,2},{1... | collective-permute-start | bytes 7667720 | tf_op jit(solution)/shard_map/ppermute | solution.py:570
